TPU v7x, 32 devices: a whole 2x2x4 slice. The times are simulated.
32 devices in a mesh: section: 4 (over y, x), dp: 8 (over z, core).
Axes of the slice: x: 2, y: 2, z: 4, core: 2. Of those that a mesh axis runs over, the one named last changes fastest.
Arguments:
- spikes: bfloat16 [32, 8, 4, 4, 1024], P('dp'), may hold values from 0 to 2
- labels: int32 [32], P('dp'), may hold values from 0 to 999
- readout: float32 [1024, 1000], replicated, may hold values from -0.1875 to 0.1875
- weights: float32 [4, 9216, 1024], P('section', 'dp'), may hold values from -6 to 6
- first_moment: float32 [4, 9216, 1024], P('section', 'dp'), may hold values from -4 to 4
- second_moment: float32 [4, 9216, 1024], P('section', 'dp'), may hold values from 1 to 16
Outputs:
- new_weights: float32 [4, 9216, 1024], P('section', 'dp')
- new_first: float32 [4, 9216, 1024], P('section', 'dp')
- new_second: float32 [4, 9216, 1024], P('section', 'dp')
All inputs are finite; a program needn't handle non-finite values.
Results may differ from a plain program's by a relative error of at most 0.015.
Values may be sent and summed in bfloat16 or wider, within the bound.
No kernel may reach another device: no remote copies, remote signals or barrier semaphores. Data moves between devices by JAX's collectives and lax.ppermute only.
A program may use at most 192 MiB of HBM per device.

v0:
```python
import jax
import jax.numpy as jnp
from jax import lax
from jax.sharding import PartitionSpec as P

leak_rate = 0.5
spike_slope = 4.0
threshold = 1.0
loss_scale = 4096.0
beta_first = 0.8
beta_second = 0.95
learn_rate = 0.5
adam_eps = 1e-08


def from_behind(block, axis, distance):
    devices = range(lax.axis_size(axis))
    route = [(i - distance, i) for i in devices if i - distance in devices]
    return lax.ppermute(block, axis, route)


def unfold(field_in):
    height_cells = field_in.shape[2]
    width_cells = field_in.shape[3]
    padded = jnp.pad(field_in, ((0, 0), (0, 0), (1, 1), (1, 1), (0, 0)))
    pieces = [
        padded[:, :, row_shift : row_shift + height_cells, col_shift : col_shift + width_cells, :]
        for row_shift in range(3)
        for col_shift in range(3)
    ]
    stacked = jnp.stack(pieces, axis=4)
    return stacked.reshape(-1, 9 * field_in.shape[4])


def leaky(current):
    membrane = jnp.zeros_like(current[:, 0])
    fired_list = []
    for step_index in range(current.shape[1]):
        membrane = leak_rate * membrane + current[:, step_index]
        fired = jax.nn.sigmoid(spike_slope * (membrane - threshold))
        membrane = membrane - threshold * fired
        fired_list.append(fired)
    return jnp.stack(fired_list, axis=1)


def block_forward(field_in, kernel):
    rows_all = unfold(field_in)
    conv_scale = float(kernel.shape[0]) ** (-0.5)
    current = jnp.dot(rows_all, kernel, preferred_element_type=jnp.float32) * conv_scale
    shaped = current.reshape(field_in.shape[0], field_in.shape[1], -1)
    fired = leaky(shaped)
    output = (field_in.astype(jnp.float32) + fired.reshape(field_in.shape)).astype(jnp.bfloat16)
    return (output, shaped)


def block_backward(field_shape, shaped, kernel, upstream):
    up_float = upstream.astype(jnp.float32)
    unused, pull_back = jax.vjp(leaky, shaped)
    current_grad = pull_back(up_float.reshape(shaped.shape))[0]
    conv_scale = float(kernel.shape[0]) ** (-0.5)
    raw_grad = (current_grad * conv_scale).astype(jnp.bfloat16).reshape(-1, kernel.shape[1])
    row_grads = jnp.einsum("rc,kc->rk", raw_grad, kernel, preferred_element_type=jnp.float32)
    unused_two, unfold_back = jax.vjp(unfold, jnp.zeros(field_shape, jnp.float32))
    field_grad = unfold_back(row_grads)[0]
    back_grad = (up_float + field_grad).astype(jnp.bfloat16)
    return (back_grad, raw_grad)


def head_grads(final, group_labels, readout):
    pooled = jnp.mean(final.astype(jnp.float32), axis=(1, 2, 3))
    logits = jnp.dot(pooled, readout, precision=lax.Precision.HIGHEST)
    largest = jnp.max(logits, axis=-1, keepdims=True)
    exponent = jnp.exp(logits - largest)
    probability = exponent / jnp.sum(exponent, axis=-1, keepdims=True)
    classes = jnp.arange(readout.shape[1], dtype=jnp.int32)
    onehot = (group_labels[:, None] == classes[None, :]).astype(jnp.float32)
    dlogits = loss_scale * (probability - onehot)
    dpooled = jnp.dot(dlogits, readout.T, precision=lax.Precision.HIGHEST)
    cell_count = final.shape[1] * final.shape[2] * final.shape[3]
    spread = jnp.broadcast_to((dpooled / cell_count)[:, None, None, None, :], final.shape)
    return spread.astype(jnp.bfloat16)


def adam_update(weights, first_moment, second_moment, grad_total):
    new_first = beta_first * first_moment + (1.0 - beta_first) * grad_total
    new_second = beta_second * second_moment + (1.0 - beta_second) * grad_total * grad_total
    new_weights = weights - learn_rate * new_first / (jnp.sqrt(new_second) + adam_eps)
    return (new_weights, new_first, new_second)


def shards(spikes, labels, readout, weights, first_moment, second_moment):
    sections = lax.axis_size("section")
    position = lax.axis_index("section")
    micro_count = spikes.shape[0]
    channels = spikes.shape[4]
    cells_shape = (1,) + spikes.shape[1:]
    state_width = spikes.shape[2] * spikes.shape[3] * channels
    row_count_micro = spikes.shape[1] * spikes.shape[2] * spikes.shape[3]
    local_kernel = weights[0].astype(jnp.bfloat16)
    kernel = lax.all_gather(local_kernel, "dp", axis=0, tiled=True)

    def forward_active(field_in):
        return block_forward(field_in, kernel)

    def forward_passive(field_in):
        return (
            jnp.zeros_like(field_in),
            jnp.zeros((1, field_in.shape[1], state_width), jnp.float32),
        )

    def forward_tick(step_number, state_tuple):
        arriving, stash_in, stash_state, finals = state_tuple
        slot_number = step_number - position
        active_slot = (slot_number >= 0) & (slot_number < micro_count)
        slot_index = jnp.clip(slot_number, 0, micro_count - 1)
        own_input = lax.dynamic_slice_in_dim(spikes, slot_index, 1, 0)
        field_in = jnp.where(position == 0, own_input, arriving)
        output, shaped = lax.cond(active_slot, forward_active, forward_passive, field_in)
        old_in = lax.dynamic_slice_in_dim(stash_in, slot_index, 1, 0)
        stash_in = lax.dynamic_update_slice_in_dim(
            stash_in, jnp.where(active_slot, field_in, old_in), slot_index, 0
        )
        old_state = lax.dynamic_slice_in_dim(stash_state, slot_index, 1, 0)
        stash_state = lax.dynamic_update_slice_in_dim(
            stash_state, jnp.where(active_slot, shaped, old_state), slot_index, 0
        )
        old_final = lax.dynamic_slice_in_dim(finals, slot_index, 1, 0)
        keep_final = active_slot & (position == sections - 1)
        finals = lax.dynamic_update_slice_in_dim(
            finals, jnp.where(keep_final, output, old_final), slot_index, 0
        )
        arriving = from_behind(output, "section", 1)
        return (arriving, stash_in, stash_state, finals)

    start_tuple = (
        jnp.zeros(cells_shape, jnp.bfloat16),
        jnp.zeros(spikes.shape, jnp.bfloat16),
        jnp.zeros((micro_count, spikes.shape[1], state_width), jnp.float32),
        jnp.zeros(spikes.shape, jnp.bfloat16),
    )
    arriving, stash_in, stash_state, finals = lax.fori_loop(
        0, sections + micro_count - 1, forward_tick, start_tuple
    )
    upstream_all = head_grads(finals, labels, readout)

    def backward_active(operands):
        return block_backward(cells_shape, operands[0], kernel, operands[1])

    def backward_passive(operands):
        return (
            jnp.zeros(cells_shape, jnp.bfloat16),
            jnp.zeros((row_count_micro, channels), jnp.bfloat16),
        )

    def backward_tick(step_number, state_tuple):
        arriving_grad, stash_grad = state_tuple
        slot_number = step_number - (sections - 1 - position)
        active_slot = (slot_number >= 0) & (slot_number < micro_count)
        slot_index = jnp.clip(slot_number, 0, micro_count - 1)
        own_grad = lax.dynamic_slice_in_dim(upstream_all, slot_index, 1, 0)
        upstream = jnp.where(position == sections - 1, own_grad, arriving_grad)
        shaped = lax.dynamic_slice_in_dim(stash_state, slot_index, 1, 0)
        back_grad, raw_grad = lax.cond(
            active_slot, backward_active, backward_passive, (shaped, upstream)
        )
        old_grad = lax.dynamic_slice_in_dim(stash_grad, slot_index, 1, 0)
        stash_grad = lax.dynamic_update_slice_in_dim(
            stash_grad, jnp.where(active_slot, raw_grad[None], old_grad), slot_index, 0
        )
        arriving_grad = from_behind(back_grad, "section", -1)
        return (arriving_grad, stash_grad)

    back_tuple = (
        jnp.zeros(cells_shape, jnp.bfloat16),
        jnp.zeros((micro_count, row_count_micro, channels), jnp.bfloat16),
    )
    arriving_grad, stash_grad = lax.fori_loop(
        0, sections + micro_count - 1, backward_tick, back_tuple
    )
    rows_all = unfold(stash_in)
    raw_grads = stash_grad.reshape(-1, channels)
    full_grad = jnp.einsum("rk,rc->kc", rows_all, raw_grads, preferred_element_type=jnp.float32)
    grad_shard = lax.psum_scatter(
        full_grad.astype(jnp.bfloat16), "dp", scatter_dimension=0, tiled=True
    ).astype(jnp.float32)
    return adam_update(weights, first_moment, second_moment, grad_shard[None])


def solution(mesh):
    return jax.shard_map(
        shards,
        mesh=mesh,
        in_specs=(
            P("dp", None, None, None, None),
            P("dp"),
            P(),
            P("section", "dp", None),
            P("section", "dp", None),
            P("section", "dp", None),
        ),
        out_specs=(P("section", "dp", None), P("section", "dp", None), P("section", "dp", None)),
        check_vma=False,
    )
```

profile of v0, /device:TPU:0, one launch (start us, length us, event | category | flops | bytes accessed | tf_op | source)
XLA Modules:
  0.0 984.7 jit_solution(7520663115612741709)
XLA Ops:
  7.2 4.1 convert_element_type.64
  11.4 171.1 %all-gather.3.cloned.1.call-done = bf16[1,9216,1024]{2,1,0:T(8,128)(2,1)} async-done(((bf16[1,1152,1024]{2,1,0:T(8,128)(2,1)}), bf16[1,9216,1024]{2,1,0:T(8,128)(2,1)}) %all-gather.3.cloned.1.call-update) | async-done | bytes 18874384 | tf_op jit(solution)/shard_map/all_gather | solution.py:100
  185.0 251.6 %while.38 = (s32[]{:T(128)}, bf16[1,8,4,4,1024]{4,3,2,1,0:T(4,128)(2,1)S(1)}, bf16[4,8,4,4,1024]{4,3,2,1,0:T(4,128)(2,1)S(1)}, f32[4,8,16384]{2,1,0:T(8,128)}, b...) while((s32[]{:T(128)}, ...), condition=%wide.region_3.4_spmd, body=%wide.region_0.3_spmd.sunk | while | flops 2417967104 | bytes 47579456 | solution.py:141
  186.2 30.1 %conditional.5 = (bf16[1,8,4,4,1024]{4,3,2,1,0:T(4,128)(2,1)S(1)}, f32[1,8,16384]{2,1,0:T(8,128)}) conditional(s32[]{:T(128)} %convert_element_type.100, () %tuple.135, (bf16[1,8,4,4,1024]{4,3,2,1,0:T(4,128)(2,1)S(1)}, bf16[9216,1024]{1,0:T(8,128)(2,1)}) %tuple.136), branch_computations={%region_1.1_spmd, %region_2.2_spmd} | conditional | flops 2417442816 | bytes 42860596 | solution.py:118
  187.8 2.2 copy.18
  190.0 1.8 copy.40
  191.8 7.9 convolution_multiply_fusion
  213.0 2.1 divide_reduce_fusion
  217.6 2.1 select_dynamic-update-slice_fusion.9
  219.9 4.0 collective-permute-done
  225.1 30.1 %conditional.5 = (bf16[1,8,4,4,1024]{4,3,2,1,0:T(4,128)(2,1)S(1)}, f32[1,8,16384]{2,1,0:T(8,128)}) conditional(s32[]{:T(128)} %convert_element_type.100, () %tuple.135, (bf16[1,8,4,4,1024]{4,3,2,1,0:T(4,128)(2,1)S(1)}, bf16[9216,1024]{1,0:T(8,128)(2,1)}) %tuple.136), branch_computations={%region_1.1_spmd, %region_2.2_spmd} | conditional | flops 2417442816 | bytes 42860596 | solution.py:118
  226.6 2.2 copy.18
  230.7 7.9 convolution_multiply_fusion
  251.9 2.1 divide_reduce_fusion
  255.2 4.4 collective-permute-start
  259.6 2.1 select_dynamic-update-slice_fusion.9
  261.9 3.2 collective-permute-done
  266.3 30.1 %conditional.5 = (bf16[1,8,4,4,1024]{4,3,2,1,0:T(4,128)(2,1)S(1)}, f32[1,8,16384]{2,1,0:T(8,128)}) conditional(s32[]{:T(128)} %convert_element_type.100, () %tuple.135, (bf16[1,8,4,4,1024]{4,3,2,1,0:T(4,128)(2,1)S(1)}, bf16[9216,1024]{1,0:T(8,128)(2,1)}) %tuple.136), branch_computations={%region_1.1_spmd, %region_2.2_spmd} | conditional | flops 2417442816 | bytes 42860596 | solution.py:118
  267.8 2.2 copy.18
  270.1 1.8 copy.40
  271.9 7.9 convolution_multiply_fusion
  293.1 2.1 divide_reduce_fusion
  296.4 4.4 collective-permute-start
  300.8 2.1 select_dynamic-update-slice_fusion.9
  303.1 2.3 collective-permute-done
  306.7 30.1 %conditional.5 = (bf16[1,8,4,4,1024]{4,3,2,1,0:T(4,128)(2,1)S(1)}, f32[1,8,16384]{2,1,0:T(8,128)}) conditional(s32[]{:T(128)} %convert_element_type.100, () %tuple.135, (bf16[1,8,4,4,1024]{4,3,2,1,0:T(4,128)(2,1)S(1)}, bf16[9216,1024]{1,0:T(8,128)(2,1)}) %tuple.136), branch_computations={%region_1.1_spmd, %region_2.2_spmd} | conditional | flops 2417442816 | bytes 42860596 | solution.py:118
  308.2 2.2 copy.18
  312.3 7.9 convolution_multiply_fusion
  333.4 2.1 divide_reduce_fusion
  336.7 4.4 collective-permute-start
  341.2 2.1 select_dynamic-update-slice_fusion.9
  347.2 33.6 %collective-permute-start = (bf16[1,8,4,4,1024]{4,3,2,1,0:T(4,128)(2,1)S(1)}, bf16[1,8,4,4,1024]{4,3,2,1,0:T(4,128)(2,1)S(1)}, u32[]{:S(2)}, u32[]{:S(2)}) collective-permute-start(bf16[1,8,4,4,1024]{4,3,2,1,0:T(4,128)(2,1)S(1)} %get-tuple-element.668), channel_id=1, source_target_pairs={{0,8},{8,16},{16,24},{1,9},{9,17},{17,25},{2,10},{10,18},{18,26},{... | collective-permute-start | bytes 786440 | tf_op jit(solution)/shard_map/while/body/eval_jaxpr/ppermute | solution.py:19
  380.8 1.9 select_dynamic-update-slice_fusion.9
  386.8 5.3 collective-permute-start
  392.1 1.9 select_dynamic-update-slice_fusion.9
  398.2 34.5 %collective-permute-start = (bf16[1,8,4,4,1024]{4,3,2,1,0:T(4,128)(2,1)S(1)}, bf16[1,8,4,4,1024]{4,3,2,1,0:T(4,128)(2,1)S(1)}, u32[]{:S(2)}, u32[]{:S(2)}) collective-permute-start(bf16[1,8,4,4,1024]{4,3,2,1,0:T(4,128)(2,1)S(1)} %get-tuple-element.668), channel_id=1, source_target_pairs={{0,8},{8,16},{16,24},{1,9},{9,17},{17,25},{2,10},{10,18},{18,26},{... | collective-permute-start | bytes 786440 | tf_op jit(solution)/shard_map/while/body/eval_jaxpr/ppermute | solution.py:19
  432.6 1.9 select_dynamic-update-slice_fusion.9
  443.4 11.7 %copy.28 = bf16[4,8,4,4,9,1024]{5,4,3,2,1,0:T(8,128)(2,1)S(1)} copy(bf16[4,8,4,4,9,1024]{5,3,2,1,0,4:T(4,128)(2,1)S(1)} %fusion.50) | data formatting | bytes 18874368 | tf_op jit(solution)/shard_map/stack | solution.py:31
  455.1 8.9 copy.41
  464.0 3.6 fusion.65
  467.8 2.1 fusion.34
  470.0 294.4 %while.39 = (s32[]{:T(128)}, bf16[1,8,4,4,1024]{4,1,3,2,0:T(8,128)(2,1)S(1)}, bf16[4,128,1024]{2,1,0:T(8,128)(2,1)S(1)}, s32[]{:T(128)}, pred[]{:T(512)}, /*inde...) while((s32[]{:T(128)}, ...), condition=%wide.region_10.11_spmd.clone, body=%wide.region_7.10_spmd.clone.sunk | while | flops 2421374976 | bytes 47587756 | solution.py:177
  471.8 8.2 collective-permute-done.1
  481.5 33.1 %collective-permute-done.1 = bf16[1,8,4,4,1024]{4,1,3,2,0:T(8,128)(2,1)S(1)} collective-permute-done((bf16[1,8,4,4,1024]{4,1,3,2,0:T(8,128)(2,1)S(1)}, bf16[1,8,4,4,1024]{4,1,3,2,0:T(8,128)(2,1)S(1)}, u32[]{:S(2)}, u32[]{:S(2)}) %collective-permute-start.1) | collective-permute-done | bytes 262176 | tf_op jit(solution)/shard_map/while/body/eval_jaxpr/ppermute | solution.py:19
  516.0 95.0 %collective-permute-done.1 = bf16[1,8,4,4,1024]{4,1,3,2,0:T(8,128)(2,1)S(1)} collective-permute-done((bf16[1,8,4,4,1024]{4,1,3,2,0:T(8,128)(2,1)S(1)}, bf16[1,8,4,4,1024]{4,1,3,2,0:T(8,128)(2,1)S(1)}, u32[]{:S(2)}, u32[]{:S(2)}) %collective-permute-start.1) | collective-permute-done | bytes 262176 | tf_op jit(solution)/shard_map/while/body/eval_jaxpr/ppermute | solution.py:19
  611.0 29.5 %conditional.6 = (bf16[1,8,4,4,1024]{4,1,3,2,0:T(8,128)(2,1)S(1)}, bf16[1,128,1024]{2,1,0:T(8,128)(2,1)S(1)}) conditional(s32[]{:T(128)} %convert_element_type.101, () %tuple.138, (pred[]{:T(512)}, bf16[4,1024]{1,0:T(4,128)(2,1)S(1)}, s32[]{:T(128)}, bf16[1,8,4,4,1024]{4,1,3,2,0:T(8,128)(2,1)S(1)}, f32[4,8,16384]{2,1,0:T(8,128)}, ...), branch_computations={%region_8.8_spmd, %region_9.9_spmd} | conditional | flops 2421243904 | bytes 45752480 | solution.py:163
  622.0 14.8 %convolution_bitcast_fusion = f32[1,8,4,4,9,1024]{5,1,4,3,2,0:T(8,128)} fusion(bf16[8,4,4,1024,1]{3,0,4,2,1:T(8,128)(2,1)S(1)} %bitcast.148, bf16[9,1024,1024,1,1]{2,1,0,4,3:T(8,128)(2,1)} %bitcast.142), kind=kOutput, calls=%fused_computation.1 | convolution fusion | flops 2415919104 | bytes 23855104 | tf_op jit(solution)/shard_map/while/body/eval_jaxpr/cond/branch_1_fun/rc,kc->rk/dot_general | solution.py:62
  636.9 3.0 slice_bitcast_fusion.8
  641.9 7.8 collective-permute-done.1
  649.6 29.4 %conditional.6 = (bf16[1,8,4,4,1024]{4,1,3,2,0:T(8,128)(2,1)S(1)}, bf16[1,128,1024]{2,1,0:T(8,128)(2,1)S(1)}) conditional(s32[]{:T(128)} %convert_element_type.101, () %tuple.138, (pred[]{:T(512)}, bf16[4,1024]{1,0:T(4,128)(2,1)S(1)}, s32[]{:T(128)}, bf16[1,8,4,4,1024]{4,1,3,2,0:T(8,128)(2,1)S(1)}, f32[4,8,16384]{2,1,0:T(8,128)}, ...), branch_computations={%region_8.8_spmd, %region_9.9_spmd} | conditional | flops 2421243904 | bytes 45752480 | solution.py:163
  660.6 14.8 %convolution_bitcast_fusion = f32[1,8,4,4,9,1024]{5,1,4,3,2,0:T(8,128)} fusion(bf16[8,4,4,1024,1]{3,0,4,2,1:T(8,128)(2,1)S(1)} %bitcast.148, bf16[9,1024,1024,1,1]{2,1,0,4,3:T(8,128)(2,1)} %bitcast.142), kind=kOutput, calls=%fused_computation.1 | convolution fusion | flops 2415919104 | bytes 23855104 | tf_op jit(solution)/shard_map/while/body/eval_jaxpr/cond/branch_1_fun/rc,kc->rk/dot_general | solution.py:62
  675.5 3.0 slice_bitcast_fusion.8
  680.5 7.7 collective-permute-done.1
  688.2 29.4 %conditional.6 = (bf16[1,8,4,4,1024]{4,1,3,2,0:T(8,128)(2,1)S(1)}, bf16[1,128,1024]{2,1,0:T(8,128)(2,1)S(1)}) conditional(s32[]{:T(128)} %convert_element_type.101, () %tuple.138, (pred[]{:T(512)}, bf16[4,1024]{1,0:T(4,128)(2,1)S(1)}, s32[]{:T(128)}, bf16[1,8,4,4,1024]{4,1,3,2,0:T(8,128)(2,1)S(1)}, f32[4,8,16384]{2,1,0:T(8,128)}, ...), branch_computations={%region_8.8_spmd, %region_9.9_spmd} | conditional | flops 2421243904 | bytes 45752480 | solution.py:163
  699.2 14.8 %convolution_bitcast_fusion = f32[1,8,4,4,9,1024]{5,1,4,3,2,0:T(8,128)} fusion(bf16[8,4,4,1024,1]{3,0,4,2,1:T(8,128)(2,1)S(1)} %bitcast.148, bf16[9,1024,1024,1,1]{2,1,0,4,3:T(8,128)(2,1)} %bitcast.142), kind=kOutput, calls=%fused_computation.1 | convolution fusion | flops 2415919104 | bytes 23855104 | tf_op jit(solution)/shard_map/while/body/eval_jaxpr/cond/branch_1_fun/rc,kc->rk/dot_general | solution.py:62
  714.0 3.0 slice_bitcast_fusion.8
  719.1 7.7 collective-permute-done.1
  726.8 29.4 %conditional.6 = (bf16[1,8,4,4,1024]{4,1,3,2,0:T(8,128)(2,1)S(1)}, bf16[1,128,1024]{2,1,0:T(8,128)(2,1)S(1)}) conditional(s32[]{:T(128)} %convert_element_type.101, () %tuple.138, (pred[]{:T(512)}, bf16[4,1024]{1,0:T(4,128)(2,1)S(1)}, s32[]{:T(128)}, bf16[1,8,4,4,1024]{4,1,3,2,0:T(8,128)(2,1)S(1)}, f32[4,8,16384]{2,1,0:T(8,128)}, ...), branch_computations={%region_8.8_spmd, %region_9.9_spmd} | conditional | flops 2421243904 | bytes 45752480 | solution.py:163
  737.7 14.8 %convolution_bitcast_fusion = f32[1,8,4,4,9,1024]{5,1,4,3,2,0:T(8,128)} fusion(bf16[8,4,4,1024,1]{3,0,4,2,1:T(8,128)(2,1)S(1)} %bitcast.148, bf16[9,1024,1024,1,1]{2,1,0,4,3:T(8,128)(2,1)} %bitcast.142), kind=kOutput, calls=%fused_computation.1 | convolution fusion | flops 2415919104 | bytes 23855104 | tf_op jit(solution)/shard_map/while/body/eval_jaxpr/cond/branch_1_fun/rc,kc->rk/dot_general | solution.py:62
  752.5 3.0 slice_bitcast_fusion.8
  757.6 6.9 collective-permute-done.1
  764.4 17.1 %convolution_convert_fusion = bf16[9216,1024]{1,0:T(8,128)(2,1)} fusion(bf16[512,9216]{1,0:T(8,128)(2,1)} %bitcast.149, bf16[512,1024]{1,0:T(8,128)(2,1)S(1)} %bitcast.150), kind=kOutput, calls=%fused_computation.125 | convolution fusion | flops 9673113600 | bytes 29360128 | tf_op jit(solution)/shard_map/rk,rc->kc/dot_general | solution.py:182
  781.6 184.5 %reduce-scatter.2.cloned.1.call-done = bf16[1152,1024]{1,0:T(8,128)(2,1)} async-done(((bf16[9216,1024]{1,0:T(8,128)(2,1)}), bf16[1152,1024]{1,0:T(8,128)(2,1)}) %reduce-scatter.2.cloned.1.call-update) | async-done | bytes 2359312 | tf_op jit(solution)/shard_map/reduce_scatter | solution.py:183
  966.1 11.3 %divide_subtract_fusion = (f32[1,1152,1024]{2,1,0:T(8,128)}, f32[1,1152,1024]{2,1,0:T(8,128)}, f32[1,1152,1024]{2,1,0:T(8,128)}) fusion(f32[1,1152,1024]{2,1,0:T(8,128)} %param.17, bf16[1152,1024]{1,0:T(8,128)(2,1)} %reduce-scatter.2.cloned.1.call-done, f32[1,1152,1024]{2,1,0:T(8,128)} %param.18, f32[1,1152,1024]{2,1,0:T(8,128)} %param.19), kind=kLoop, calls=%fused_computation.140 | loop fusion | flops 14155776 | bytes 30670848 | tf_op jit(solution)/shard_map/sub | solution.py:87
  (294 shorter events, 155.6 us)
Async XLA Ops:
  7.2 175.3 %all-gather.3.cloned.1.call-start = ((), (), s32[]{:S(2)}) async-start(), calls=%async_computation.2 | async-start | bytes 21233664 | tf_op jit(solution)/shard_map/all_gather | solution.py:100
  11.4 954.7 %reduce-scatter.2.cloned.1.call-start = ((), (), s32[]{:S(2)}) async-start(), calls=%async_computation.1 | async-start | bytes 21233664 | tf_op jit(solution)/shard_map/reduce_scatter | solution.py:183
  216.3 7.6 collective-permute-start
  255.2 9.9 %collective-permute-start = (bf16[1,8,4,4,1024]{4,3,2,1,0:T(4,128)(2,1)S(1)}, bf16[1,8,4,4,1024]{4,3,2,1,0:T(4,128)(2,1)S(1)}, u32[]{:S(2)}, u32[]{:S(2)}) collective-permute-start(bf16[1,8,4,4,1024]{4,3,2,1,0:T(4,128)(2,1)S(1)} %get-tuple-element.668), channel_id=1, source_target_pairs={{0,8},{8,16},{16,24},{1,9},{9,17},{17,25},{2,10},{10,18},{18,26},{... | collective-permute-start | bytes 786440 | tf_op jit(solution)/shard_map/while/body/eval_jaxpr/ppermute | solution.py:19
  296.4 9.0 collective-permute-start
  336.7 8.3 collective-permute-start
  347.2 37.5 %collective-permute-start = (bf16[1,8,4,4,1024]{4,3,2,1,0:T(4,128)(2,1)S(1)}, bf16[1,8,4,4,1024]{4,3,2,1,0:T(4,128)(2,1)S(1)}, u32[]{:S(2)}, u32[]{:S(2)}) collective-permute-start(bf16[1,8,4,4,1024]{4,3,2,1,0:T(4,128)(2,1)S(1)} %get-tuple-element.668), channel_id=1, source_target_pairs={{0,8},{8,16},{16,24},{1,9},{9,17},{17,25},{2,10},{10,18},{18,26},{... | collective-permute-start | bytes 786440 | tf_op jit(solution)/shard_map/while/body/eval_jaxpr/ppermute | solution.py:19
  386.8 9.2 collective-permute-start
  398.2 38.3 %collective-permute-start = (bf16[1,8,4,4,1024]{4,3,2,1,0:T(4,128)(2,1)S(1)}, bf16[1,8,4,4,1024]{4,3,2,1,0:T(4,128)(2,1)S(1)}, u32[]{:S(2)}, u32[]{:S(2)}) collective-permute-start(bf16[1,8,4,4,1024]{4,3,2,1,0:T(4,128)(2,1)S(1)} %get-tuple-element.668), channel_id=1, source_target_pairs={{0,8},{8,16},{16,24},{1,9},{9,17},{17,25},{2,10},{10,18},{18,26},{... | collective-permute-start | bytes 786440 | tf_op jit(solution)/shard_map/while/body/eval_jaxpr/ppermute | solution.py:19
  455.1 8.9 copy-start
  455.1 12.7 %copy-start.1 = (s32[4]{0:T(128)S(1)}, s32[4]{0:T(128)}, u32[]{:S(2)}) copy-start(s32[4]{0:T(128)} %param.15) | copy-start | bytes 52
  470.4 9.6 collective-permute-start.1
  480.1 34.5 %collective-permute-start.1 = (bf16[1,8,4,4,1024]{4,1,3,2,0:T(8,128)(2,1)S(1)}, bf16[1,8,4,4,1024]{4,1,3,2,0:T(8,128)(2,1)S(1)}, u32[]{:S(2)}, u32[]{:S(2)}) collective-permute-start(bf16[1,8,4,4,1024]{4,1,3,2,0:T(8,128)(2,1)S(1)} %get-tuple-element.679), channel_id=1, source_target_pairs={{8,0},{16,8},{24,16},{9,1},{17,9},{25,17},{10,2},{18,10},{26,18},{... | collective-permute-start | bytes 786440 | tf_op jit(solution)/shard_map/while/body/eval_jaxpr/ppermute | solution.py:19
  514.6 96.4 %collective-permute-start.1 = (bf16[1,8,4,4,1024]{4,1,3,2,0:T(8,128)(2,1)S(1)}, bf16[1,8,4,4,1024]{4,1,3,2,0:T(8,128)(2,1)S(1)}, u32[]{:S(2)}, u32[]{:S(2)}) collective-permute-start(bf16[1,8,4,4,1024]{4,1,3,2,0:T(8,128)(2,1)S(1)} %get-tuple-element.679), channel_id=1, source_target_pairs={{8,0},{16,8},{24,16},{9,1},{17,9},{25,17},{10,2},{18,10},{26,18},{... | collective-permute-start | bytes 786440 | tf_op jit(solution)/shard_map/while/body/eval_jaxpr/ppermute | solution.py:19
  640.5 9.1 collective-permute-start.1
  679.1 9.1 collective-permute-start.1
  717.7 9.1 collective-permute-start.1
  756.2 8.3 collective-permute-start.1
Sparse Core Ops, SparseCore 0:
  11.5 170.9 all-gather.2
  781.7 184.3 reduce-scatter.1
where the time goes:
time: 997 us; the launch traced here: 985 us
  waiting for transfers between devices  538 us (54%)
  other arithmetic  145 us (15%)
  matrix products  114 us (11%)
  starting transfers between devices  96.9 us (10%)
  local copies, waits for them, and re-layouts  73.7 us (7%)
  between operations  14.6 us (1%)
    reduce_scatter x1, waiting for transfers between devices, shards(): lax.psum_scatter(full_grad.astype(jnp.bfloat16), 'dp', scatter_dimension=...  184 us
    ppermute x14, waiting for transfers between devices, from_behind(): return lax.ppermute(block, axis, route)  183 us
    all_gather x1, waiting for transfers between devices, shards(): kernel = lax.all_gather(local_kernel, 'dp', axis=0, tiled=True)  171 us
    ppermute x14, starting transfers between devices, from_behind(): return lax.ppermute(block, axis, route)  96.9 us
    dot_general x4, matrix products, block_backward(): jnp.einsum('rc,kc->rk', raw_grad, kernel, preferred_element_type=jnp.floa...  59.4 us
    add x44, other arithmetic, leaky(): membrane = leak_rate * membrane + current[:, step_index]  56.4 us
    another operation x14, local copies, waits for them, and re-layouts, unfold(): stacked = jnp.stack(pieces, axis=4)  34.2 us
    div x32, other arithmetic, leaky(): fired = jax.nn.sigmoid(spike_slope * (membrane - threshold))  32.5 us
  transfers between devices with their start and end apart: 16, of which 16 were waited for; matrix products, arithmetic and copies ran while one was open for 2% of the time, Pallas kernels for 0%

commit v1 on v0

v1 whole, which is shorter than its diff:
```python
import functools
import jax
import jax.numpy as jnp
from jax import lax
from jax.experimental import pallas as pl
from jax.experimental.pallas import tpu as pltpu
from jax.sharding import PartitionSpec as P

leak_rate = 0.5
spike_slope = 4.0
threshold = 1.0
loss_scale = 4096.0
beta_first = 0.8
beta_second = 0.95
learn_rate = 0.5
adam_eps = 1e-08
HIGH = lax.Precision.HIGHEST
VMEM = pltpu.VMEM
LIMIT = 56 * 2**20


def fetch_weights(scal, sources, weights, sems):
    z, core = scal[1], scal[2]
    ring, depth = sources[0].shape[0], sources[0].shape[1]
    copies = []
    for which, source in enumerate(sources):
        owner_core = core if which == 0 else 1 - core
        for j in range(ring):
            place = lax.rem(z + j, ring)
            row = pl.multiple_of((place * 2 + owner_core) * depth, depth)
            copies.append(
                pltpu.make_async_copy(
                    source.at[j], weights.at[pl.ds(row, depth), :], sems.at[which, j]
                )
            )
    for copy in copies:
        copy.start()
    return copies


def forward_kernel(dims, last, scal, *refs):
    sections, height, width, images, steps = dims
    slices = refs[:sections]
    refs = refs[sections:]
    sources = refs[:2]
    refs = refs[2:]
    if last:
        readout, out, fired_out, logits_out, weights, padded, work, sems = refs
    else:
        out, fired_out, weights, padded, work, sems = refs
    copies = fetch_weights(scal, sources, weights, sems)
    rows, lanes = slices[0].shape
    group = images * steps
    channels = sections * lanes
    padded[...] = jnp.zeros_like(padded)
    for k in range(sections):
        padded[scal[0] ^ k, 1 : height + 1, 1 : width + 1] = slices[k][...].reshape(
            height, width, group, lanes
        )
    for copy in copies:
        copy.wait()
    total = jnp.zeros((rows, lanes), jnp.float32)
    for offset in range(9):
        r, c = divmod(offset, 3)
        lhs = jnp.concatenate(
            [
                padded[j, r : r + height, c : c + width].reshape(rows, lanes)
                for j in range(sections)
            ],
            axis=1,
        )
        total += jnp.dot(
            lhs,
            weights[offset * channels : (offset + 1) * channels, :],
            preferred_element_type=jnp.float32,
        )
    scale = float(9 * channels) ** (-0.5)
    current = total * scale
    count = rows // steps
    tiles = lanes // 128
    for tile in range(tiles):
        here, there = work.at[tile], fired_out.at[tile]
        here[...] = current[:, tile * 128 : (tile + 1) * 128]
        membrane = jnp.zeros((count, 128), jnp.float32)
        for t in range(steps):
            spot = pl.ds(t, count, stride=steps)
            h = leak_rate * membrane + here[spot, :]
            fired = jax.nn.sigmoid(spike_slope * (h - threshold))
            membrane = h - threshold * fired
            there[spot, :] = fired
    fired = jnp.concatenate([fired_out[tile] for tile in range(tiles)], axis=1)
    result = (slices[0][...].astype(jnp.float32) + fired).astype(jnp.bfloat16)
    out[...] = result
    if last:
        summed = jnp.sum(
            result.astype(jnp.float32).reshape(height * width, group, lanes), axis=0
        )
        pooled = jnp.sum(summed.reshape(images, steps, lanes), axis=1) / float(
            height * width * steps
        )
        logits_out[...] = jnp.dot(
            pooled, readout[...], precision=HIGH, preferred_element_type=jnp.float32
        )


def backward_kernel(dims, stage, classes, scal, *refs):
    sections, height, width, images, steps = dims
    if stage == 0:
        logit_parts = refs[:sections]
        labels, readout = refs[sections : sections + 2]
        refs = refs[sections + 2 :]
    else:
        own_part = refs[0]
        arrived = refs[1:sections]
        refs = refs[sections:]
    fired = refs[0]
    refs = refs[1:]
    if stage < 2:
        sources = refs[:2]
        refs = refs[2:]
        raw_out, own_out = refs[:2]
        sends = refs[2 : 1 + sections]
        weights, padded, upstream, work, sems = refs[1 + sections :]
        copies = fetch_weights(scal, sources, weights, sems)
        padded[...] = jnp.zeros_like(padded)
    else:
        raw_out, upstream, work = refs
    tiles, rows = fired.shape[:2]
    lanes = tiles * 128
    group = images * steps
    channels = sections * lanes
    cells = height * width
    count = rows // steps
    if stage == 0:
        logits = logit_parts[0][...]
        for part in logit_parts[1:]:
            logits = logits + part[...]
        lane = lax.broadcasted_iota(jnp.int32, logits.shape, 1)
        logits = jnp.where(lane < classes, logits, -jnp.inf)
        exponent = jnp.exp(logits - jnp.max(logits, axis=-1, keepdims=True))
        probability = exponent / jnp.sum(exponent, axis=-1, keepdims=True)
        onehot = (labels[...] == lane).astype(jnp.float32)
        dlogits = loss_scale * (probability - onehot)
        dpooled = lax.dot_general(
            dlogits,
            readout[...],
            (((1,), (1,)), ((), ())),
            precision=HIGH,
            preferred_element_type=jnp.float32,
        )
        spread = (dpooled / float(cells * steps)).astype(jnp.bfloat16).astype(jnp.float32)
        arriving = jnp.broadcast_to(
            spread[None, :, None, :], (cells, images, steps, lanes)
        ).reshape(rows, lanes)
    else:
        arriving = own_part[...]
        for part in arrived:
            arriving = arriving + part[...].astype(jnp.float32)
        arriving = arriving.astype(jnp.bfloat16).astype(jnp.float32)
    scale = float(9 * channels) ** (-0.5)
    for tile in range(tiles):
        upstream[tile] = arriving[:, tile * 128 : (tile + 1) * 128]
        here, there, fired_here = upstream.at[tile], work.at[tile], fired.at[tile]
        dmembrane = jnp.zeros((count, 128), jnp.float32)
        for t in reversed(range(steps)):
            spot = pl.ds(t, count, stride=steps)
            f = fired_here[spot, :]
            slope = spike_slope * (f * (1.0 - f))
            dh = dmembrane + (here[spot, :] - threshold * dmembrane) * slope
            there[spot, :] = dh * scale
            dmembrane = leak_rate * dh
    raw = jnp.concatenate([work[tile] for tile in range(tiles)], axis=1).astype(jnp.bfloat16)
    raw_out[...] = raw
    if stage == 2:
        return
    padded[1 : height + 1, 1 : width + 1] = raw.reshape(height, width, group, lanes)
    for copy in copies:
        copy.wait()
    for k in list(range(1, sections)) + [0]:
        total = jnp.zeros((rows, lanes), jnp.float32)
        for offset in range(9):
            r, c = divmod(offset, 3)
            lhs = padded[2 - r : 2 - r + height, 2 - c : 2 - c + width].reshape(rows, lanes)
            row = pl.multiple_of(offset * channels + (scal[0] ^ k) * lanes, lanes)
            total += lax.dot_general(
                lhs,
                weights[pl.ds(row, lanes), :],
                (((1,), (1,)), ((), ())),
                preferred_element_type=jnp.float32,
            )
        if k == 0:
            own_out[...] = total + jnp.concatenate([upstream[tile] for tile in range(tiles)], axis=1)
        else:
            sends[k - 1][...] = total.astype(jnp.bfloat16)


def vmem(count):
    return [pl.BlockSpec(memory_space=VMEM)] * count


def run_forward(dims, last, scal, slices, sources, readout):
    sections, height, width, images, steps = dims
    rows, lanes = slices[0].shape
    depth = sources[0].shape[1]
    ring = sources[0].shape[0]
    shapes = [
        jax.ShapeDtypeStruct((rows, lanes), jnp.bfloat16),
        jax.ShapeDtypeStruct((lanes // 128, rows, 128), jnp.float32),
    ]
    operands = [scal, *slices, *sources]
    extra = []
    if last:
        shapes.append(jax.ShapeDtypeStruct((images, readout.shape[1]), jnp.float32))
        operands.append(readout)
        extra = vmem(1)
    return pl.pallas_call(
        functools.partial(forward_kernel, dims, last),
        out_shape=shapes,
        in_specs=[pl.BlockSpec(memory_space=pltpu.SMEM)]
        + vmem(sections)
        + [pl.BlockSpec(memory_space=pl.ANY)] * 2
        + extra,
        out_specs=vmem(len(shapes)),
        scratch_shapes=[
            VMEM((2 * ring * depth, lanes), jnp.bfloat16),
            VMEM((sections, height + 2, width + 2, images * steps, lanes), jnp.bfloat16),
            VMEM((lanes // 128, rows, 128), jnp.float32),
            pltpu.SemaphoreType.DMA((2, ring)),
        ],
        compiler_params=pltpu.CompilerParams(vmem_limit_bytes=LIMIT),
        cost_estimate=pl.CostEstimate(
            flops=2 * rows * lanes * 2 * ring * depth,
            bytes_accessed=4 * ring * depth * lanes,
            transcendentals=rows * lanes,
        ),
        name="forward_block",
    )(*operands)


def run_backward(dims, stage, classes, scal, heads, fired, sources):
    sections, height, width, images, steps = dims
    tiles, rows = fired.shape[:2]
    lanes = tiles * 128
    half = jax.ShapeDtypeStruct((rows, lanes), jnp.bfloat16)
    full = jax.ShapeDtypeStruct((rows, lanes), jnp.float32)
    operands = [scal, *heads, fired]
    specs = [pl.BlockSpec(memory_space=pltpu.SMEM)] + vmem(len(heads) + 1)
    work = [VMEM(fired.shape, jnp.float32), VMEM(fired.shape, jnp.float32)]
    cost = 0
    if stage < 2:
        ring, depth = sources[0].shape[:2]
        operands += list(sources)
        specs += [pl.BlockSpec(memory_space=pl.ANY)] * 2
        shapes = [half, full] + [half] * (sections - 1)
        work = (
            [
                VMEM((2 * ring * depth, lanes), jnp.bfloat16),
                VMEM((height + 2, width + 2, images * steps, lanes), jnp.bfloat16),
            ]
            + work
            + [pltpu.SemaphoreType.DMA((2, ring))]
        )
        cost = 2 * ring * depth
    else:
        shapes = [half]
    return pl.pallas_call(
        functools.partial(backward_kernel, dims, stage, classes),
        out_shape=shapes,
        in_specs=specs,
        out_specs=vmem(len(shapes)),
        scratch_shapes=work,
        compiler_params=pltpu.CompilerParams(vmem_limit_bytes=LIMIT),
        cost_estimate=pl.CostEstimate(
            flops=2 * rows * lanes * cost + rows * lanes * 100,
            bytes_accessed=2 * cost * lanes + 8 * rows * lanes,
            transcendentals=0,
        ),
        name="backward_block",
    )(*operands)


def after(value, earlier):
    if earlier is None:
        return value
    return lax.optimization_barrier((value, earlier))[0]


def ring_steps(piece, z, ring, gate):
    def pairs(step, way):
        if way > 0:
            hops = [(i, i + 1) for i in range(step - 1, ring - 1)]
        else:
            hops = [(i, i - 1) for i in range(1, ring - step + 1)]
        return [(2 * a + core, 2 * b + core) for a, b in hops for core in range(2)]

    low, high = {}, {}
    up, down = piece, piece
    for step in range(1, ring):
        up, down = gate(up), gate(down)
        up = lax.ppermute(up, "dp", pairs(step, 1))
        down = lax.ppermute(down, "dp", pairs(step, -1))
        low[step], high[step] = up, down
        yield up
    result = [piece]
    for j in range(1, ring):
        result.append(jnp.where(z + j < ring, high[j], low[ring - j]))
    yield result


def swap_core(value, count):
    return lax.ppermute(value, "dp", [(i, i ^ 1) for i in range(count)])


def gather_ring(piece, z, ring):
    for result in ring_steps(piece, z, ring, lambda value: value):
        pass
    own = jnp.stack(result)
    return own, swap_core(own, 2 * ring)


def adam_update(weights, first_moment, second_moment, grad_total):
    new_first = beta_first * first_moment + (1.0 - beta_first) * grad_total
    new_second = beta_second * second_moment + (1.0 - beta_second) * grad_total * grad_total
    new_weights = weights - learn_rate * new_first / (jnp.sqrt(new_second) + adam_eps)
    return (new_weights, new_first, new_second)


def shards(spikes, labels, readout, weights, first_moment, second_moment):
    sections = lax.axis_size("section")
    devices = lax.axis_size("dp")
    ring = devices // 2
    s = lax.axis_index("section")
    d = lax.axis_index("dp")
    z, core = d // 2, d % 2
    images, steps, height, width, channels = spikes.shape
    group = images * steps
    rows = height * width * group
    lanes = channels // sections
    depth = weights.shape[1]
    classes = readout.shape[1]
    dims = (sections, height, width, images, steps)
    scal = jnp.stack([s, z, core]).astype(jnp.int32)

    def exchange(values):
        return [
            lax.ppermute(values[k], "section", [(i, i ^ (k + 1)) for i in range(sections)])
            for k in range(sections - 1)
        ]

    def columns(array, k):
        return lax.dynamic_slice_in_dim(array, (s ^ k) * lanes, lanes, 1)

    def pick(options, index):
        return lax.dynamic_index_in_dim(jnp.stack(options), index, 0, keepdims=False)

    pieces = [columns(weights[0], k).astype(jnp.bfloat16) for k in range(sections)]
    pieces = [pieces[0]] + exchange(pieces[1:])
    field = spikes.transpose(2, 3, 0, 1, 4).reshape(rows, channels)
    slices = [columns(field, k) for k in range(sections)]
    padded_classes = -(-classes // 128) * 128
    readout_own = lax.dynamic_slice_in_dim(readout, s * lanes, lanes, 0)
    readout_own = jnp.pad(readout_own, ((0, 0), (0, padded_classes - classes)))

    history = []

    def gate(value):
        if len(history) >= 4:
            value = after(value, history[-4])
        return value

    sources = [None] * sections
    for first in range(0, sections, 2):
        blocks = [b for b in (first, first + 1) if b < sections]
        walks = {b: ring_steps(pick(pieces, s ^ b), z, ring, gate) for b in blocks}
        for step in range(ring):
            for b in blocks:
                sources[b] = next(walks[b])
                if step < ring - 1:
                    history.extend([sources[b], sources[b]])
        for b in blocks:
            own = jnp.stack(sources[b])
            sources[b] = (own, swap_core(own, devices))

    inputs, fired_all = [], []
    for b in range(sections):
        inputs.append(slices)
        last = b == sections - 1
        result = run_forward(dims, last, scal, slices, sources[b], readout_own)
        fired_all.append(result[1])
        if not last:
            slices = [result[0]] + exchange([result[0]] * (sections - 1))
    logits = result[2]
    heads = [logits] + exchange([logits] * (sections - 1))
    heads += [labels[:, None], readout_own]

    def ordered(parts):
        return jnp.concatenate([pick(parts, s ^ j) for j in range(sections)], axis=1)

    own_inputs = [pick([inputs[b][k] for b in range(sections)], s) for k in range(sections)]
    x_all = gather_ring(ordered(own_inputs), z, ring)

    raws = [None] * sections
    for b in reversed(range(sections)):
        stage = 0 if b == sections - 1 else (2 if b == 0 else 1)
        result = run_backward(dims, stage, classes, scal, heads, fired_all[b], sources[b])
        raws[b] = result[0]
        if b > 0:
            heads = [result[1]] + exchange(result[2:])

    sent = [pick(raws, s ^ k) for k in range(sections)]
    own_raw = ordered([sent[0]] + exchange(sent[1:]))
    raw_all = gather_ring(own_raw, z, ring)

    x_all = jnp.concatenate(x_all).reshape(devices, height, width, group, channels)
    x_all = jnp.pad(x_all, ((0, 0), (1, 1), (1, 1), (0, 0), (0, 0)))
    start = d * depth
    channel = start % channels
    step = 1
    while channels % (2 * step) == 0 and depth % (2 * step) == 0:
        step *= 2
    spans = -(-(channels - step + depth) // channels)
    shifted = []
    for i in range(spans):
        offset = jnp.minimum(start // channels + i, 8)
        shifted.append(
            lax.dynamic_slice(
                x_all,
                (0, offset // 3, offset % 3, 0, 0),
                (devices, height, width, group, channels),
            ).reshape(devices * rows, channels)
        )
    cols = lax.dynamic_slice_in_dim(jnp.concatenate(shifted, axis=1), channel, depth, 1)
    raw_all = jnp.concatenate(raw_all).reshape(devices * rows, channels)
    grad = lax.dot_general(
        cols, raw_all, (((0,), (0,)), ((), ())), preferred_element_type=jnp.float32
    )
    return adam_update(weights, first_moment, second_moment, grad[None])


def solution(mesh):
    return jax.shard_map(
        shards,
        mesh=mesh,
        in_specs=(
            P("dp", None, None, None, None),
            P("dp"),
            P(),
            P("section", "dp", None),
            P("section", "dp", None),
            P("section", "dp", None),
        ),
        out_specs=(P("section", "dp", None), P("section", "dp", None), P("section", "dp", None)),
        check_vma=False,
    )
```

time: 997 us -> 540 us (0.54)
  waiting for transfers between devices: 538 us -> 308 us
  other arithmetic: 145 us -> 24.9 us
  matrix products: 114 us -> 21.3 us
  Pallas kernels: 0 us -> 56.6 us
  local copies, waits for them, and re-layouts: 73.7 us -> 29.8 us
  between operations: 14.6 us -> 2.13 us
    reduce_scatter x1 -> x0, waiting for transfers between devices: 184 us -> none  [shards(): lax.psum_scatter(full_grad.astype(jnp.bfloat16), 'dp', scatter_dimension=...]
    all_gather x1 -> x0, waiting for transfers between devices: 171 us -> none  [shards(): kernel = lax.all_gather(local_kernel, 'dp', axis=0, tiled=True)]
    ppermute x14 -> x69, waiting for transfers between devices: 183 us -> 308 us  [the longest x18 209 us: ring_steps(): down = lax.ppermute(down, 'dp', pairs(step, -1))]
    dot_general x11 -> x1, matrix products: 114 us -> 21.3 us  [shards(): lax.dot_general(cols, raw_all, (((0,), (0,)), ((), ())), preferred_elemen...]
    pallas_call x0 -> x8, Pallas kernels: none -> 56.6 us  [the longest x4 30.7 us: run_forward(): pl.pallas_call(functools.partial(forward_kernel, dims, last), out_shape=s...]
    add x44 -> x0, other arithmetic: 56.4 us -> none  [leaky(): membrane = leak_rate * membrane + current[:, step_index]]
    another operation x63 -> x0, local copies, waits for them, and re-layouts: 38.9 us -> none  [the longest x14 34.2 us: unfold(): stacked = jnp.stack(pieces, axis=4)]
    div x32 -> x0, other arithmetic: 32.5 us -> none  [leaky(): fired = jax.nn.sigmoid(spike_slope * (membrane - threshold))]
  transfers between devices with their start and end apart: 16 -> 69, of which waited for: 16 -> 42; matrix products, arithmetic and copies ran while one was open for 2% -> 7% of each run, Pallas kernels for 0% -> 5%
where the time goes in v1:
time: 540 us; the launch traced here: 535 us
  waiting for transfers between devices  308 us (57%)
  starting transfers between devices  92.2 us (17%)
  Pallas kernels  56.6 us (10%)
  local copies, waits for them, and re-layouts  29.8 us (6%)
  other arithmetic  24.9 us (5%)
  matrix products  21.3 us (4%)
    ppermute x18, waiting for transfers between devices, ring_steps(): down = lax.ppermute(down, 'dp', pairs(step, -1))  209 us
    ppermute x27, waiting for transfers between devices, exchange(): lax.ppermute(values[k], 'section', [(i, i ^ k + 1) for i in range(section...  88.5 us
    ppermute x18, starting transfers between devices, ring_steps(): up = lax.ppermute(up, 'dp', pairs(step, 1))  35.8 us
    ppermute x27, starting transfers between devices, exchange(): lax.ppermute(values[k], 'section', [(i, i ^ k + 1) for i in range(section...  33.1 us
    pallas_call x4, Pallas kernels, run_forward(): pl.pallas_call(functools.partial(forward_kernel, dims, last), out_shape=s...  30.7 us
    pallas_call x4, Pallas kernels, run_backward(): pl.pallas_call(functools.partial(backward_kernel, dims, stage, classes),...  26 us
    ppermute x18, starting transfers between devices, ring_steps(): down = lax.ppermute(down, 'dp', pairs(step, -1))  23.3 us
    dot_general x1, matrix products, shards(): lax.dot_general(cols, raw_all, (((0,), (0,)), ((), ())), preferred_elemen...  21.3 us
  transfers between devices with their start and end apart: 69, of which 42 were waited for; matrix products, arithmetic and copies ran while one was open for 7% of the time, Pallas kernels for 5%

profile of v1, /device:TPU:0, one launch (start us, length us, event | category | flops | bytes accessed | tf_op | source)
XLA Modules:
  0.0 534.5 jit_solution(7141048823372555217)
XLA Ops:
  0.7 3.4 dynamic-slice_convert_fusion.3
  4.1 3.0 collective-permute-start.1
  8.5 12.2 %collective-permute-done.1 = bf16[1152,256]{1,0:T(8,128)(2,1)S(1)} collective-permute-done((bf16[1152,256]{1,0:T(8,128)(2,1)}, bf16[1152,256]{1,0:T(8,128)(2,1)S(1)}, u32[]{:S(2)}, u32[]{:S(2)}) %collective-permute-start.1) | collective-permute-done | bytes 589856 | tf_op jit(solution)/shard_map/ppermute | solution.py:346
  20.8 2.5 collective-permute-done
  23.3 10.9 %collective-permute-done.2 = bf16[1152,256]{1,0:T(8,128)(2,1)S(1)} collective-permute-done((bf16[1152,256]{1,0:T(8,128)(2,1)S(1)}, bf16[1152,256]{1,0:T(8,128)(2,1)S(1)}, u32[]{:S(2)}, u32[]{:S(2)}) %collective-permute-start.2) | collective-permute-done | bytes 589856 | tf_op jit(solution)/shard_map/ppermute | solution.py:346
  34.7 3.7 collective-permute-start.14
  39.7 5.4 %collective-permute-start.4 = (bf16[1152,256]{1,0:T(8,128)(2,1)S(1)}, bf16[1152,256]{1,0:T(8,128)(2,1)}, u32[]{:S(2)}, u32[]{:S(2)}) collective-permute-start(bf16[1152,256]{1,0:T(8,128)(2,1)S(1)} %bitcast.136), channel_id=1, source_target_pairs={{0,2},{1,3},{2,4},{3,5},{4,6},{5,7},{8,10},{9,11},{10,12},{11,13},... | collective-permute-start | bytes 1769480 | tf_op jit(solution)/shard_map/ppermute | solution.py:300
  46.4 5.8 %collective-permute-done.14 = bf16[1152,256]{1,0:T(8,128)(2,1)S(1)} collective-permute-done((bf16[1152,256]{1,0:T(8,128)(2,1)S(1)}, bf16[1152,256]{1,0:T(8,128)(2,1)S(1)}, u32[]{:S(2)}, u32[]{:S(2)}) %collective-permute-start.14) | collective-permute-done | bytes 589856 | tf_op jit(solution)/shard_map/ppermute | solution.py:300
  53.6 3.0 collective-permute-done.13
  58.0 4.4 collective-permute-done.4
  63.9 5.4 %collective-permute-done.3 = bf16[1152,256]{1,0:T(8,128)(2,1)} collective-permute-done((bf16[1152,256]{1,0:T(8,128)(2,1)S(1)}, bf16[1152,256]{1,0:T(8,128)(2,1)}, u32[]{:S(2)}, u32[]{:S(2)}) %collective-permute-start.3) | collective-permute-done | bytes 589856 | tf_op jit(solution)/shard_map/ppermute | solution.py:301
  71.3 10.5 %collective-permute-done.17 = bf16[1152,256]{1,0:T(8,128)(2,1)S(1)} collective-permute-done((bf16[1152,256]{1,0:T(8,128)(2,1)}, bf16[1152,256]{1,0:T(8,128)(2,1)S(1)}, u32[]{:S(2)}, u32[]{:S(2)}) %collective-permute-start.17) | collective-permute-done | bytes 589856 | tf_op jit(solution)/shard_map/ppermute | solution.py:301
  83.9 10.7 %collective-permute-done.7 = bf16[1152,256]{1,0:T(8,128)(2,1)} collective-permute-done((bf16[1152,256]{1,0:T(8,128)(2,1)}, bf16[1152,256]{1,0:T(8,128)(2,1)}, u32[]{:S(2)}, u32[]{:S(2)}) %collective-permute-start.7) | collective-permute-done | bytes 589856 | tf_op jit(solution)/shard_map/ppermute | solution.py:301
  97.1 4.6 collective-permute-start.41
  103.1 8.7 %collective-permute-start.24 = (bf16[1152,256]{1,0:T(8,128)(2,1)S(1)}, bf16[1152,256]{1,0:T(8,128)(2,1)S(1)}, u32[]{:S(2)}, u32[]{:S(2)}) collective-permute-start(bf16[1152,256]{1,0:T(8,128)(2,1)S(1)} %bitcast.132), channel_id=1, source_target_pairs={{0,2},{1,3},{2,4},{3,5},{4,6},{5,7},{8,10},{9,11},{10,12},{11,13},... | collective-permute-start | bytes 1769480 | tf_op jit(solution)/shard_map/ppermute | solution.py:300
  114.1 5.7 %collective-permute-done.8 = bf16[1152,256]{1,0:T(8,128)(2,1)S(1)} collective-permute-done((bf16[1152,256]{1,0:T(8,128)(2,1)}, bf16[1152,256]{1,0:T(8,128)(2,1)S(1)}, u32[]{:S(2)}, u32[]{:S(2)}) %collective-permute-start.8) | collective-permute-done | bytes 589856 | tf_op jit(solution)/shard_map/ppermute | solution.py:301
  121.1 1.7 pad_maximum_fusion.3.refs_4_
  123.6 18.8 %collective-permute-done.23 = bf16[1152,256]{1,0:T(8,128)(2,1)S(1)} collective-permute-done((bf16[1152,256]{1,0:T(8,128)(2,1)S(1)}, bf16[1152,256]{1,0:T(8,128)(2,1)S(1)}, u32[]{:S(2)}, u32[]{:S(2)}) %collective-permute-start.23) | collective-permute-done | bytes 589856 | tf_op jit(solution)/shard_map/ppermute | solution.py:301
  145.8 1.7 pad_maximum_fusion.4.refs_4_.refs_5_
  148.2 15.7 %collective-permute-done.27 = bf16[1152,256]{1,0:T(8,128)(2,1)S(1)} collective-permute-done((bf16[1152,256]{1,0:T(8,128)(2,1)S(1)}, bf16[1152,256]{1,0:T(8,128)(2,1)S(1)}, u32[]{:S(2)}, u32[]{:S(2)}) %collective-permute-start.27) | collective-permute-done | bytes 589856 | tf_op jit(solution)/shard_map/ppermute | solution.py:301
  164.7 8.3 %collective-permute-done.44 = bf16[1152,256]{1,0:T(8,128)(2,1)S(1)} collective-permute-done((bf16[1152,256]{1,0:T(8,128)(2,1)S(1)}, bf16[1152,256]{1,0:T(8,128)(2,1)S(1)}, u32[]{:S(2)}, u32[]{:S(2)}) %collective-permute-start.44) | collective-permute-done | bytes 589856 | tf_op jit(solution)/shard_map/ppermute | solution.py:301
  175.9 15.2 %collective-permute-done.28 = bf16[1152,256]{1,0:T(8,128)(2,1)S(1)} collective-permute-done((bf16[1152,256]{1,0:T(8,128)(2,1)S(1)}, bf16[1152,256]{1,0:T(8,128)(2,1)S(1)}, u32[]{:S(2)}, u32[]{:S(2)}) %collective-permute-start.28) | collective-permute-done | bytes 589856 | tf_op jit(solution)/shard_map/ppermute | solution.py:301
  191.7 7.6 %collective-permute-done.45 = bf16[1152,256]{1,0:T(8,128)(2,1)S(1)} collective-permute-done((bf16[1152,256]{1,0:T(8,128)(2,1)S(1)}, bf16[1152,256]{1,0:T(8,128)(2,1)S(1)}, u32[]{:S(2)}, u32[]{:S(2)}) %collective-permute-start.45) | collective-permute-done | bytes 589856 | tf_op jit(solution)/shard_map/ppermute | solution.py:301
  199.3 1.8 pad_maximum_fusion.6.refs_4_.refs_7_
  201.1 1.8 copy.9
  204.6 7.3 %forward_block.4 = (bf16[512,256]{1,0:T(8,128)(2,1)}, f32[2,512,128]{2,1,0:T(8,128)}) custom-call(s32[3]{0:T(128)} %pad_add_fusion.scal, bf16[512,256]{1,0:T(8,128)(2,1)} %get-tuple-element.123.refs_0_, bf16[512,256]{1,0:T(8,128)(2,1)} %get-tuple-element.122.refs_1_, bf16[512,256]{1,0:T(8,128)(2,1)} %get-tuple-element.121.refs_2_, ...), custom_call_target="tpu_custom_call" | custom-call | flops 2415919104 | bytes 4718592 | tf_op jit(solution)/shard_map/forward_block/pallas_call | solution.py:216
  211.9 2.5 collective-permute-start.12
  215.4 6.8 %collective-permute-done.12.refs_3_ = bf16[512,256]{1,0:T(8,128)(2,1)S(1)} collective-permute-done((bf16[512,256]{1,0:T(8,128)(2,1)}, bf16[512,256]{1,0:T(8,128)(2,1)S(1)}, u32[]{:S(2)}, u32[]{:S(2)}) %collective-permute-start.12) | collective-permute-done | bytes 262176 | tf_op jit(solution)/shard_map/ppermute | solution.py:346
  222.2 5.2 collective-permute-done.11.refs_2_
  228.8 7.3 %forward_block.5 = (bf16[512,256]{1,0:T(8,128)(2,1)}, f32[2,512,128]{2,1,0:T(8,128)}) custom-call(s32[3]{0:T(128)} %pad_add_fusion.scal, bf16[512,256]{1,0:T(8,128)(2,1)} %get-tuple-element.48.refs_0_, bf16[512,256]{1,0:T(8,128)(2,1)} %copy-done.12, bf16[512,256]{1,0:T(8,128)(2,1)} %copy-done.10, bf16[512,256]{1,0:T(8,128)(2,1)} %copy-done.19, ...), custom_call_target="tpu_custom_call" | custom-call | flops 2415919104 | bytes 4718592 | tf_op jit(solution)/shard_map/forward_block/pallas_call | solution.py:216
  236.1 1.8 collective-permute-start.22
  239.6 6.8 %collective-permute-done.22.refs_3_ = bf16[512,256]{1,0:T(8,128)(2,1)S(1)} collective-permute-done((bf16[512,256]{1,0:T(8,128)(2,1)}, bf16[512,256]{1,0:T(8,128)(2,1)S(1)}, u32[]{:S(2)}, u32[]{:S(2)}) %collective-permute-start.22) | collective-permute-done | bytes 262176 | tf_op jit(solution)/shard_map/ppermute | solution.py:346
  246.5 4.7 collective-permute-done.21.refs_2_
  252.0 7.3 %forward_block.6 = (bf16[512,256]{1,0:T(8,128)(2,1)}, f32[2,512,128]{2,1,0:T(8,128)}) custom-call(s32[3]{0:T(128)} %pad_add_fusion.scal, bf16[512,256]{1,0:T(8,128)(2,1)} %get-tuple-element.53.refs_0_, bf16[512,256]{1,0:T(8,128)(2,1)} %copy-done.14, bf16[512,256]{1,0:T(8,128)(2,1)} %copy-done.16, bf16[512,256]{1,0:T(8,128)(2,1)} %copy-done.26, ...), custom_call_target="tpu_custom_call" | custom-call | flops 2415919104 | bytes 4718592 | tf_op jit(solution)/shard_map/forward_block/pallas_call | solution.py:216
  265.5 4.2 collective-permute-done.32.refs_3_
  269.7 4.6 collective-permute-done.31.refs_2_
  275.7 8.8 %forward_block.7 = (bf16[512,256]{1,0:T(8,128)(2,1)}, f32[2,512,128]{2,1,0:T(8,128)}, f32[4,1024]{1,0:T(4,128)}) custom-call(s32[3]{0:T(128)} %pad_add_fusion.scal, bf16[512,256]{1,0:T(8,128)(2,1)} %get-tuple-element.59.refs_0_, bf16[512,256]{1,0:T(8,128)(2,1)} %copy-done.21, bf16[512,256]{1,0:T(8,128)(2,1)} %copy-done.23, bf16[512,256]{1,0:T(8,128)(2,1)} %copy-done.29, ...), custom_call_target="tpu_custom_call" | custom-call | flops 2415919104 | bytes 4718592 | tf_op jit(solution)/shard_map/forward_block/pallas_call | solution.py:216
  285.7 2.1 collective-permute-start.48
  289.8 1.8 collective-permute-done.47.refs_1_
  292.3 8.3 %backward_block.4 = (bf16[512,256]{1,0:T(8,128)(2,1)}, f32[512,256]{1,0:T(8,128)}, bf16[512,256]{1,0:T(8,128)(2,1)}, bf16[512,256]{1,0:T(8,128)(2,1)}, bf16[512,256]{1,0:T(8,128)(2,1)}) custom-call(s32[3]{0:T(128)} %pad_add_fusion.scal, f32[4,1024]{1,0:T(4,128)} %get-tuple-element.65.refs_0_, f32[4,1024]{1,0:T(4,128)} %copy-done.46, f32[4,1024]{1,0:T(4,128)} %copy-done.45, ...), custom_call_target="tpu_custom_call" | custom-call | flops 2429026304 | bytes 5767168 | tf_op jit(solution)/shard_map/backward_block/pallas_call | solution.py:266
  304.6 5.5 %collective-permute-done.50.refs_1_ = bf16[512,256]{1,0:T(8,128)(2,1)S(1)} collective-permute-done((bf16[512,256]{1,0:T(8,128)(2,1)}, bf16[512,256]{1,0:T(8,128)(2,1)S(1)}, u32[]{:S(2)}, u32[]{:S(2)}) %collective-permute-start.50) | collective-permute-done | bytes 262176 | tf_op jit(solution)/shard_map/ppermute | solution.py:346
  310.1 3.4 collective-permute-done.51.refs_2_
  314.4 7.6 %backward_block.5 = (bf16[512,256]{1,0:T(8,128)(2,1)}, f32[512,256]{1,0:T(8,128)}, bf16[512,256]{1,0:T(8,128)(2,1)}, bf16[512,256]{1,0:T(8,128)(2,1)}, bf16[512,256]{1,0:T(8,128)(2,1)}) custom-call(s32[3]{0:T(128)} %pad_add_fusion.scal, f32[512,256]{1,0:T(8,128)} %get-tuple-element.67.refs_0_, bf16[512,256]{1,0:T(8,128)(2,1)} %copy-done.40, ...), custom_call_target="tpu_custom_call" | custom-call | flops 2429026304 | bytes 5767168 | tf_op jit(solution)/shard_map/backward_block/pallas_call | solution.py:266
  324.0 1.6 collective-permute-start.55
  326.2 4.5 collective-permute-done.53.refs_1_
  330.7 4.0 collective-permute-done.54.refs_2_
  335.4 7.4 %backward_block.6 = (bf16[512,256]{1,0:T(8,128)(2,1)}, f32[512,256]{1,0:T(8,128)}, bf16[512,256]{1,0:T(8,128)(2,1)}, bf16[512,256]{1,0:T(8,128)(2,1)}, bf16[512,256]{1,0:T(8,128)(2,1)}) custom-call(s32[3]{0:T(128)} %pad_add_fusion.scal, f32[512,256]{1,0:T(8,128)} %get-tuple-element.72.refs_0_, bf16[512,256]{1,0:T(8,128)(2,1)} %copy-done.38, ...), custom_call_target="tpu_custom_call" | custom-call | flops 2429026304 | bytes 5767168 | tf_op jit(solution)/shard_map/backward_block/pallas_call | solution.py:266
  349.6 3.6 collective-permute-done.57.refs_2_
  354.0 2.7 backward_block.7
  362.7 2.6 collective-permute-done.61
  365.3 2.7 collective-permute-done.60
  368.5 1.8 collective-permute-start.63
  372.4 17.0 %collective-permute-done.33 = bf16[512,1024]{1,0:T(8,128)(2,1)S(1)} collective-permute-done((bf16[512,1024]{1,0:T(8,128)(2,1)S(1)}, bf16[512,1024]{1,0:T(8,128)(2,1)S(1)}, u32[]{:S(2)}, u32[]{:S(2)}) %collective-permute-start.33) | collective-permute-done | bytes 1048608 | tf_op jit(solution)/shard_map/ppermute | solution.py:301
  392.2 19.7 %collective-permute-done.62 = bf16[512,1024]{1,0:T(8,128)(2,1)S(1)} collective-permute-done((bf16[512,1024]{1,0:T(8,128)(2,1)S(1)}, bf16[512,1024]{1,0:T(8,128)(2,1)S(1)}, u32[]{:S(2)}, u32[]{:S(2)}) %collective-permute-start.62) | collective-permute-done | bytes 1048608 | tf_op jit(solution)/shard_map/ppermute | solution.py:301
  413.1 21.2 %collective-permute-done.37 = bf16[512,1024]{1,0:T(8,128)(2,1)S(1)} collective-permute-done((bf16[512,1024]{1,0:T(8,128)(2,1)S(1)}, bf16[512,1024]{1,0:T(8,128)(2,1)S(1)}, u32[]{:S(2)}, u32[]{:S(2)}) %collective-permute-start.37) | collective-permute-done | bytes 1048608 | tf_op jit(solution)/shard_map/ppermute | solution.py:301
  437.7 19.0 %collective-permute-done.66 = bf16[512,1024]{1,0:T(8,128)(2,1)S(1)} collective-permute-done((bf16[512,1024]{1,0:T(8,128)(2,1)S(1)}, bf16[512,1024]{1,0:T(8,128)(2,1)S(1)}, u32[]{:S(2)}, u32[]{:S(2)}) %collective-permute-start.66) | collective-permute-done | bytes 1048608 | tf_op jit(solution)/shard_map/ppermute | solution.py:301
  458.1 21.2 %collective-permute-done.38 = bf16[512,1024]{1,0:T(8,128)(2,1)S(1)} collective-permute-done((bf16[512,1024]{1,0:T(8,128)(2,1)S(1)}, bf16[512,1024]{1,0:T(8,128)(2,1)S(1)}, u32[]{:S(2)}, u32[]{:S(2)}) %collective-permute-start.38) | collective-permute-done | bytes 1048608 | tf_op jit(solution)/shard_map/ppermute | solution.py:301
  479.4 2.3 pad_maximum_fusion
  484.7 9.6 %collective-permute-done.67 = bf16[512,1024]{1,0:T(8,128)(2,1)S(1)} collective-permute-done((bf16[512,1024]{1,0:T(8,128)(2,1)S(1)}, bf16[512,1024]{1,0:T(8,128)(2,1)S(1)}, u32[]{:S(2)}, u32[]{:S(2)}) %collective-permute-start.67) | collective-permute-done | bytes 1048608 | tf_op jit(solution)/shard_map/ppermute | solution.py:301
  495.8 2.3 pad_maximum_fusion.1
  499.5 2.6 constant_dynamic-update-slice_fusion
  502.2 6.0 %pad_dynamic-slice_fusion = (bf16[8,4,4,32,1024]{4,3,2,1,0:T(8,128)(2,1)S(1)}, bf16[8,4,4,32,1024]{4,3,2,1,0:T(8,128)(2,1)}) fusion(s32[]{:T(128)S(6)} %select_n.217, s32[]{:T(128)S(6)} %select_n.219, bf16[8,4,4,32,1024]{4,3,2,1,0:T(8,128)(2,1)S(1)} %constant_dynamic-update-slice_fusion, s32[]{:T(128)S(6)} %select_n.213, s32[]{:T(128)S(6)} %select_n.215), kind=kLoop, calls=%fused_computation | loop fusion | bytes 25165840 | tf_op jit(solution)/shard_map/dynamic_slice | solution.py:426
  508.1 4.6 constant_dynamic-update-slice_fusion.4
  512.7 21.3 %divide_subtract_fusion = (f32[1,1152,1024]{2,1,0:T(8,128)}, f32[1,1152,1024]{2,1,0:T(8,128)}, f32[1,1152,1024]{2,1,0:T(8,128)}) fusion(f32[1,1152,1024]{2,1,0:T(8,128)} %param.9, f32[1,1152,1024]{2,1,0:T(8,128)} %param.10, f32[1,1152,1024]{2,1,0:T(8,128)} %param.11, bf16[4096,1024]{1,0:T(8,128)(2,1)} %bitcast.80, s32[]{:T(128)S(6)} %select_n.221, ...), kind=kOutput, calls=%fused_computation.10 | convolution fusion | flops 9695526912 | bytes 53477380 | tf_op jit(solution)/shard_map/dot_general | solution.py:434
  (231 shorter events, 86.2 us)
Async XLA Ops:
  4.1 16.7 %collective-permute-start.1 = (bf16[1152,256]{1,0:T(8,128)(2,1)}, bf16[1152,256]{1,0:T(8,128)(2,1)S(1)}, u32[]{:S(2)}, u32[]{:S(2)}) collective-permute-start(bf16[1152,256]{1,0:T(8,128)(2,1)} %get-tuple-element.97), channel_id=1, source_target_pairs={{0,16},{8,24},{16,0},{24,8},{1,17},{9,25},{17,1},{25,9},{2,18},{10... | collective-permute-start | bytes 1769480 | tf_op jit(solution)/shard_map/ppermute | solution.py:346
  7.0 16.3 %collective-permute-start = (bf16[1152,256]{1,0:T(8,128)(2,1)S(1)}, bf16[1152,256]{1,0:T(8,128)(2,1)S(1)}, u32[]{:S(2)}, u32[]{:S(2)}) collective-permute-start(bf16[1152,256]{1,0:T(8,128)(2,1)S(1)} %get-tuple-element.98), channel_id=1, source_target_pairs={{0,8},{8,0},{16,24},{24,16},{1,9},{9,1},{17,25},{25,17},{2,10},{10... | collective-permute-start | bytes 1769480 | tf_op jit(solution)/shard_map/ppermute | solution.py:346
  8.5 25.7 %collective-permute-start.2 = (bf16[1152,256]{1,0:T(8,128)(2,1)S(1)}, bf16[1152,256]{1,0:T(8,128)(2,1)S(1)}, u32[]{:S(2)}, u32[]{:S(2)}) collective-permute-start(bf16[1152,256]{1,0:T(8,128)(2,1)S(1)} %get-tuple-element.99), channel_id=1, source_target_pairs={{0,24},{8,16},{16,8},{24,0},{1,25},{9,17},{17,9},{25,1},{2,26},{10... | collective-permute-start | bytes 1769480 | tf_op jit(solution)/shard_map/ppermute | solution.py:346
  34.7 17.5 %collective-permute-start.14 = (bf16[1152,256]{1,0:T(8,128)(2,1)S(1)}, bf16[1152,256]{1,0:T(8,128)(2,1)S(1)}, u32[]{:S(2)}, u32[]{:S(2)}) collective-permute-start(bf16[1152,256]{1,0:T(8,128)(2,1)S(1)} %bitcast.134), channel_id=1, source_target_pairs={{0,2},{1,3},{2,4},{3,5},{4,6},{5,7},{8,10},{9,11},{10,12},{11,13},... | collective-permute-start | bytes 1769480 | tf_op jit(solution)/shard_map/ppermute | solution.py:300
  38.4 18.3 %collective-permute-start.13 = (bf16[1152,256]{1,0:T(8,128)(2,1)S(1)}, bf16[1152,256]{1,0:T(8,128)(2,1)}, u32[]{:S(2)}, u32[]{:S(2)}) collective-permute-start(bf16[1152,256]{1,0:T(8,128)(2,1)S(1)} %bitcast.135), channel_id=1, source_target_pairs={{2,0},{3,1},{4,2},{5,3},{6,4},{7,5},{10,8},{11,9},{12,10},{13,11},... | collective-permute-start | bytes 1769480 | tf_op jit(solution)/shard_map/ppermute | solution.py:301
  39.7 22.7 %collective-permute-start.4 = (bf16[1152,256]{1,0:T(8,128)(2,1)S(1)}, bf16[1152,256]{1,0:T(8,128)(2,1)}, u32[]{:S(2)}, u32[]{:S(2)}) collective-permute-start(bf16[1152,256]{1,0:T(8,128)(2,1)S(1)} %bitcast.136), channel_id=1, source_target_pairs={{0,2},{1,3},{2,4},{3,5},{4,6},{5,7},{8,10},{9,11},{10,12},{11,13},... | collective-permute-start | bytes 1769480 | tf_op jit(solution)/shard_map/ppermute | solution.py:300
  45.1 24.2 %collective-permute-start.3 = (bf16[1152,256]{1,0:T(8,128)(2,1)S(1)}, bf16[1152,256]{1,0:T(8,128)(2,1)}, u32[]{:S(2)}, u32[]{:S(2)}) collective-permute-start(bf16[1152,256]{1,0:T(8,128)(2,1)S(1)} %bitcast.137), channel_id=1, source_target_pairs={{2,0},{3,1},{4,2},{5,3},{6,4},{7,5},{10,8},{11,9},{12,10},{13,11},... | collective-permute-start | bytes 1769480 | tf_op jit(solution)/shard_map/ppermute | solution.py:301
  52.1 18.5 %collective-permute-start.15 = (bf16[1152,256]{1,0:T(8,128)(2,1)S(1)}, bf16[1152,256]{1,0:T(8,128)(2,1)}, u32[]{:S(2)}, u32[]{:S(2)}) collective-permute-start(bf16[1152,256]{1,0:T(8,128)(2,1)S(1)} %collective-permute-done.14), channel_id=1, source_target_pairs={{2,4},{3,5},{4,6},{5,7},{10,12},{11,13},{12,14},{13,15},{18,20},{1... | collective-permute-start | bytes 1769480 | tf_op jit(solution)/shard_map/ppermute | solution.py:300
  56.7 25.2 %collective-permute-start.17 = (bf16[1152,256]{1,0:T(8,128)(2,1)}, bf16[1152,256]{1,0:T(8,128)(2,1)S(1)}, u32[]{:S(2)}, u32[]{:S(2)}) collective-permute-start(bf16[1152,256]{1,0:T(8,128)(2,1)} %collective-permute-done.13), channel_id=1, source_target_pairs={{2,0},{3,1},{4,2},{5,3},{10,8},{11,9},{12,10},{13,11},{18,16},{19,... | collective-permute-start | bytes 1769480 | tf_op jit(solution)/shard_map/ppermute | solution.py:301
  62.4 20.7 %collective-permute-start.5 = (bf16[1152,256]{1,0:T(8,128)(2,1)}, bf16[1152,256]{1,0:T(8,128)(2,1)}, u32[]{:S(2)}, u32[]{:S(2)}) collective-permute-start(bf16[1152,256]{1,0:T(8,128)(2,1)} %collective-permute-done.4), channel_id=1, source_target_pairs={{2,4},{3,5},{4,6},{5,7},{10,12},{11,13},{12,14},{13,15},{18,20},{1... | collective-permute-start | bytes 1769480 | tf_op jit(solution)/shard_map/ppermute | solution.py:300
  69.3 25.3 %collective-permute-start.7 = (bf16[1152,256]{1,0:T(8,128)(2,1)}, bf16[1152,256]{1,0:T(8,128)(2,1)}, u32[]{:S(2)}, u32[]{:S(2)}) collective-permute-start(bf16[1152,256]{1,0:T(8,128)(2,1)} %collective-permute-done.3), channel_id=1, source_target_pairs={{2,0},{3,1},{4,2},{5,3},{10,8},{11,9},{12,10},{13,11},{18,16},{19,... | collective-permute-start | bytes 1769480 | tf_op jit(solution)/shard_map/ppermute | solution.py:301
  70.6 26.5 %collective-permute-start.16 = (bf16[1152,256]{1,0:T(8,128)(2,1)}, bf16[1152,256]{1,0:T(8,128)(2,1)S(1)}, u32[]{:S(2)}, u32[]{:S(2)}) collective-permute-start(bf16[1152,256]{1,0:T(8,128)(2,1)} %collective-permute-done.15), channel_id=1, source_target_pairs={{4,6},{5,7},{12,14},{13,15},{20,22},{21,23},{28,30},{29,31}} | collective-permute-start | bytes 1769480 | tf_op jit(solution)/shard_map/ppermute | solution.py:300
  81.9 61.2 %collective-permute-start.18 = (bf16[1152,256]{1,0:T(8,128)(2,1)S(1)}, bf16[1152,256]{1,0:T(8,128)(2,1)S(1)}, u32[]{:S(2)}, u32[]{:S(2)}) collective-permute-start(bf16[1152,256]{1,0:T(8,128)(2,1)S(1)} %collective-permute-done.17), channel_id=1, source_target_pairs={{2,0},{3,1},{10,8},{11,9},{18,16},{19,17},{26,24},{27,25}} | collective-permute-start | bytes 1769480 | tf_op jit(solution)/shard_map/ppermute | solution.py:301
  83.2 19.9 %collective-permute-start.6 = (bf16[1152,256]{1,0:T(8,128)(2,1)}, bf16[1152,256]{1,0:T(8,128)(2,1)S(1)}, u32[]{:S(2)}, u32[]{:S(2)}) collective-permute-start(bf16[1152,256]{1,0:T(8,128)(2,1)} %collective-permute-done.5), channel_id=1, source_target_pairs={{4,6},{5,7},{12,14},{13,15},{20,22},{21,23},{28,30},{29,31}} | collective-permute-start | bytes 1769480 | tf_op jit(solution)/shard_map/ppermute | solution.py:300
  94.6 25.2 %collective-permute-start.8 = (bf16[1152,256]{1,0:T(8,128)(2,1)}, bf16[1152,256]{1,0:T(8,128)(2,1)S(1)}, u32[]{:S(2)}, u32[]{:S(2)}) collective-permute-start(bf16[1152,256]{1,0:T(8,128)(2,1)} %collective-permute-done.7), channel_id=1, source_target_pairs={{2,0},{3,1},{10,8},{11,9},{18,16},{19,17},{26,24},{27,25}} | collective-permute-start | bytes 1769480 | tf_op jit(solution)/shard_map/ppermute | solution.py:301
  97.1 25.7 %collective-permute-start.41 = (bf16[1152,256]{1,0:T(8,128)(2,1)S(1)}, bf16[1152,256]{1,0:T(8,128)(2,1)S(1)}, u32[]{:S(2)}, u32[]{:S(2)}) collective-permute-start(bf16[1152,256]{1,0:T(8,128)(2,1)S(1)} %bitcast.130), channel_id=1, source_target_pairs={{0,2},{1,3},{2,4},{3,5},{4,6},{5,7},{8,10},{9,11},{10,12},{11,13},... | collective-permute-start | bytes 1769480 | tf_op jit(solution)/shard_map/ppermute | solution.py:300
  101.7 42.7 %collective-permute-start.40 = (bf16[1152,256]{1,0:T(8,128)(2,1)S(1)}, bf16[1152,256]{1,0:T(8,128)(2,1)S(1)}, u32[]{:S(2)}, u32[]{:S(2)}) collective-permute-start(bf16[1152,256]{1,0:T(8,128)(2,1)S(1)} %bitcast.131), channel_id=1, source_target_pairs={{2,0},{3,1},{4,2},{5,3},{6,4},{7,5},{10,8},{11,9},{12,10},{13,11},... | collective-permute-start | bytes 1769480 | tf_op jit(solution)/shard_map/ppermute | solution.py:301
  103.1 19.8 %collective-permute-start.24 = (bf16[1152,256]{1,0:T(8,128)(2,1)S(1)}, bf16[1152,256]{1,0:T(8,128)(2,1)S(1)}, u32[]{:S(2)}, u32[]{:S(2)}) collective-permute-start(bf16[1152,256]{1,0:T(8,128)(2,1)S(1)} %bitcast.132), channel_id=1, source_target_pairs={{0,2},{1,3},{2,4},{3,5},{4,6},{5,7},{8,10},{9,11},{10,12},{11,13},... | collective-permute-start | bytes 1769480 | tf_op jit(solution)/shard_map/ppermute | solution.py:300
  119.8 22.6 %collective-permute-start.23 = (bf16[1152,256]{1,0:T(8,128)(2,1)S(1)}, bf16[1152,256]{1,0:T(8,128)(2,1)S(1)}, u32[]{:S(2)}, u32[]{:S(2)}) collective-permute-start(bf16[1152,256]{1,0:T(8,128)(2,1)S(1)} %bitcast.133), channel_id=1, source_target_pairs={{2,0},{3,1},{4,2},{5,3},{6,4},{7,5},{10,8},{11,9},{12,10},{13,11},... | collective-permute-start | bytes 1769480 | tf_op jit(solution)/shard_map/ppermute | solution.py:301
  122.8 81.7 %collective-permute-start.9 = (bf16[4,1152,256]{2,1,0:T(8,128)(2,1)}, bf16[4,1152,256]{2,1,0:T(8,128)(2,1)}, u32[]{:S(2)}, u32[]{:S(2)}) collective-permute-start(bf16[4,1152,256]{2,1,0:T(8,128)(2,1)} %pad_maximum_fusion.3.refs_4_), channel_id=1, source_target_pairs={{0,1},{1,0},{2,3},{3,2},{4,5},{5,4},{6,7},{7,6},{8,9},{9,8},{10,11... | collective-permute-start | bytes 7077896 | tf_op jit(solution)/shard_map/ppermute | solution.py:311
  122.9 24.6 %collective-permute-start.42 = (bf16[1152,256]{1,0:T(8,128)(2,1)S(1)}, bf16[1152,256]{1,0:T(8,128)(2,1)S(1)}, u32[]{:S(2)}, u32[]{:S(2)}) collective-permute-start(bf16[1152,256]{1,0:T(8,128)(2,1)S(1)} %collective-permute-done.41), channel_id=1, source_target_pairs={{2,4},{3,5},{4,6},{5,7},{10,12},{11,13},{12,14},{13,15},{18,20},{1... | collective-permute-start | bytes 1769480 | tf_op jit(solution)/shard_map/ppermute | solution.py:300
  143.1 20.8 %collective-permute-start.27 = (bf16[1152,256]{1,0:T(8,128)(2,1)S(1)}, bf16[1152,256]{1,0:T(8,128)(2,1)S(1)}, u32[]{:S(2)}, u32[]{:S(2)}) collective-permute-start(bf16[1152,256]{1,0:T(8,128)(2,1)S(1)} %collective-permute-done.23), channel_id=1, source_target_pairs={{2,0},{3,1},{4,2},{5,3},{10,8},{11,9},{12,10},{13,11},{18,16},{19,... | collective-permute-start | bytes 1769480 | tf_op jit(solution)/shard_map/ppermute | solution.py:301
  144.5 28.5 %collective-permute-start.44 = (bf16[1152,256]{1,0:T(8,128)(2,1)S(1)}, bf16[1152,256]{1,0:T(8,128)(2,1)S(1)}, u32[]{:S(2)}, u32[]{:S(2)}) collective-permute-start(bf16[1152,256]{1,0:T(8,128)(2,1)S(1)} %collective-permute-done.40), channel_id=1, source_target_pairs={{2,0},{3,1},{4,2},{5,3},{10,8},{11,9},{12,10},{13,11},{18,16},{19,... | collective-permute-start | bytes 1769480 | tf_op jit(solution)/shard_map/ppermute | solution.py:301
  147.5 67.4 %collective-permute-start.19 = (bf16[4,1152,256]{2,1,0:T(8,128)(2,1)}, bf16[4,1152,256]{2,1,0:T(8,128)(2,1)}, u32[]{:S(2)}, u32[]{:S(2)}) collective-permute-start(bf16[4,1152,256]{2,1,0:T(8,128)(2,1)} %pad_maximum_fusion.4.refs_4_.refs_5_), channel_id=1, source_target_pairs={{0,1},{1,0},{2,3},{3,2},{4,5},{5,4},{6,7},{7,6},{8,9},{9,8},{10,11... | collective-permute-start | bytes 7077896 | tf_op jit(solution)/shard_map/ppermute | solution.py:311
  147.5 44.1 %collective-permute-start.43 = (bf16[1152,256]{1,0:T(8,128)(2,1)S(1)}, bf16[1152,256]{1,0:T(8,128)(2,1)S(1)}, u32[]{:S(2)}, u32[]{:S(2)}) collective-permute-start(bf16[1152,256]{1,0:T(8,128)(2,1)S(1)} %collective-permute-done.42), channel_id=1, source_target_pairs={{4,6},{5,7},{12,14},{13,15},{20,22},{21,23},{28,30},{29,31}} | collective-permute-start | bytes 1769480 | tf_op jit(solution)/shard_map/ppermute | solution.py:300
  163.9 10.4 %collective-permute-start.26 = (bf16[1152,256]{1,0:T(8,128)(2,1)S(1)}, bf16[1152,256]{1,0:T(8,128)(2,1)S(1)}, u32[]{:S(2)}, u32[]{:S(2)}) collective-permute-start(bf16[1152,256]{1,0:T(8,128)(2,1)S(1)} %collective-permute-done.25), channel_id=1, source_target_pairs={{4,6},{5,7},{12,14},{13,15},{20,22},{21,23},{28,30},{29,31}} | collective-permute-start | bytes 1769480 | tf_op jit(solution)/shard_map/ppermute | solution.py:300
  172.9 18.1 %collective-permute-start.28 = (bf16[1152,256]{1,0:T(8,128)(2,1)S(1)}, bf16[1152,256]{1,0:T(8,128)(2,1)S(1)}, u32[]{:S(2)}, u32[]{:S(2)}) collective-permute-start(bf16[1152,256]{1,0:T(8,128)(2,1)S(1)} %collective-permute-done.27), channel_id=1, source_target_pairs={{2,0},{3,1},{10,8},{11,9},{18,16},{19,17},{26,24},{27,25}} | collective-permute-start | bytes 1769480 | tf_op jit(solution)/shard_map/ppermute | solution.py:301
  174.3 24.9 %collective-permute-start.45 = (bf16[1152,256]{1,0:T(8,128)(2,1)S(1)}, bf16[1152,256]{1,0:T(8,128)(2,1)S(1)}, u32[]{:S(2)}, u32[]{:S(2)}) collective-permute-start(bf16[1152,256]{1,0:T(8,128)(2,1)S(1)} %collective-permute-done.44), channel_id=1, source_target_pairs={{2,0},{3,1},{10,8},{11,9},{18,16},{19,17},{26,24},{27,25}} | collective-permute-start | bytes 1769480 | tf_op jit(solution)/shard_map/ppermute | solution.py:301
  191.5 59.8 %collective-permute-start.29 = (bf16[4,1152,256]{2,1,0:T(8,128)(2,1)S(1)}, bf16[4,1152,256]{2,1,0:T(8,128)(2,1)}, u32[]{:S(2)}, u32[]{:S(2)}) collective-permute-start(bf16[4,1152,256]{2,1,0:T(8,128)(2,1)S(1)} %pad_maximum_fusion.5.refs_4_.refs_5_), channel_id=1, source_target_pairs={{0,1},{1,0},{2,3},{3,2},{4,5},{5,4},{6,7},{7,6},{8,9},{9,8},{10,11... | collective-permute-start | bytes 7077896 | tf_op jit(solution)/shard_map/ppermute | solution.py:311
  201.0 64.4 %collective-permute-start.46 = (bf16[4,1152,256]{2,1,0:T(8,128)(2,1)}, bf16[4,1152,256]{2,1,0:T(8,128)(2,1)}, u32[]{:S(2)}, u32[]{:S(2)}) collective-permute-start(bf16[4,1152,256]{2,1,0:T(8,128)(2,1)} %pad_maximum_fusion.6.refs_4_.refs_7_), channel_id=1, source_target_pairs={{0,1},{1,0},{2,3},{3,2},{4,5},{5,4},{6,7},{7,6},{8,9},{9,8},{10,11... | collective-permute-start | bytes 7077896 | tf_op jit(solution)/shard_map/ppermute | solution.py:311
  211.9 10.3 %collective-permute-start.12 = (bf16[512,256]{1,0:T(8,128)(2,1)}, bf16[512,256]{1,0:T(8,128)(2,1)S(1)}, u32[]{:S(2)}, u32[]{:S(2)}) collective-permute-start(bf16[512,256]{1,0:T(8,128)(2,1)} %get-tuple-element.48.refs_0_), channel_id=1, source_target_pairs={{0,24},{8,16},{16,8},{24,0},{1,25},{9,17},{17,9},{25,1},{2,26},{10... | collective-permute-start | bytes 786440 | tf_op jit(solution)/shard_map/ppermute | solution.py:346
  214.4 13.0 %collective-permute-start.11 = (bf16[512,256]{1,0:T(8,128)(2,1)}, bf16[512,256]{1,0:T(8,128)(2,1)S(1)}, u32[]{:S(2)}, u32[]{:S(2)}) collective-permute-start(bf16[512,256]{1,0:T(8,128)(2,1)} %get-tuple-element.48.refs_0_), channel_id=1, source_target_pairs={{0,16},{8,24},{16,0},{24,8},{1,17},{9,25},{17,1},{25,9},{2,18},{10... | collective-permute-start | bytes 786440 | tf_op jit(solution)/shard_map/ppermute | solution.py:346
  214.9 12.6 %collective-permute-start.10 = (bf16[512,256]{1,0:T(8,128)(2,1)}, bf16[512,256]{1,0:T(8,128)(2,1)S(1)}, u32[]{:S(2)}, u32[]{:S(2)}) collective-permute-start(bf16[512,256]{1,0:T(8,128)(2,1)} %get-tuple-element.48.refs_0_), channel_id=1, source_target_pairs={{0,8},{8,0},{16,24},{24,16},{1,9},{9,1},{17,25},{25,17},{2,10},{10... | collective-permute-start | bytes 786440 | tf_op jit(solution)/shard_map/ppermute | solution.py:346
  236.1 10.4 %collective-permute-start.22 = (bf16[512,256]{1,0:T(8,128)(2,1)}, bf16[512,256]{1,0:T(8,128)(2,1)S(1)}, u32[]{:S(2)}, u32[]{:S(2)}) collective-permute-start(bf16[512,256]{1,0:T(8,128)(2,1)} %get-tuple-element.53.refs_0_), channel_id=1, source_target_pairs={{0,24},{8,16},{16,8},{24,0},{1,25},{9,17},{17,9},{25,1},{2,26},{10... | collective-permute-start | bytes 786440 | tf_op jit(solution)/shard_map/ppermute | solution.py:346
  237.9 13.2 %collective-permute-start.21 = (bf16[512,256]{1,0:T(8,128)(2,1)}, bf16[512,256]{1,0:T(8,128)(2,1)S(1)}, u32[]{:S(2)}, u32[]{:S(2)}) collective-permute-start(bf16[512,256]{1,0:T(8,128)(2,1)} %get-tuple-element.53.refs_0_), channel_id=1, source_target_pairs={{0,16},{8,24},{16,0},{24,8},{1,17},{9,25},{17,1},{25,9},{2,18},{10... | collective-permute-start | bytes 786440 | tf_op jit(solution)/shard_map/ppermute | solution.py:346
  239.1 12.1 %collective-permute-start.20 = (bf16[512,256]{1,0:T(8,128)(2,1)}, bf16[512,256]{1,0:T(8,128)(2,1)S(1)}, u32[]{:S(2)}, u32[]{:S(2)}) collective-permute-start(bf16[512,256]{1,0:T(8,128)(2,1)} %get-tuple-element.53.refs_0_), channel_id=1, source_target_pairs={{0,8},{8,0},{16,24},{24,16},{1,9},{9,1},{17,25},{25,17},{2,10},{10... | collective-permute-start | bytes 786440 | tf_op jit(solution)/shard_map/ppermute | solution.py:346
  259.3 10.4 %collective-permute-start.32 = (bf16[512,256]{1,0:T(8,128)(2,1)}, bf16[512,256]{1,0:T(8,128)(2,1)S(1)}, u32[]{:S(2)}, u32[]{:S(2)}) collective-permute-start(bf16[512,256]{1,0:T(8,128)(2,1)} %get-tuple-element.59.refs_0_), channel_id=1, source_target_pairs={{0,24},{8,16},{16,8},{24,0},{1,25},{9,17},{17,9},{25,1},{2,26},{10... | collective-permute-start | bytes 786440 | tf_op jit(solution)/shard_map/ppermute | solution.py:346
  260.8 13.5 %collective-permute-start.31 = (bf16[512,256]{1,0:T(8,128)(2,1)}, bf16[512,256]{1,0:T(8,128)(2,1)S(1)}, u32[]{:S(2)}, u32[]{:S(2)}) collective-permute-start(bf16[512,256]{1,0:T(8,128)(2,1)} %get-tuple-element.59.refs_0_), channel_id=1, source_target_pairs={{0,16},{8,24},{16,0},{24,8},{1,17},{9,25},{17,1},{25,9},{2,18},{10... | collective-permute-start | bytes 786440 | tf_op jit(solution)/shard_map/ppermute | solution.py:346
  262.3 12.1 %collective-permute-start.30 = (bf16[512,256]{1,0:T(8,128)(2,1)}, bf16[512,256]{1,0:T(8,128)(2,1)S(1)}, u32[]{:S(2)}, u32[]{:S(2)}) collective-permute-start(bf16[512,256]{1,0:T(8,128)(2,1)} %get-tuple-element.59.refs_0_), channel_id=1, source_target_pairs={{0,8},{8,0},{16,24},{24,16},{1,9},{9,1},{17,25},{25,17},{2,10},{10... | collective-permute-start | bytes 786440 | tf_op jit(solution)/shard_map/ppermute | solution.py:346
  300.6 9.5 %collective-permute-start.50 = (bf16[512,256]{1,0:T(8,128)(2,1)}, bf16[512,256]{1,0:T(8,128)(2,1)S(1)}, u32[]{:S(2)}, u32[]{:S(2)}) collective-permute-start(bf16[512,256]{1,0:T(8,128)(2,1)} %get-tuple-element.68), channel_id=1, source_target_pairs={{0,8},{8,0},{16,24},{24,16},{1,9},{9,1},{17,25},{25,17},{2,10},{10... | collective-permute-start | bytes 786440 | tf_op jit(solution)/shard_map/ppermute | solution.py:346
  301.2 12.4 %collective-permute-start.51 = (bf16[512,256]{1,0:T(8,128)(2,1)}, bf16[512,256]{1,0:T(8,128)(2,1)S(1)}, u32[]{:S(2)}, u32[]{:S(2)}) collective-permute-start(bf16[512,256]{1,0:T(8,128)(2,1)} %get-tuple-element.69), channel_id=1, source_target_pairs={{0,16},{8,24},{16,0},{24,8},{1,17},{9,25},{17,1},{25,9},{2,18},{10... | collective-permute-start | bytes 786440 | tf_op jit(solution)/shard_map/ppermute | solution.py:346
  302.7 10.8 %collective-permute-start.52 = (bf16[512,256]{1,0:T(8,128)(2,1)}, bf16[512,256]{1,0:T(8,128)(2,1)S(1)}, u32[]{:S(2)}, u32[]{:S(2)}) collective-permute-start(bf16[512,256]{1,0:T(8,128)(2,1)} %get-tuple-element.70), channel_id=1, source_target_pairs={{0,24},{8,16},{16,8},{24,0},{1,25},{9,17},{17,9},{25,1},{2,26},{10... | collective-permute-start | bytes 786440 | tf_op jit(solution)/shard_map/ppermute | solution.py:346
  322.0 8.7 %collective-permute-start.53 = (bf16[512,256]{1,0:T(8,128)(2,1)}, bf16[512,256]{1,0:T(8,128)(2,1)S(1)}, u32[]{:S(2)}, u32[]{:S(2)}) collective-permute-start(bf16[512,256]{1,0:T(8,128)(2,1)} %get-tuple-element.73), channel_id=1, source_target_pairs={{0,8},{8,0},{16,24},{24,16},{1,9},{9,1},{17,25},{25,17},{2,10},{10... | collective-permute-start | bytes 786440 | tf_op jit(solution)/shard_map/ppermute | solution.py:346
  323.3 11.3 %collective-permute-start.54 = (bf16[512,256]{1,0:T(8,128)(2,1)}, bf16[512,256]{1,0:T(8,128)(2,1)S(1)}, u32[]{:S(2)}, u32[]{:S(2)}) collective-permute-start(bf16[512,256]{1,0:T(8,128)(2,1)} %get-tuple-element.74), channel_id=1, source_target_pairs={{0,16},{8,24},{16,0},{24,8},{1,17},{9,25},{17,1},{25,9},{2,18},{10... | collective-permute-start | bytes 786440 | tf_op jit(solution)/shard_map/ppermute | solution.py:346
  324.0 10.7 %collective-permute-start.55 = (bf16[512,256]{1,0:T(8,128)(2,1)}, bf16[512,256]{1,0:T(8,128)(2,1)S(1)}, u32[]{:S(2)}, u32[]{:S(2)}) collective-permute-start(bf16[512,256]{1,0:T(8,128)(2,1)} %get-tuple-element.75), channel_id=1, source_target_pairs={{0,24},{8,16},{16,8},{24,0},{1,25},{9,17},{17,9},{25,1},{2,26},{10... | collective-permute-start | bytes 786440 | tf_op jit(solution)/shard_map/ppermute | solution.py:346
  343.6 9.6 %collective-permute-start.57 = (bf16[512,256]{1,0:T(8,128)(2,1)}, bf16[512,256]{1,0:T(8,128)(2,1)S(1)}, u32[]{:S(2)}, u32[]{:S(2)}) collective-permute-start(bf16[512,256]{1,0:T(8,128)(2,1)} %get-tuple-element.79), channel_id=1, source_target_pairs={{0,16},{8,24},{16,0},{24,8},{1,17},{9,25},{17,1},{25,9},{2,18},{10... | collective-permute-start | bytes 786440 | tf_op jit(solution)/shard_map/ppermute | solution.py:346
  345.1 8.1 %collective-permute-start.58 = (bf16[512,256]{1,0:T(8,128)(2,1)}, bf16[512,256]{1,0:T(8,128)(2,1)S(1)}, u32[]{:S(2)}, u32[]{:S(2)}) collective-permute-start(bf16[512,256]{1,0:T(8,128)(2,1)} %get-tuple-element.80), channel_id=1, source_target_pairs={{0,24},{8,16},{16,8},{24,0},{1,25},{9,17},{17,9},{25,1},{2,26},{10... | collective-permute-start | bytes 786440 | tf_op jit(solution)/shard_map/ppermute | solution.py:346
  346.8 23.5 %collective-permute-start.34 = (bf16[512,1024]{1,0:T(8,128)(2,1)S(1)}, bf16[512,1024]{1,0:T(8,128)(2,1)S(1)}, u32[]{:S(2)}, u32[]{:S(2)}) collective-permute-start(bf16[512,1024]{1,0:T(8,128)(2,1)S(1)} %get-tuple-element.105), channel_id=1, source_target_pairs={{0,2},{1,3},{2,4},{3,5},{4,6},{5,7},{8,10},{9,11},{10,12},{11,13},... | collective-permute-start | bytes 3145736 | tf_op jit(solution)/shard_map/ppermute | solution.py:300
  357.8 7.4 %collective-permute-start.61 = (bf16[512,256]{1,0:T(8,128)(2,1)S(1)}, bf16[512,256]{1,0:T(8,128)(2,1)S(1)}, u32[]{:S(2)}, u32[]{:S(2)}) collective-permute-start(bf16[512,256]{1,0:T(8,128)(2,1)S(1)} %get-tuple-element.117), channel_id=1, source_target_pairs={{0,24},{8,16},{16,8},{24,0},{1,25},{9,17},{17,9},{25,1},{2,26},{10... | collective-permute-start | bytes 786440 | tf_op jit(solution)/shard_map/ppermute | solution.py:346
  359.3 8.7 %collective-permute-start.60 = (bf16[512,256]{1,0:T(8,128)(2,1)S(1)}, bf16[512,256]{1,0:T(8,128)(2,1)S(1)}, u32[]{:S(2)}, u32[]{:S(2)}) collective-permute-start(bf16[512,256]{1,0:T(8,128)(2,1)S(1)} %get-tuple-element.118), channel_id=1, source_target_pairs={{0,16},{8,24},{16,0},{24,8},{1,17},{9,25},{17,1},{25,9},{2,18},{10... | collective-permute-start | bytes 786440 | tf_op jit(solution)/shard_map/ppermute | solution.py:346
  360.9 7.3 %collective-permute-start.59 = (bf16[512,256]{1,0:T(8,128)(2,1)S(1)}, bf16[512,256]{1,0:T(8,128)(2,1)S(1)}, u32[]{:S(2)}, u32[]{:S(2)}) collective-permute-start(bf16[512,256]{1,0:T(8,128)(2,1)S(1)} %get-tuple-element.119), channel_id=1, source_target_pairs={{0,8},{8,0},{16,24},{24,16},{1,9},{9,1},{17,25},{25,17},{2,10},{10... | collective-permute-start | bytes 786440 | tf_op jit(solution)/shard_map/ppermute | solution.py:346
  361.4 28.0 %collective-permute-start.33 = (bf16[512,1024]{1,0:T(8,128)(2,1)S(1)}, bf16[512,1024]{1,0:T(8,128)(2,1)S(1)}, u32[]{:S(2)}, u32[]{:S(2)}) collective-permute-start(bf16[512,1024]{1,0:T(8,128)(2,1)S(1)} %get-tuple-element.105), channel_id=1, source_target_pairs={{2,0},{3,1},{4,2},{5,3},{6,4},{7,5},{10,8},{11,9},{12,10},{13,11},... | collective-permute-start | bytes 3145736 | tf_op jit(solution)/shard_map/ppermute | solution.py:301
  368.5 22.1 %collective-permute-start.63 = (bf16[512,1024]{1,0:T(8,128)(2,1)S(1)}, bf16[512,1024]{1,0:T(8,128)(2,1)S(1)}, u32[]{:S(2)}, u32[]{:S(2)}) collective-permute-start(bf16[512,1024]{1,0:T(8,128)(2,1)S(1)} %get-tuple-element.111), channel_id=1, source_target_pairs={{0,2},{1,3},{2,4},{3,5},{4,6},{5,7},{8,10},{9,11},{10,12},{11,13},... | collective-permute-start | bytes 3145736 | tf_op jit(solution)/shard_map/ppermute | solution.py:300
  370.3 21.1 %collective-permute-start.35 = (bf16[512,1024]{1,0:T(8,128)(2,1)S(1)}, bf16[512,1024]{1,0:T(8,128)(2,1)S(1)}, u32[]{:S(2)}, u32[]{:S(2)}) collective-permute-start(bf16[512,1024]{1,0:T(8,128)(2,1)S(1)} %collective-permute-done.34), channel_id=1, source_target_pairs={{2,4},{3,5},{4,6},{5,7},{10,12},{11,13},{12,14},{13,15},{18,20},{1... | collective-permute-start | bytes 3145736 | tf_op jit(solution)/shard_map/ppermute | solution.py:300
  371.1 40.8 %collective-permute-start.62 = (bf16[512,1024]{1,0:T(8,128)(2,1)S(1)}, bf16[512,1024]{1,0:T(8,128)(2,1)S(1)}, u32[]{:S(2)}, u32[]{:S(2)}) collective-permute-start(bf16[512,1024]{1,0:T(8,128)(2,1)S(1)} %get-tuple-element.111), channel_id=1, source_target_pairs={{2,0},{3,1},{4,2},{5,3},{6,4},{7,5},{10,8},{11,9},{12,10},{13,11},... | collective-permute-start | bytes 3145736 | tf_op jit(solution)/shard_map/ppermute | solution.py:301
  389.4 44.9 %collective-permute-start.37 = (bf16[512,1024]{1,0:T(8,128)(2,1)S(1)}, bf16[512,1024]{1,0:T(8,128)(2,1)S(1)}, u32[]{:S(2)}, u32[]{:S(2)}) collective-permute-start(bf16[512,1024]{1,0:T(8,128)(2,1)S(1)} %collective-permute-done.33), channel_id=1, source_target_pairs={{2,0},{3,1},{4,2},{5,3},{10,8},{11,9},{12,10},{13,11},{18,16},{19,... | collective-permute-start | bytes 3145736 | tf_op jit(solution)/shard_map/ppermute | solution.py:301
  390.7 46.0 %collective-permute-start.64 = (bf16[512,1024]{1,0:T(8,128)(2,1)S(1)}, bf16[512,1024]{1,0:T(8,128)(2,1)S(1)}, u32[]{:S(2)}, u32[]{:S(2)}) collective-permute-start(bf16[512,1024]{1,0:T(8,128)(2,1)S(1)} %collective-permute-done.63), channel_id=1, source_target_pairs={{2,4},{3,5},{4,6},{5,7},{10,12},{11,13},{12,14},{13,15},{18,20},{1... | collective-permute-start | bytes 3145736 | tf_op jit(solution)/shard_map/ppermute | solution.py:300
  391.4 46.2 %collective-permute-start.36 = (bf16[512,1024]{1,0:T(8,128)(2,1)S(1)}, bf16[512,1024]{1,0:T(8,128)(2,1)S(1)}, u32[]{:S(2)}, u32[]{:S(2)}) collective-permute-start(bf16[512,1024]{1,0:T(8,128)(2,1)S(1)} %collective-permute-done.35), channel_id=1, source_target_pairs={{4,6},{5,7},{12,14},{13,15},{20,22},{21,23},{28,30},{29,31}} | collective-permute-start | bytes 3145736 | tf_op jit(solution)/shard_map/ppermute | solution.py:300
  411.9 44.9 %collective-permute-start.66 = (bf16[512,1024]{1,0:T(8,128)(2,1)S(1)}, bf16[512,1024]{1,0:T(8,128)(2,1)S(1)}, u32[]{:S(2)}, u32[]{:S(2)}) collective-permute-start(bf16[512,1024]{1,0:T(8,128)(2,1)S(1)} %collective-permute-done.62), channel_id=1, source_target_pairs={{2,0},{3,1},{4,2},{5,3},{10,8},{11,9},{12,10},{13,11},{18,16},{19,... | collective-permute-start | bytes 3145736 | tf_op jit(solution)/shard_map/ppermute | solution.py:301
  434.3 44.9 %collective-permute-start.38 = (bf16[512,1024]{1,0:T(8,128)(2,1)S(1)}, bf16[512,1024]{1,0:T(8,128)(2,1)S(1)}, u32[]{:S(2)}, u32[]{:S(2)}) collective-permute-start(bf16[512,1024]{1,0:T(8,128)(2,1)S(1)} %collective-permute-done.37), channel_id=1, source_target_pairs={{2,0},{3,1},{10,8},{11,9},{18,16},{19,17},{26,24},{27,25}} | collective-permute-start | bytes 3145736 | tf_op jit(solution)/shard_map/ppermute | solution.py:301
  436.7 45.0 %collective-permute-start.65 = (bf16[512,1024]{1,0:T(8,128)(2,1)S(1)}, bf16[512,1024]{1,0:T(8,128)(2,1)S(1)}, u32[]{:S(2)}, u32[]{:S(2)}) collective-permute-start(bf16[512,1024]{1,0:T(8,128)(2,1)S(1)} %collective-permute-done.64), channel_id=1, source_target_pairs={{4,6},{5,7},{12,14},{13,15},{20,22},{21,23},{28,30},{29,31}} | collective-permute-start | bytes 3145736 | tf_op jit(solution)/shard_map/ppermute | solution.py:300
  456.8 37.6 %collective-permute-start.67 = (bf16[512,1024]{1,0:T(8,128)(2,1)S(1)}, bf16[512,1024]{1,0:T(8,128)(2,1)S(1)}, u32[]{:S(2)}, u32[]{:S(2)}) collective-permute-start(bf16[512,1024]{1,0:T(8,128)(2,1)S(1)} %collective-permute-done.66), channel_id=1, source_target_pairs={{2,0},{3,1},{10,8},{11,9},{18,16},{19,17},{26,24},{27,25}} | collective-permute-start | bytes 3145736 | tf_op jit(solution)/shard_map/ppermute | solution.py:301
  481.7 17.8 %collective-permute-start.39 = (bf16[4,512,1024]{2,1,0:T(8,128)(2,1)}, bf16[4,512,1024]{2,1,0:T(8,128)(2,1)}, u32[]{:S(2)}, u32[]{:S(2)}) collective-permute-start(bf16[4,512,1024]{2,1,0:T(8,128)(2,1)} %pad_maximum_fusion), channel_id=1, source_target_pairs={{0,1},{1,0},{2,3},{3,2},{4,5},{5,4},{6,7},{7,6},{8,9},{9,8},{10,11... | collective-permute-start | bytes 12582920 | tf_op jit(solution)/shard_map/ppermute | solution.py:311
  498.1 10.1 %collective-permute-start.68 = (bf16[4,512,1024]{2,1,0:T(8,128)(2,1)}, bf16[4,512,1024]{2,1,0:T(8,128)(2,1)}, u32[]{:S(2)}, u32[]{:S(2)}) collective-permute-start(bf16[4,512,1024]{2,1,0:T(8,128)(2,1)} %pad_maximum_fusion.1), channel_id=1, source_target_pairs={{0,1},{1,0},{2,3},{3,2},{4,5},{5,4},{6,7},{7,6},{8,9},{9,8},{10,11... | collective-permute-start | bytes 12582920 | tf_op jit(solution)/shard_map/ppermute | solution.py:311
  (52 other events, 464.6 us)

commit v2 on v1

--- a/solution.py
+++ b/solution.py
@@ -16,21 +16,25 @@
 adam_eps = 1e-08
 HIGH = lax.Precision.HIGHEST
 VMEM = pltpu.VMEM
-LIMIT = 56 * 2**20
+LIMIT = 24 * 2**20
+parts = 2
 
 
 def fetch_weights(scal, sources, weights, sems):
     z, core = scal[1], scal[2]
-    ring, depth = sources[0].shape[0], sources[0].shape[1]
+    ring, part_rows = sources[0].shape[0], sources[0].shape[1]
+    depth = part_rows * (len(sources) // 2)
     copies = []
-    for which, source in enumerate(sources):
+    for index, source in enumerate(sources):
+        part, which = divmod(index, 2)
         owner_core = core if which == 0 else 1 - core
         for j in range(ring):
             place = lax.rem(z + j, ring)
-            row = pl.multiple_of((place * 2 + owner_core) * depth, depth)
+            row = (place * 2 + owner_core) * depth + part * part_rows
+            row = pl.multiple_of(row, part_rows)
             copies.append(
                 pltpu.make_async_copy(
-                    source.at[j], weights.at[pl.ds(row, depth), :], sems.at[which, j]
+                    source.at[j], weights.at[pl.ds(row, part_rows), :], sems.at[index, j]
                 )
             )
     for copy in copies:
@@ -42,8 +46,8 @@
     sections, height, width, images, steps = dims
     slices = refs[:sections]
     refs = refs[sections:]
-    sources = refs[:2]
-    refs = refs[2:]
+    sources = refs[: 2 * parts]
+    refs = refs[2 * parts :]
     if last:
         readout, out, fired_out, logits_out, weights, padded, work, sems = refs
     else:
@@ -116,8 +120,8 @@
     fired = refs[0]
     refs = refs[1:]
     if stage < 2:
-        sources = refs[:2]
-        refs = refs[2:]
+        sources = refs[: 2 * parts]
+        refs = refs[2 * parts :]
         raw_out, own_out = refs[:2]
         sends = refs[2 : 1 + sections]
         weights, padded, upstream, work, sems = refs[1 + sections :]
@@ -201,8 +205,8 @@
 def run_forward(dims, last, scal, slices, sources, readout):
     sections, height, width, images, steps = dims
     rows, lanes = slices[0].shape
-    depth = sources[0].shape[1]
-    ring = sources[0].shape[0]
+    ring, part_rows = sources[0].shape[:2]
+    depth = parts * part_rows
     shapes = [
         jax.ShapeDtypeStruct((rows, lanes), jnp.bfloat16),
         jax.ShapeDtypeStruct((lanes // 128, rows, 128), jnp.float32),
@@ -218,14 +222,14 @@
         out_shape=shapes,
         in_specs=[pl.BlockSpec(memory_space=pltpu.SMEM)]
         + vmem(sections)
-        + [pl.BlockSpec(memory_space=pl.ANY)] * 2
+        + [pl.BlockSpec(memory_space=pl.ANY)] * len(sources)
         + extra,
         out_specs=vmem(len(shapes)),
         scratch_shapes=[
             VMEM((2 * ring * depth, lanes), jnp.bfloat16),
             VMEM((sections, height + 2, width + 2, images * steps, lanes), jnp.bfloat16),
             VMEM((lanes // 128, rows, 128), jnp.float32),
-            pltpu.SemaphoreType.DMA((2, ring)),
+            pltpu.SemaphoreType.DMA((2 * parts, ring)),
         ],
         compiler_params=pltpu.CompilerParams(vmem_limit_bytes=LIMIT),
         cost_estimate=pl.CostEstimate(
@@ -248,9 +252,10 @@
     work = [VMEM(fired.shape, jnp.float32), VMEM(fired.shape, jnp.float32)]
     cost = 0
     if stage < 2:
-        ring, depth = sources[0].shape[:2]
+        ring, part_rows = sources[0].shape[:2]
+        depth = parts * part_rows
         operands += list(sources)
-        specs += [pl.BlockSpec(memory_space=pl.ANY)] * 2
+        specs += [pl.BlockSpec(memory_space=pl.ANY)] * len(sources)
         shapes = [half, full] + [half] * (sections - 1)
         work = (
             [
@@ -258,7 +263,7 @@
                 VMEM((height + 2, width + 2, images * steps, lanes), jnp.bfloat16),
             ]
             + work
-            + [pltpu.SemaphoreType.DMA((2, ring))]
+            + [pltpu.SemaphoreType.DMA((2 * parts, ring))]
         )
         cost = 2 * ring * depth
     else:
@@ -279,43 +284,46 @@
     )(*operands)
 
 
-def after(value, earlier):
-    if earlier is None:
-        return value
-    return lax.optimization_barrier((value, earlier))[0]
-
-
-def ring_steps(piece, z, ring, gate):
-    def pairs(step, way):
-        if way > 0:
-            hops = [(i, i + 1) for i in range(step - 1, ring - 1)]
+def after(value, *earlier):
+    return lax.optimization_barrier((value, *earlier))[0]
+
+
+def hops(step, way, ring):
+    if way > 0:
+        pairs = [(i, i + 1) for i in range(step - 1, ring - 1)]
+    else:
+        pairs = [(i, i - 1) for i in range(1, ring - step + 1)]
+    return [(2 * a + core, 2 * b + core) for a, b in pairs for core in range(2)]
+
+
+def ring_gather(pieces, ring, gates=()):
+    low = [[] for _ in pieces]
+    high = [[] for _ in pieces]
+    for step in range(1, ring):
+        for h, piece in enumerate(pieces):
+            up = low[h][-1] if step > 1 else piece
+            down = high[h][-1] if step > 1 else piece
+            if step == 1 and gates:
+                up = down = after(piece, *gates[h])
+            low[h].append(lax.ppermute(up, "dp", hops(step, 1, ring)))
+            high[h].append(lax.ppermute(down, "dp", hops(step, -1, ring)))
+    return low, high
+
+
+def swap_core(value):
+    count = lax.axis_size("dp")
+    return lax.ppermute(value, "dp", [(i, i ^ 1) for i in range(count)])
+
+
+def by_step(piece, low, high, z, ring):
+    result = [[piece]]
+    for step in range(1, ring):
+        up, down = low[step - 1], high[step - 1]
+        if 2 * step < ring:
+            result.append([down, up])
         else:
-            hops = [(i, i - 1) for i in range(1, ring - step + 1)]
-        return [(2 * a + core, 2 * b + core) for a, b in hops for core in range(2)]
-
-    low, high = {}, {}
-    up, down = piece, piece
-    for step in range(1, ring):
-        up, down = gate(up), gate(down)
-        up = lax.ppermute(up, "dp", pairs(step, 1))
-        down = lax.ppermute(down, "dp", pairs(step, -1))
-        low[step], high[step] = up, down
-        yield up
-    result = [piece]
-    for j in range(1, ring):
-        result.append(jnp.where(z + j < ring, high[j], low[ring - j]))
-    yield result
-
-
-def swap_core(value, count):
-    return lax.ppermute(value, "dp", [(i, i ^ 1) for i in range(count)])
-
-
-def gather_ring(piece, z, ring):
-    for result in ring_steps(piece, z, ring, lambda value: value):
-        pass
-    own = jnp.stack(result)
-    return own, swap_core(own, 2 * ring)
+            result.append([jnp.where(z + step < ring, down, up)])
+    return result
 
 
 def adam_update(weights, first_moment, second_moment, grad_total):
@@ -353,42 +361,53 @@
     def pick(options, index):
         return lax.dynamic_index_in_dim(jnp.stack(options), index, 0, keepdims=False)
 
-    pieces = [columns(weights[0], k).astype(jnp.bfloat16) for k in range(sections)]
-    pieces = [pieces[0]] + exchange(pieces[1:])
+    part_rows = depth // parts
+    pieces = []
+    for h in range(parts):
+        own = [
+            columns(weights[0, h * part_rows : (h + 1) * part_rows], k).astype(jnp.bfloat16)
+            for k in range(sections)
+        ]
+        if h:
+            own = [own[0]] + [after(own[k], pieces[-1][k]) for k in range(1, sections)]
+        pieces.append([own[0]] + exchange(own[1:]))
     field = spikes.transpose(2, 3, 0, 1, 4).reshape(rows, channels)
     slices = [columns(field, k) for k in range(sections)]
     padded_classes = -(-classes // 128) * 128
     readout_own = lax.dynamic_slice_in_dim(readout, s * lanes, lanes, 0)
     readout_own = jnp.pad(readout_own, ((0, 0), (0, padded_classes - classes)))
 
-    history = []
-
-    def gate(value):
-        if len(history) >= 4:
-            value = after(value, history[-4])
-        return value
-
-    sources = [None] * sections
-    for first in range(0, sections, 2):
-        blocks = [b for b in (first, first + 1) if b < sections]
-        walks = {b: ring_steps(pick(pieces, s ^ b), z, ring, gate) for b in blocks}
-        for step in range(ring):
-            for b in blocks:
-                sources[b] = next(walks[b])
-                if step < ring - 1:
-                    history.extend([sources[b], sources[b]])
-        for b in blocks:
-            own = jnp.stack(sources[b])
-            sources[b] = (own, swap_core(own, devices))
-
-    inputs, fired_all = [], []
+    inputs, results, chains, sources = [slices], [], [], []
+
+    def gather_block(b):
+        gates = ()
+        if b > 0:
+            low, high = chains[b - 1]
+            near = max(ring - 3, 0)
+            gates = [(low[h][near], high[h][near]) for h in range(parts)]
+            if b > 1:
+                gates = [gate + (results[b - 2][0],) for gate in gates]
+        own = [pick(pieces[h], s ^ b) for h in range(parts)]
+        low, high = ring_gather(own, ring, gates)
+        chains.append((low, high))
+        flat = []
+        for h in range(parts):
+            held = [own[h]]
+            for j in range(1, ring):
+                held.append(jnp.where(z + j < ring, high[h][j - 1], low[h][ring - j - 1]))
+            held = jnp.stack(held)
+            flat += [held, swap_core(held)]
+        sources.append(flat)
+
+    gather_block(0)
     for b in range(sections):
-        inputs.append(slices)
+        if b + 1 < sections:
+            gather_block(b + 1)
         last = b == sections - 1
-        result = run_forward(dims, last, scal, slices, sources[b], readout_own)
-        fired_all.append(result[1])
+        result = run_forward(dims, last, scal, inputs[b], sources[b], readout_own)
+        results.append(result)
         if not last:
-            slices = [result[0]] + exchange([result[0]] * (sections - 1))
+            inputs.append([result[0]] + exchange([result[0]] * (sections - 1)))
     logits = result[2]
     heads = [logits] + exchange([logits] * (sections - 1))
     heads += [labels[:, None], readout_own]
@@ -397,43 +416,75 @@
         return jnp.concatenate([pick(parts, s ^ j) for j in range(sections)], axis=1)
 
     own_inputs = [pick([inputs[b][k] for b in range(sections)], s) for k in range(sections)]
-    x_all = gather_ring(ordered(own_inputs), z, ring)
+    own_x = ordered(own_inputs)
+    x_low, x_high = ring_gather([own_x], ring)
+    x_low, x_high = x_low[0], x_high[0]
 
     raws = [None] * sections
     for b in reversed(range(sections)):
         stage = 0 if b == sections - 1 else (2 if b == 0 else 1)
-        result = run_backward(dims, stage, classes, scal, heads, fired_all[b], sources[b])
+        step = sections - 1 - b
+        if 0 < step < ring:
+            heads[0] = after(heads[0], x_low[step - 1], x_high[step - 1])
+        result = run_backward(dims, stage, classes, scal, heads, results[b][1], sources[b])
         raws[b] = result[0]
         if b > 0:
             heads = [result[1]] + exchange(result[2:])
 
     sent = [pick(raws, s ^ k) for k in range(sections)]
     own_raw = ordered([sent[0]] + exchange(sent[1:]))
-    raw_all = gather_ring(own_raw, z, ring)
-
-    x_all = jnp.concatenate(x_all).reshape(devices, height, width, group, channels)
-    x_all = jnp.pad(x_all, ((0, 0), (1, 1), (1, 1), (0, 0), (0, 0)))
+    raw_parts = [own_raw[h * rows // parts : (h + 1) * rows // parts] for h in range(parts)]
+    raw_low, raw_high = ring_gather(raw_parts, ring)
+    raw_steps = [by_step(raw_parts[h], raw_low[h], raw_high[h], z, ring) for h in range(parts)]
+    x_steps = by_step(own_x, x_low, x_high, z, ring)
+
+    def both_cores(values):
+        return [array for value in values for array in (value, swap_core(value))]
+
+    def raw_of(step, *earlier):
+        count = len(raw_steps[0][step])
+        values = [raw_steps[h][step] for h in range(parts)]
+        if earlier:
+            values = [[after(value, *earlier) for value in part] for part in values]
+        swapped = [both_cores(part) for part in values]
+        return [swapped[h][i] for i in range(2 * count) for h in range(parts)]
+
     start = d * depth
     channel = start % channels
     step = 1
     while channels % (2 * step) == 0 and depth % (2 * step) == 0:
         step *= 2
     spans = -(-(channels - step + depth) // channels)
-    shifted = []
-    for i in range(spans):
-        offset = jnp.minimum(start // channels + i, 8)
-        shifted.append(
-            lax.dynamic_slice(
-                x_all,
-                (0, offset // 3, offset % 3, 0, 0),
-                (devices, height, width, group, channels),
-            ).reshape(devices * rows, channels)
-        )
-    cols = lax.dynamic_slice_in_dim(jnp.concatenate(shifted, axis=1), channel, depth, 1)
-    raw_all = jnp.concatenate(raw_all).reshape(devices * rows, channels)
-    grad = lax.dot_general(
-        cols, raw_all, (((0,), (0,)), ((), ())), preferred_element_type=jnp.float32
-    )
+
+    def cols_of(pieces):
+        count = len(pieces)
+        fields = jnp.stack(pieces).reshape(count, height, width, group, channels)
+        fields = jnp.pad(fields, ((0, 0), (1, 1), (1, 1), (0, 0), (0, 0)))
+        shifted = []
+        for i in range(spans):
+            offset = jnp.minimum(start // channels + i, 8)
+            shifted.append(
+                lax.dynamic_slice(
+                    fields,
+                    (0, offset // 3, offset % 3, 0, 0),
+                    (count, height, width, group, channels),
+                ).reshape(count * rows, channels)
+            )
+        return lax.dynamic_slice_in_dim(jnp.concatenate(shifted, axis=1), channel, depth, 1)
+
+    def product(x_pieces, raw_pieces):
+        return lax.dot_general(
+            cols_of(x_pieces),
+            jnp.concatenate(raw_pieces),
+            (((0,), (0,)), ((), ())),
+            preferred_element_type=jnp.float32,
+        )
+
+    early_x = both_cores([piece for pieces in x_steps[:-1] for piece in pieces])
+    early_raw = [piece for step in range(ring - 1) for piece in raw_of(step)]
+    late_x = both_cores(x_steps[-1])
+    early = product(early_x, early_raw)
+    grad = early + product(late_x, raw_of(ring - 1, early))
     return adam_update(weights, first_moment, second_moment, grad[None])
 
 

time: 540 us -> 534 us (0.989)
  the two profiles are of different devices: /device:TPU:0 before, /device:TPU:25 now
where the time goes in v2:
time: 534 us; the launch traced here: 525 us
  waiting for transfers between devices  215 us (40%)
  starting transfers between devices  175 us (33%)
  Pallas kernels  42.9 us (8%)
  local copies, waits for them, and re-layouts  41.8 us (8%)
  matrix products  28.9 us (5%)
  other arithmetic  17.9 us (3%)
    ppermute x33, waiting for transfers between devices, ring_gather(): low[h].append(lax.ppermute(up, 'dp', hops(step, 1, ring)))  135 us
    ppermute x30, waiting for transfers between devices, exchange(): lax.ppermute(values[k], 'section', [(i, i ^ k + 1) for i in range(section...  64.5 us
    ppermute x33, starting transfers between devices, ring_gather(): high[h].append(lax.ppermute(down, 'dp', hops(step, -1, ring)))  56.6 us
    ppermute x23, starting transfers between devices, swap_core(): return lax.ppermute(value, 'dp', [(i, i ^ 1) for i in range(count)])  45.7 us
    ppermute x33, starting transfers between devices, ring_gather(): low[h].append(lax.ppermute(up, 'dp', hops(step, 1, ring)))  43.2 us
    ppermute x30, starting transfers between devices, exchange(): lax.ppermute(values[k], 'section', [(i, i ^ k + 1) for i in range(section...  29.4 us
    dot_general x2, matrix products, product(): lax.dot_general(cols_of(x_pieces), jnp.concatenate(raw_pieces), (((0,), (...  28.9 us
    unnamed x124, local copies, waits for them, and re-layouts  24.3 us
  transfers between devices with their start and end apart: 119, of which 41 were waited for; matrix products, arithmetic and copies ran while one was open for 10% of the time, Pallas kernels for 8%

profile of v2, /device:TPU:25, one launch (start us, length us, event | category | flops | bytes accessed | tf_op | source)
XLA Modules:
  0.0 524.6 jit_solution(18000513959962341105)
XLA Ops:
  0.7 2.7 fusion.45
  7.2 5.3 %collective-permute-done.2 = bf16[576,256]{1,0:T(8,128)(2,1)S(1)} collective-permute-done((bf16[576,256]{1,0:T(8,128)(2,1)S(1)}, bf16[576,256]{1,0:T(8,128)(2,1)S(1)}, u32[]{:S(2)}, u32[]{:S(2)}) %collective-permute-start.2) | collective-permute-done | bytes 294944 | tf_op jit(solution)/shard_map/ppermute | solution.py:354
  14.7 6.1 %collective-permute-done.1 = bf16[576,256]{1,0:T(8,128)(2,1)S(1)} collective-permute-done((bf16[576,256]{1,0:T(8,128)(2,1)S(1)}, bf16[576,256]{1,0:T(8,128)(2,1)S(1)}, u32[]{:S(2)}, u32[]{:S(2)}) %collective-permute-start.1) | collective-permute-done | bytes 294944 | tf_op jit(solution)/shard_map/ppermute | solution.py:354
  22.2 2.9 collective-permute-done.12
  25.1 7.4 %collective-permute-done.11 = bf16[576,256]{1,0:T(8,128)(2,1)S(1)} collective-permute-done((bf16[576,256]{1,0:T(8,128)(2,1)S(1)}, bf16[576,256]{1,0:T(8,128)(2,1)S(1)}, u32[]{:S(2)}, u32[]{:S(2)}) %collective-permute-start.11) | collective-permute-done | bytes 294944 | tf_op jit(solution)/shard_map/ppermute | solution.py:354
  33.6 2.8 collective-permute-start.3
  37.7 4.0 collective-permute-start.13
  48.9 3.8 collective-permute-done.14
  56.0 3.1 collective-permute-done.5
  61.7 3.7 collective-permute-done.15
  72.5 3.6 collective-permute-done.6
  79.0 10.6 %collective-permute-done.16 = bf16[576,256]{1,0:T(8,128)(2,1)S(1)} collective-permute-done((bf16[576,256]{1,0:T(8,128)(2,1)}, bf16[576,256]{1,0:T(8,128)(2,1)S(1)}, u32[]{:S(2)}, u32[]{:S(2)}) %collective-permute-start.16) | collective-permute-done | bytes 294944 | tf_op jit(solution)/shard_map/ppermute | solution.py:308
  89.6 4.1 collective-permute-start.9
  98.0 6.9 %collective-permute-done.25 = bf16[576,256]{1,0:T(8,128)(2,1)S(1)} collective-permute-done((bf16[576,256]{1,0:T(8,128)(2,1)S(1)}, bf16[576,256]{1,0:T(8,128)(2,1)S(1)}, u32[]{:S(2)}, u32[]{:S(2)}) %collective-permute-start.25) | collective-permute-done | bytes 294944 | tf_op jit(solution)/shard_map/ppermute | solution.py:308
  107.0 4.3 collective-permute-done.32
  113.4 4.2 collective-permute-done.26
  119.1 4.9 collective-permute-done.33
  125.1 4.8 forward_block.4
  134.6 4.0 collective-permute-done.20.refs_1_
  138.6 2.3 collective-permute-start.22
  142.2 4.4 collective-permute-done.22.refs_3_
  153.8 4.3 collective-permute-done.48
  160.6 4.8 forward_block.5
  165.5 7.9 %collective-permute-start.65 = (bf16[576,256]{1,0:T(8,128)(2,1)}, bf16[576,256]{1,0:T(8,128)(2,1)S(1)}, u32[]{:S(2)}, u32[]{:S(2)}) collective-permute-start(bf16[576,256]{1,0:T(8,128)(2,1)} %bitcast.74), channel_id=1, source_target_pairs={{2,0},{3,1},{4,2},{5,3},{6,4},{7,5},{10,8},{11,9},{12,10},{13,11},... | collective-permute-start | bytes 884744 | tf_op jit(solution)/shard_map/ppermute | solution.py:309
  174.7 4.0 collective-permute-start.72
  181.6 6.2 %collective-permute-done.43 = bf16[576,256]{1,0:T(8,128)(2,1)S(1)} collective-permute-done((bf16[576,256]{1,0:T(8,128)(2,1)S(1)}, bf16[576,256]{1,0:T(8,128)(2,1)S(1)}, u32[]{:S(2)}, u32[]{:S(2)}) %collective-permute-start.43) | collective-permute-done | bytes 294944 | tf_op jit(solution)/shard_map/ppermute | solution.py:308
  190.6 10.1 %collective-permute-done.50 = bf16[576,256]{1,0:T(8,128)(2,1)S(1)} collective-permute-done((bf16[576,256]{1,0:T(8,128)(2,1)S(1)}, bf16[576,256]{1,0:T(8,128)(2,1)S(1)}, u32[]{:S(2)}, u32[]{:S(2)}) %collective-permute-start.50) | collective-permute-done | bytes 294944 | tf_op jit(solution)/shard_map/ppermute | solution.py:308
  200.7 4.9 collective-permute-start.46
  209.9 6.9 %collective-permute-done.67 = bf16[576,256]{1,0:T(8,128)(2,1)S(1)} collective-permute-done((bf16[576,256]{1,0:T(8,128)(2,1)S(1)}, bf16[576,256]{1,0:T(8,128)(2,1)S(1)}, u32[]{:S(2)}, u32[]{:S(2)}) %collective-permute-start.67) | collective-permute-done | bytes 294944 | tf_op jit(solution)/shard_map/ppermute | solution.py:308
  217.8 5.3 %collective-permute-done.74 = bf16[576,256]{1,0:T(8,128)(2,1)S(1)} collective-permute-done((bf16[576,256]{1,0:T(8,128)(2,1)S(1)}, bf16[576,256]{1,0:T(8,128)(2,1)S(1)}, u32[]{:S(2)}, u32[]{:S(2)}) %collective-permute-start.74) | collective-permute-done | bytes 294944 | tf_op jit(solution)/shard_map/ppermute | solution.py:308
  225.2 7.6 %collective-permute-done.68 = bf16[576,256]{1,0:T(8,128)(2,1)S(1)} collective-permute-done((bf16[576,256]{1,0:T(8,128)(2,1)S(1)}, bf16[576,256]{1,0:T(8,128)(2,1)S(1)}, u32[]{:S(2)}, u32[]{:S(2)}) %collective-permute-start.68) | collective-permute-done | bytes 294944 | tf_op jit(solution)/shard_map/ppermute | solution.py:308
  237.8 6.7 %collective-permute-done.38.refs_2_ = bf16[512,256]{1,0:T(8,128)(2,1)S(1)} collective-permute-done((bf16[512,256]{1,0:T(8,128)(2,1)S(1)}, bf16[512,256]{1,0:T(8,128)(2,1)S(1)}, u32[]{:S(2)}, u32[]{:S(2)}) %collective-permute-start.38) | collective-permute-done | bytes 262176 | tf_op jit(solution)/shard_map/ppermute | solution.py:354
  244.5 2.6 collective-permute-start.71
  247.1 4.8 forward_block.6
  255.0 6.9 %collective-permute-done.56.refs_3_ = bf16[512,256]{1,0:T(8,128)(2,1)S(1)} collective-permute-done((bf16[512,256]{1,0:T(8,128)(2,1)S(1)}, bf16[512,256]{1,0:T(8,128)(2,1)S(1)}, u32[]{:S(2)}, u32[]{:S(2)}) %collective-permute-start.56) | collective-permute-done | bytes 262176 | tf_op jit(solution)/shard_map/ppermute | solution.py:354
  262.1 3.5 collective-permute-done.55.refs_2_
  272.8 5.3 %collective-permute-start.58 = (bf16[512,1024]{1,0:T(8,128)(2,1)}, bf16[512,1024]{1,0:T(8,128)(2,1)}, u32[]{:S(2)}, u32[]{:S(2)}) collective-permute-start(bf16[512,1024]{1,0:T(8,128)(2,1)} %pad_maximum_fusion.11), channel_id=1, source_target_pairs={{2,0},{3,1},{4,2},{5,3},{6,4},{7,5},{10,8},{11,9},{12,10},{13,11},... | collective-permute-start | bytes 3145736 | tf_op jit(solution)/shard_map/ppermute | solution.py:309
  278.1 15.9 %collective-permute-done.60 = bf16[512,1024]{1,0:T(8,128)(2,1)} collective-permute-done((bf16[512,1024]{1,0:T(8,128)(2,1)}, bf16[512,1024]{1,0:T(8,128)(2,1)}, u32[]{:S(2)}, u32[]{:S(2)}) %collective-permute-start.60) | collective-permute-done | bytes 1048608 | tf_op jit(solution)/shard_map/ppermute | solution.py:308
  297.5 2.5 copy.12
  307.1 7.9 %forward_block.7 = (bf16[512,256]{1,0:T(8,128)(2,1)}, f32[2,512,128]{2,1,0:T(8,128)S(1)}, f32[4,1024]{1,0:T(4,128)}) custom-call(s32[3]{0:T(128)S(1)} %pad_add_fusion.scal, bf16[512,256]{1,0:T(8,128)(2,1)S(1)} %copy-done.7, bf16[512,256]{1,0:T(8,128)(2,1)S(1)} %copy-done.13, bf16[512,256]{1,0:T(8,128)(2,1)S(1)} %copy-done.9, ...), custom_call_target="tpu_custom_call" | custom-call | flops 2415919104 | bytes 4718592 | tf_op jit(solution)/shard_map/forward_block/pallas_call | solution.py:220
  318.9 2.9 collective-permute-start.57
  324.1 9.0 %backward_block.4 = (bf16[512,256]{1,0:T(8,128)(2,1)S(1)}, f32[512,256]{1,0:T(8,128)S(1)}, bf16[512,256]{1,0:T(8,128)(2,1)S(1)}, bf16[512,256]{1,0:T(8,128)(2,1)S(1)}, bf16[512,256]{1,0:T(8,128)(2,1)S(1)}) custom-call(s32[3]{0:T(128)S(1)} %pad_add_fusion.scal, f32[4,1024]{1,0:T(4,128)} %get-tuple-element.52.refs_0_, ...), custom_call_target="tpu_custom_call" | custom-call | flops 2429026304 | bytes 5767168 | tf_op jit(solution)/shard_map/backward_block/pallas_call | solution.py:271
  335.5 3.6 collective-permute-done.82.refs_1_
  341.7 4.1 collective-permute-done.84.refs_3_
  345.8 5.2 backward_block.5
  360.1 8.3 %collective-permute-start.59 = (bf16[512,1024]{1,0:T(8,128)(2,1)}, bf16[512,1024]{1,0:T(8,128)(2,1)S(1)}, u32[]{:S(2)}, u32[]{:S(2)}) collective-permute-start(bf16[512,1024]{1,0:T(8,128)(2,1)} %collective-permute-done.58), channel_id=1, source_target_pairs={{0,1},{1,0},{2,3},{3,2},{4,5},{5,4},{6,7},{7,6},{8,9},{9,8},{10,11... | collective-permute-start | bytes 3145736 | tf_op jit(solution)/shard_map/ppermute | solution.py:315
  371.1 5.4 %backward_block.6 = (bf16[512,256]{1,0:T(8,128)(2,1)S(1)}, f32[512,256]{1,0:T(8,128)S(1)}, bf16[512,256]{1,0:T(8,128)(2,1)S(1)}, bf16[512,256]{1,0:T(8,128)(2,1)S(1)}, bf16[512,256]{1,0:T(8,128)(2,1)S(1)}) custom-call(s32[3]{0:T(128)S(1)} %pad_add_fusion.scal, f32[512,256]{1,0:T(8,128)S(1)} %copy-done.33, bf16[512,256]{1,0:T(8,128)(2,1)} %collective-permute-done.85.refs_1_, ...), custom_call_target="tpu_custom_call" | custom-call | flops 2429026304 | bytes 5767168 | tf_op jit(solution)/shard_map/backward_block/pallas_call | solution.py:271
  380.6 4.1 collective-permute-start.61
  384.8 3.4 collective-permute-start.64
  395.8 6.3 %collective-permute-done.94 = bf16[512,256]{1,0:T(8,128)(2,1)S(1)} collective-permute-done((bf16[512,256]{1,0:T(8,128)(2,1)S(1)}, bf16[512,256]{1,0:T(8,128)(2,1)S(1)}, u32[]{:S(2)}, u32[]{:S(2)}) %collective-permute-start.94) | collective-permute-done | bytes 262176 | tf_op jit(solution)/shard_map/ppermute | solution.py:354
  402.6 2.4 collective-permute-start.96
  405.0 6.1 %collective-permute-start.98 = (bf16[256,1024]{1,0:T(8,128)(2,1)S(1)}, bf16[256,1024]{1,0:T(8,128)(2,1)S(1)}, u32[]{:S(2)}, u32[]{:S(2)}) collective-permute-start(bf16[256,1024]{1,0:T(8,128)(2,1)S(1)} %get-tuple-element.107), channel_id=1, source_target_pairs={{2,0},{3,1},{4,2},{5,3},{6,4},{7,5},{10,8},{11,9},{12,10},{13,11},... | collective-permute-start | bytes 1572872 | tf_op jit(solution)/shard_map/ppermute | solution.py:309
  411.2 2.7 collective-permute-start.99
  418.6 3.8 collective-permute-done.98
  423.7 9.9 %collective-permute-done.99 = bf16[256,1024]{1,0:T(8,128)(2,1)S(1)} collective-permute-done((bf16[256,1024]{1,0:T(8,128)(2,1)S(1)}, bf16[256,1024]{1,0:T(8,128)(2,1)S(1)}, u32[]{:S(2)}, u32[]{:S(2)}) %collective-permute-start.99) | collective-permute-done | bytes 524320 | tf_op jit(solution)/shard_map/ppermute | solution.py:309
  435.4 5.9 %collective-permute-done.103 = bf16[256,1024]{1,0:T(8,128)(2,1)S(1)} collective-permute-done((bf16[256,1024]{1,0:T(8,128)(2,1)S(1)}, bf16[256,1024]{1,0:T(8,128)(2,1)S(1)}, u32[]{:S(2)}, u32[]{:S(2)}) %collective-permute-start.103) | collective-permute-done | bytes 524320 | tf_op jit(solution)/shard_map/ppermute | solution.py:308
  445.9 9.9 %collective-permute-done.107 = bf16[256,1024]{1,0:T(8,128)(2,1)S(1)} collective-permute-done((bf16[256,1024]{1,0:T(8,128)(2,1)S(1)}, bf16[256,1024]{1,0:T(8,128)(2,1)S(1)}, u32[]{:S(2)}, u32[]{:S(2)}) %collective-permute-start.107) | collective-permute-done | bytes 524320 | tf_op jit(solution)/shard_map/ppermute | solution.py:308
  456.1 3.1 collective-permute-start.110
  459.1 7.9 %collective-permute-done.109 = bf16[256,1024]{1,0:T(8,128)(2,1)S(1)} collective-permute-done((bf16[256,1024]{1,0:T(8,128)(2,1)S(1)}, bf16[256,1024]{1,0:T(8,128)(2,1)S(1)}, u32[]{:S(2)}, u32[]{:S(2)}) %collective-permute-start.109) | collective-permute-done | bytes 524320 | tf_op jit(solution)/shard_map/ppermute | solution.py:308
  467.3 3.4 copy-done.47
  472.4 5.1 pad_dynamic-slice_fusion
  483.4 14.3 %fusion.1 = f32[1152,1024]{1,0:T(8,128)} fusion(bf16[4096,1024]{1,0:T(8,128)(2,1)} %constant_dynamic-update-slice_fusion.7, s32[]{:T(128)S(6)} %select_n.299, bf16[4096,1024]{1,0:T(8,128)(2,1)S(1)} %bitcast.168, bf16[4096,1024]{1,0:T(8,128)(2,1)S(1)} %bitcast.167), kind=kOutput, calls=%fused_computation.9 | convolution fusion | flops 9682550784 | bytes 29884420 | tf_op jit(solution)/shard_map/dot_general | solution.py:476
  498.0 6.7 %collective-permute-done.114 = bf16[256,1024]{1,0:T(8,128)(2,1)S(1)} collective-permute-done((bf16[256,1024]{1,0:T(8,128)(2,1)S(1)}, bf16[256,1024]{1,0:T(8,128)(2,1)S(1)}, u32[]{:S(2)}, u32[]{:S(2)}) %collective-permute-start.114) | collective-permute-done | bytes 524320 | tf_op jit(solution)/shard_map/ppermute | solution.py:308
  509.5 14.6 %divide_subtract_fusion = (f32[1,1152,1024]{2,1,0:T(8,128)}, f32[1,1152,1024]{2,1,0:T(8,128)}, f32[1,1152,1024]{2,1,0:T(8,128)}) fusion(f32[1,1152,1024]{2,1,0:T(8,128)S(1)} %bitcast.195, f32[1,1152,1024]{2,1,0:T(8,128)} %param.10, f32[1,1152,1024]{2,1,0:T(8,128)} %param.11, f32[1152,1024]{1,0:T(8,128)} %fusion.1, bf16[256,1024]{1,0:T(8,128)(2,1)} %copy-done.49, ...), kind=kOutput, calls=%fused_computation.22 | convolution fusion | flops 2443182080 | bytes 39321604 | tf_op jit(solution)/shard_map/dot_general | solution.py:476
  (378 shorter events, 159.3 us)
Async XLA Ops:
  5.8 15.0 %collective-permute-start.1 = (bf16[576,256]{1,0:T(8,128)(2,1)S(1)}, bf16[576,256]{1,0:T(8,128)(2,1)S(1)}, u32[]{:S(2)}, u32[]{:S(2)}) collective-permute-start(bf16[576,256]{1,0:T(8,128)(2,1)S(1)} %get-tuple-element.104), channel_id=1, source_target_pairs={{0,16},{8,24},{16,0},{24,8},{1,17},{9,25},{17,1},{25,9},{2,18},{10... | collective-permute-start | bytes 884744 | tf_op jit(solution)/shard_map/ppermute | solution.py:354
  6.1 16.0 %collective-permute-start = (bf16[576,256]{1,0:T(8,128)(2,1)S(1)}, bf16[576,256]{1,0:T(8,128)(2,1)S(1)}, u32[]{:S(2)}, u32[]{:S(2)}) collective-permute-start(bf16[576,256]{1,0:T(8,128)(2,1)S(1)} %get-tuple-element.105), channel_id=1, source_target_pairs={{0,8},{8,0},{16,24},{24,16},{1,9},{9,1},{17,25},{25,17},{2,10},{10... | collective-permute-start | bytes 884744 | tf_op jit(solution)/shard_map/ppermute | solution.py:354
  12.5 12.6 %collective-permute-start.12 = (bf16[576,256]{1,0:T(8,128)(2,1)}, bf16[576,256]{1,0:T(8,128)(2,1)S(1)}, u32[]{:S(2)}, u32[]{:S(2)}) collective-permute-start(bf16[576,256]{1,0:T(8,128)(2,1)} %get-tuple-element.42), channel_id=1, source_target_pairs={{0,24},{8,16},{16,8},{24,0},{1,25},{9,17},{17,9},{25,1},{2,26},{10... | collective-permute-start | bytes 884744 | tf_op jit(solution)/shard_map/ppermute | solution.py:354
  43.0 13.0 %collective-permute-start.7 = (bf16[576,256]{1,0:T(8,128)(2,1)}, bf16[576,256]{1,0:T(8,128)(2,1)}, u32[]{:S(2)}, u32[]{:S(2)}) collective-permute-start(bf16[576,256]{1,0:T(8,128)(2,1)} %collective-permute-done.3), channel_id=1, source_target_pairs={{2,0},{3,1},{4,2},{5,3},{10,8},{11,9},{12,10},{13,11},{18,16},{19,... | collective-permute-start | bytes 884744 | tf_op jit(solution)/shard_map/ppermute | solution.py:309
  46.1 13.0 %collective-permute-start.5 = (bf16[576,256]{1,0:T(8,128)(2,1)}, bf16[576,256]{1,0:T(8,128)(2,1)}, u32[]{:S(2)}, u32[]{:S(2)}) collective-permute-start(bf16[576,256]{1,0:T(8,128)(2,1)} %collective-permute-done.4), channel_id=1, source_target_pairs={{2,4},{3,5},{4,6},{5,7},{10,12},{11,13},{12,14},{13,15},{18,20},{1... | collective-permute-start | bytes 884744 | tf_op jit(solution)/shard_map/ppermute | solution.py:308
  47.5 14.2 %collective-permute-start.17 = (bf16[576,256]{1,0:T(8,128)(2,1)S(1)}, bf16[576,256]{1,0:T(8,128)(2,1)}, u32[]{:S(2)}, u32[]{:S(2)}) collective-permute-start(bf16[576,256]{1,0:T(8,128)(2,1)S(1)} %collective-permute-done.13), channel_id=1, source_target_pairs={{2,0},{3,1},{4,2},{5,3},{10,8},{11,9},{12,10},{13,11},{18,16},{19,... | collective-permute-start | bytes 884744 | tf_op jit(solution)/shard_map/ppermute | solution.py:309
  52.7 12.7 %collective-permute-start.15 = (bf16[576,256]{1,0:T(8,128)(2,1)S(1)}, bf16[576,256]{1,0:T(8,128)(2,1)}, u32[]{:S(2)}, u32[]{:S(2)}) collective-permute-start(bf16[576,256]{1,0:T(8,128)(2,1)S(1)} %collective-permute-done.14), channel_id=1, source_target_pairs={{2,4},{3,5},{4,6},{5,7},{10,12},{11,13},{12,14},{13,15},{18,20},{1... | collective-permute-start | bytes 884744 | tf_op jit(solution)/shard_map/ppermute | solution.py:308
  59.1 34.6 %collective-permute-start.23 = (bf16[576,256]{1,0:T(8,128)(2,1)S(1)}, bf16[576,256]{1,0:T(8,128)(2,1)S(1)}, u32[]{:S(2)}, u32[]{:S(2)}) collective-permute-start(bf16[576,256]{1,0:T(8,128)(2,1)S(1)} %bitcast.188), channel_id=1, source_target_pairs={{2,0},{3,1},{4,2},{5,3},{6,4},{7,5},{10,8},{11,9},{12,10},{13,11},... | collective-permute-start | bytes 884744 | tf_op jit(solution)/shard_map/ppermute | solution.py:309
  60.4 34.0 %collective-permute-start.24 = (bf16[576,256]{1,0:T(8,128)(2,1)S(1)}, bf16[576,256]{1,0:T(8,128)(2,1)S(1)}, u32[]{:S(2)}, u32[]{:S(2)}) collective-permute-start(bf16[576,256]{1,0:T(8,128)(2,1)S(1)} %bitcast.189), channel_id=1, source_target_pairs={{0,2},{1,3},{2,4},{3,5},{4,6},{5,7},{8,10},{9,11},{10,12},{11,13},... | collective-permute-start | bytes 884744 | tf_op jit(solution)/shard_map/ppermute | solution.py:308
  65.4 30.3 %collective-permute-start.30 = (bf16[576,256]{1,0:T(8,128)(2,1)S(1)}, bf16[576,256]{1,0:T(8,128)(2,1)S(1)}, u32[]{:S(2)}, u32[]{:S(2)}) collective-permute-start(bf16[576,256]{1,0:T(8,128)(2,1)S(1)} %bitcast.186), channel_id=1, source_target_pairs={{2,0},{3,1},{4,2},{5,3},{6,4},{7,5},{10,8},{11,9},{12,10},{13,11},... | collective-permute-start | bytes 884744 | tf_op jit(solution)/shard_map/ppermute | solution.py:309
  76.1 20.3 %collective-permute-start.31 = (bf16[576,256]{1,0:T(8,128)(2,1)S(1)}, bf16[576,256]{1,0:T(8,128)(2,1)S(1)}, u32[]{:S(2)}, u32[]{:S(2)}) collective-permute-start(bf16[576,256]{1,0:T(8,128)(2,1)S(1)} %bitcast.187), channel_id=1, source_target_pairs={{0,2},{1,3},{2,4},{3,5},{4,6},{5,7},{8,10},{9,11},{10,12},{11,13},... | collective-permute-start | bytes 884744 | tf_op jit(solution)/shard_map/ppermute | solution.py:308
  77.5 12.2 %collective-permute-start.16 = (bf16[576,256]{1,0:T(8,128)(2,1)}, bf16[576,256]{1,0:T(8,128)(2,1)S(1)}, u32[]{:S(2)}, u32[]{:S(2)}) collective-permute-start(bf16[576,256]{1,0:T(8,128)(2,1)} %collective-permute-done.15), channel_id=1, source_target_pairs={{4,6},{5,7},{12,14},{13,15},{20,22},{21,23},{28,30},{29,31}} | collective-permute-start | bytes 884744 | tf_op jit(solution)/shard_map/ppermute | solution.py:308
  89.6 35.4 %collective-permute-start.9 = (bf16[4,576,256]{2,1,0:T(8,128)(2,1)S(1)}, bf16[4,576,256]{2,1,0:T(8,128)(2,1)S(1)}, u32[]{:S(2)}, u32[]{:S(2)}) collective-permute-start(bf16[4,576,256]{2,1,0:T(8,128)(2,1)S(1)} %pad_maximum_fusion.1.refs_4_), channel_id=1, source_target_pairs={{0,1},{1,0},{2,3},{3,2},{4,5},{5,4},{6,7},{7,6},{8,9},{9,8},{10,11... | collective-permute-start | bytes 3538952 | tf_op jit(solution)/shard_map/ppermute | solution.py:315
  96.4 14.8 %collective-permute-start.32 = (bf16[576,256]{1,0:T(8,128)(2,1)S(1)}, bf16[576,256]{1,0:T(8,128)(2,1)S(1)}, u32[]{:S(2)}, u32[]{:S(2)}) collective-permute-start(bf16[576,256]{1,0:T(8,128)(2,1)S(1)} %collective-permute-done.31), channel_id=1, source_target_pairs={{2,4},{3,5},{4,6},{5,7},{10,12},{11,13},{12,14},{13,15},{18,20},{1... | collective-permute-start | bytes 884744 | tf_op jit(solution)/shard_map/ppermute | solution.py:308
  98.0 27.1 %collective-permute-start.19 = (bf16[4,576,256]{2,1,0:T(8,128)(2,1)S(1)}, bf16[4,576,256]{2,1,0:T(8,128)(2,1)S(1)}, u32[]{:S(2)}, u32[]{:S(2)}) collective-permute-start(bf16[4,576,256]{2,1,0:T(8,128)(2,1)S(1)} %pad_maximum_fusion.3.refs_6_), channel_id=1, source_target_pairs={{0,1},{1,0},{2,3},{3,2},{4,5},{5,4},{6,7},{7,6},{8,9},{9,8},{10,11... | collective-permute-start | bytes 3538952 | tf_op jit(solution)/shard_map/ppermute | solution.py:315
  117.8 41.0 %collective-permute-start.29 = (bf16[4,576,256]{2,1,0:T(8,128)(2,1)S(1)}, bf16[4,576,256]{2,1,0:T(8,128)(2,1)S(1)}, u32[]{:S(2)}, u32[]{:S(2)}) collective-permute-start(bf16[4,576,256]{2,1,0:T(8,128)(2,1)S(1)} %pad_maximum_fusion.4.refs_4_.refs_5_), channel_id=1, source_target_pairs={{0,1},{1,0},{2,3},{3,2},{4,5},{5,4},{6,7},{7,6},{8,9},{9,8},{10,11... | collective-permute-start | bytes 3538952 | tf_op jit(solution)/shard_map/ppermute | solution.py:315
  124.1 36.5 %collective-permute-start.36 = (bf16[4,576,256]{2,1,0:T(8,128)(2,1)S(1)}, bf16[4,576,256]{2,1,0:T(8,128)(2,1)S(1)}, u32[]{:S(2)}, u32[]{:S(2)}) collective-permute-start(bf16[4,576,256]{2,1,0:T(8,128)(2,1)S(1)} %pad_maximum_fusion.5.refs_6_.refs_7_), channel_id=1, source_target_pairs={{0,1},{1,0},{2,3},{3,2},{4,5},{5,4},{6,7},{7,6},{8,9},{9,8},{10,11... | collective-permute-start | bytes 3538952 | tf_op jit(solution)/shard_map/ppermute | solution.py:315
  131.8 16.0 %collective-permute-start.40 = (bf16[576,256]{1,0:T(8,128)(2,1)S(1)}, bf16[576,256]{1,0:T(8,128)(2,1)S(1)}, u32[]{:S(2)}, u32[]{:S(2)}) collective-permute-start(bf16[576,256]{1,0:T(8,128)(2,1)S(1)} %bitcast.184), channel_id=1, source_target_pairs={{2,0},{3,1},{4,2},{5,3},{6,4},{7,5},{10,8},{11,9},{12,10},{13,11},... | collective-permute-start | bytes 884744 | tf_op jit(solution)/shard_map/ppermute | solution.py:309
  150.2 15.3 %collective-permute-start.44 = (bf16[576,256]{1,0:T(8,128)(2,1)S(1)}, bf16[576,256]{1,0:T(8,128)(2,1)S(1)}, u32[]{:S(2)}, u32[]{:S(2)}) collective-permute-start(bf16[576,256]{1,0:T(8,128)(2,1)S(1)} %collective-permute-done.40), channel_id=1, source_target_pairs={{2,0},{3,1},{4,2},{5,3},{10,8},{11,9},{12,10},{13,11},{18,16},{19,... | collective-permute-start | bytes 884744 | tf_op jit(solution)/shard_map/ppermute | solution.py:309
  152.5 12.9 %collective-permute-start.42 = (bf16[576,256]{1,0:T(8,128)(2,1)S(1)}, bf16[576,256]{1,0:T(8,128)(2,1)S(1)}, u32[]{:S(2)}, u32[]{:S(2)}) collective-permute-start(bf16[576,256]{1,0:T(8,128)(2,1)S(1)} %collective-permute-done.41), channel_id=1, source_target_pairs={{2,4},{3,5},{4,6},{5,7},{10,12},{11,13},{12,14},{13,15},{18,20},{1... | collective-permute-start | bytes 884744 | tf_op jit(solution)/shard_map/ppermute | solution.py:308
  158.1 16.6 %collective-permute-start.51 = (bf16[576,256]{1,0:T(8,128)(2,1)S(1)}, bf16[576,256]{1,0:T(8,128)(2,1)S(1)}, u32[]{:S(2)}, u32[]{:S(2)}) collective-permute-start(bf16[576,256]{1,0:T(8,128)(2,1)S(1)} %collective-permute-done.47), channel_id=1, source_target_pairs={{2,0},{3,1},{4,2},{5,3},{10,8},{11,9},{12,10},{13,11},{18,16},{19,... | collective-permute-start | bytes 884744 | tf_op jit(solution)/shard_map/ppermute | solution.py:309
  158.8 15.9 %collective-permute-start.49 = (bf16[576,256]{1,0:T(8,128)(2,1)S(1)}, bf16[576,256]{1,0:T(8,128)(2,1)S(1)}, u32[]{:S(2)}, u32[]{:S(2)}) collective-permute-start(bf16[576,256]{1,0:T(8,128)(2,1)S(1)} %collective-permute-done.48), channel_id=1, source_target_pairs={{2,4},{3,5},{4,6},{5,7},{10,12},{11,13},{12,14},{13,15},{18,20},{1... | collective-permute-start | bytes 884744 | tf_op jit(solution)/shard_map/ppermute | solution.py:308
  165.5 40.1 %collective-permute-start.65 = (bf16[576,256]{1,0:T(8,128)(2,1)}, bf16[576,256]{1,0:T(8,128)(2,1)S(1)}, u32[]{:S(2)}, u32[]{:S(2)}) collective-permute-start(bf16[576,256]{1,0:T(8,128)(2,1)} %bitcast.74), channel_id=1, source_target_pairs={{2,0},{3,1},{4,2},{5,3},{6,4},{7,5},{10,8},{11,9},{12,10},{13,11},... | collective-permute-start | bytes 884744 | tf_op jit(solution)/shard_map/ppermute | solution.py:309
  173.4 32.8 %collective-permute-start.66 = (bf16[576,256]{1,0:T(8,128)(2,1)}, bf16[576,256]{1,0:T(8,128)(2,1)S(1)}, u32[]{:S(2)}, u32[]{:S(2)}) collective-permute-start(bf16[576,256]{1,0:T(8,128)(2,1)} %bitcast.74), channel_id=1, source_target_pairs={{0,2},{1,3},{2,4},{3,5},{4,6},{5,7},{8,10},{9,11},{10,12},{11,13},... | collective-permute-start | bytes 884744 | tf_op jit(solution)/shard_map/ppermute | solution.py:308
  174.7 32.8 %collective-permute-start.72 = (bf16[576,256]{1,0:T(8,128)(2,1)}, bf16[576,256]{1,0:T(8,128)(2,1)S(1)}, u32[]{:S(2)}, u32[]{:S(2)}) collective-permute-start(bf16[576,256]{1,0:T(8,128)(2,1)} %bitcast.78), channel_id=1, source_target_pairs={{2,0},{3,1},{4,2},{5,3},{6,4},{7,5},{10,8},{11,9},{12,10},{13,11},... | collective-permute-start | bytes 884744 | tf_op jit(solution)/shard_map/ppermute | solution.py:309
  187.7 20.5 %collective-permute-start.73 = (bf16[576,256]{1,0:T(8,128)(2,1)}, bf16[576,256]{1,0:T(8,128)(2,1)S(1)}, u32[]{:S(2)}, u32[]{:S(2)}) collective-permute-start(bf16[576,256]{1,0:T(8,128)(2,1)} %bitcast.78), channel_id=1, source_target_pairs={{0,2},{1,3},{2,4},{3,5},{4,6},{5,7},{8,10},{9,11},{10,12},{11,13},... | collective-permute-start | bytes 884744 | tf_op jit(solution)/shard_map/ppermute | solution.py:308
  200.7 46.4 %collective-permute-start.46 = (bf16[4,576,256]{2,1,0:T(8,128)(2,1)S(1)}, bf16[4,576,256]{2,1,0:T(8,128)(2,1)S(1)}, u32[]{:S(2)}, u32[]{:S(2)}) collective-permute-start(bf16[4,576,256]{2,1,0:T(8,128)(2,1)S(1)} %pad_maximum_fusion.6.refs_4_.refs_5_), channel_id=1, source_target_pairs={{0,1},{1,0},{2,3},{3,2},{4,5},{5,4},{6,7},{7,6},{8,9},{9,8},{10,11... | collective-permute-start | bytes 3538952 | tf_op jit(solution)/shard_map/ppermute | solution.py:315
  208.2 14.8 %collective-permute-start.74 = (bf16[576,256]{1,0:T(8,128)(2,1)S(1)}, bf16[576,256]{1,0:T(8,128)(2,1)S(1)}, u32[]{:S(2)}, u32[]{:S(2)}) collective-permute-start(bf16[576,256]{1,0:T(8,128)(2,1)S(1)} %collective-permute-done.73), channel_id=1, source_target_pairs={{2,4},{3,5},{4,6},{5,7},{10,12},{11,13},{12,14},{13,15},{18,20},{1... | collective-permute-start | bytes 884744 | tf_op jit(solution)/shard_map/ppermute | solution.py:308
  209.8 37.3 %collective-permute-start.53 = (bf16[4,576,256]{2,1,0:T(8,128)(2,1)S(1)}, bf16[4,576,256]{2,1,0:T(8,128)(2,1)S(1)}, u32[]{:S(2)}, u32[]{:S(2)}) collective-permute-start(bf16[4,576,256]{2,1,0:T(8,128)(2,1)S(1)} %pad_maximum_fusion.7.refs_6_.refs_7_), channel_id=1, source_target_pairs={{0,1},{1,0},{2,3},{3,2},{4,5},{5,4},{6,7},{7,6},{8,9},{9,8},{10,11... | collective-permute-start | bytes 3538952 | tf_op jit(solution)/shard_map/ppermute | solution.py:315
  217.5 16.8 %collective-permute-start.37 = (bf16[512,256]{1,0:T(8,128)(2,1)S(1)}, bf16[512,256]{1,0:T(8,128)(2,1)S(1)}, u32[]{:S(2)}, u32[]{:S(2)}) collective-permute-start(bf16[512,256]{1,0:T(8,128)(2,1)S(1)} %get-tuple-element.46.refs_0_), channel_id=1, source_target_pairs={{0,8},{8,0},{16,24},{24,16},{1,9},{9,1},{17,25},{25,17},{2,10},{10... | collective-permute-start | bytes 786440 | tf_op jit(solution)/shard_map/ppermute | solution.py:354
  234.1 13.0 %collective-permute-start.39 = (bf16[512,256]{1,0:T(8,128)(2,1)S(1)}, bf16[512,256]{1,0:T(8,128)(2,1)S(1)}, u32[]{:S(2)}, u32[]{:S(2)}) collective-permute-start(bf16[512,256]{1,0:T(8,128)(2,1)S(1)} %get-tuple-element.46.refs_0_), channel_id=1, source_target_pairs={{0,24},{8,16},{16,8},{24,0},{1,25},{9,17},{17,9},{25,1},{2,26},{10... | collective-permute-start | bytes 786440 | tf_op jit(solution)/shard_map/ppermute | solution.py:354
  234.3 19.1 %collective-permute-start.75 = (bf16[576,256]{1,0:T(8,128)(2,1)S(1)}, bf16[576,256]{1,0:T(8,128)(2,1)S(1)}, u32[]{:S(2)}, u32[]{:S(2)}) collective-permute-start(bf16[576,256]{1,0:T(8,128)(2,1)S(1)} %collective-permute-done.74), channel_id=1, source_target_pairs={{4,6},{5,7},{12,14},{13,15},{20,22},{21,23},{28,30},{29,31}} | collective-permute-start | bytes 884744 | tf_op jit(solution)/shard_map/ppermute | solution.py:308
  244.5 58.8 %collective-permute-start.71 = (bf16[4,576,256]{2,1,0:T(8,128)(2,1)}, bf16[4,576,256]{2,1,0:T(8,128)(2,1)}, u32[]{:S(2)}, u32[]{:S(2)}) collective-permute-start(bf16[4,576,256]{2,1,0:T(8,128)(2,1)} %pad_maximum_fusion.8.refs_4_.refs_7_), channel_id=1, source_target_pairs={{0,1},{1,0},{2,3},{3,2},{4,5},{5,4},{6,7},{7,6},{8,9},{9,8},{10,11... | collective-permute-start | bytes 3538952 | tf_op jit(solution)/shard_map/ppermute | solution.py:315
  252.0 13.6 %collective-permute-start.55 = (bf16[512,256]{1,0:T(8,128)(2,1)S(1)}, bf16[512,256]{1,0:T(8,128)(2,1)S(1)}, u32[]{:S(2)}, u32[]{:S(2)}) collective-permute-start(bf16[512,256]{1,0:T(8,128)(2,1)S(1)} %get-tuple-element.49.refs_0_), channel_id=1, source_target_pairs={{0,16},{8,24},{16,0},{24,8},{1,17},{9,25},{17,1},{25,9},{2,18},{10... | collective-permute-start | bytes 786440 | tf_op jit(solution)/shard_map/ppermute | solution.py:354
  253.5 13.0 %collective-permute-start.54 = (bf16[512,256]{1,0:T(8,128)(2,1)S(1)}, bf16[512,256]{1,0:T(8,128)(2,1)S(1)}, u32[]{:S(2)}, u32[]{:S(2)}) collective-permute-start(bf16[512,256]{1,0:T(8,128)(2,1)S(1)} %get-tuple-element.49.refs_0_), channel_id=1, source_target_pairs={{0,8},{8,0},{16,24},{24,16},{1,9},{9,1},{17,25},{25,17},{2,10},{10... | collective-permute-start | bytes 786440 | tf_op jit(solution)/shard_map/ppermute | solution.py:354
  268.2 25.7 %collective-permute-start.60 = (bf16[512,1024]{1,0:T(8,128)(2,1)}, bf16[512,1024]{1,0:T(8,128)(2,1)}, u32[]{:S(2)}, u32[]{:S(2)}) collective-permute-start(bf16[512,1024]{1,0:T(8,128)(2,1)} %pad_maximum_fusion.11), channel_id=1, source_target_pairs={{0,2},{1,3},{2,4},{3,5},{4,6},{5,7},{8,10},{9,11},{10,12},{11,13},... | collective-permute-start | bytes 3145736 | tf_op jit(solution)/shard_map/ppermute | solution.py:308
  271.7 31.6 %collective-permute-start.78 = (bf16[4,576,256]{2,1,0:T(8,128)(2,1)}, bf16[4,576,256]{2,1,0:T(8,128)(2,1)}, u32[]{:S(2)}, u32[]{:S(2)}) collective-permute-start(bf16[4,576,256]{2,1,0:T(8,128)(2,1)} %pad_maximum_fusion.9.refs_6_.refs_9_), channel_id=1, source_target_pairs={{0,1},{1,0},{2,3},{3,2},{4,5},{5,4},{6,7},{7,6},{8,9},{9,8},{10,11... | collective-permute-start | bytes 3538952 | tf_op jit(solution)/shard_map/ppermute | solution.py:315
  272.8 28.6 %collective-permute-start.58 = (bf16[512,1024]{1,0:T(8,128)(2,1)}, bf16[512,1024]{1,0:T(8,128)(2,1)}, u32[]{:S(2)}, u32[]{:S(2)}) collective-permute-start(bf16[512,1024]{1,0:T(8,128)(2,1)} %pad_maximum_fusion.11), channel_id=1, source_target_pairs={{2,0},{3,1},{4,2},{5,3},{6,4},{7,5},{10,8},{11,9},{12,10},{13,11},... | collective-permute-start | bytes 3145736 | tf_op jit(solution)/shard_map/ppermute | solution.py:309
  294.0 46.4 %collective-permute-start.63 = (bf16[512,1024]{1,0:T(8,128)(2,1)}, bf16[512,1024]{1,0:T(8,128)(2,1)}, u32[]{:S(2)}, u32[]{:S(2)}) collective-permute-start(bf16[512,1024]{1,0:T(8,128)(2,1)} %collective-permute-done.60), channel_id=1, source_target_pairs={{2,4},{3,5},{4,6},{5,7},{10,12},{11,13},{12,14},{13,15},{18,20},{1... | collective-permute-start | bytes 3145736 | tf_op jit(solution)/shard_map/ppermute | solution.py:308
  301.4 53.2 %collective-permute-start.62 = (bf16[512,1024]{1,0:T(8,128)(2,1)}, bf16[512,1024]{1,0:T(8,128)(2,1)}, u32[]{:S(2)}, u32[]{:S(2)}) collective-permute-start(bf16[512,1024]{1,0:T(8,128)(2,1)} %collective-permute-done.58), channel_id=1, source_target_pairs={{2,0},{3,1},{4,2},{5,3},{10,8},{11,9},{12,10},{13,11},{18,16},{19,... | collective-permute-start | bytes 3145736 | tf_op jit(solution)/shard_map/ppermute | solution.py:309
  318.9 40.5 %collective-permute-start.57 = (bf16[512,1024]{1,0:T(8,128)(2,1)}, bf16[512,1024]{1,0:T(8,128)(2,1)}, u32[]{:S(2)}, u32[]{:S(2)}) collective-permute-start(bf16[512,1024]{1,0:T(8,128)(2,1)} %pad_maximum_fusion.11), channel_id=1, source_target_pairs={{0,1},{1,0},{2,3},{3,2},{4,5},{5,4},{6,7},{7,6},{8,9},{9,8},{10,11... | collective-permute-start | bytes 3145736 | tf_op jit(solution)/shard_map/ppermute | solution.py:315
  340.4 37.0 %collective-permute-start.88 = (bf16[512,1024]{1,0:T(8,128)(2,1)}, bf16[512,1024]{1,0:T(8,128)(2,1)}, u32[]{:S(2)}, u32[]{:S(2)}) collective-permute-start(bf16[512,1024]{1,0:T(8,128)(2,1)} %collective-permute-done.63), channel_id=1, source_target_pairs={{4,6},{5,7},{12,14},{13,15},{20,22},{21,23},{28,30},{29,31}} | collective-permute-start | bytes 3145736 | tf_op jit(solution)/shard_map/ppermute | solution.py:308
  354.7 26.0 %collective-permute-start.89 = (bf16[512,1024]{1,0:T(8,128)(2,1)}, bf16[512,1024]{1,0:T(8,128)(2,1)}, u32[]{:S(2)}, u32[]{:S(2)}) collective-permute-start(bf16[512,1024]{1,0:T(8,128)(2,1)} %collective-permute-done.62), channel_id=1, source_target_pairs={{2,0},{3,1},{10,8},{11,9},{18,16},{19,17},{26,24},{27,25}} | collective-permute-start | bytes 3145736 | tf_op jit(solution)/shard_map/ppermute | solution.py:309
  358.1 12.9 %collective-permute-start.86 = (bf16[512,256]{1,0:T(8,128)(2,1)}, bf16[512,256]{1,0:T(8,128)(2,1)S(1)}, u32[]{:S(2)}, u32[]{:S(2)}) collective-permute-start(bf16[512,256]{1,0:T(8,128)(2,1)} %copy-done.27), channel_id=1, source_target_pairs={{0,16},{8,24},{16,0},{24,8},{1,17},{9,25},{17,1},{25,9},{2,18},{10... | collective-permute-start | bytes 786440 | tf_op jit(solution)/shard_map/ppermute | solution.py:354
  360.1 31.4 %collective-permute-start.59 = (bf16[512,1024]{1,0:T(8,128)(2,1)}, bf16[512,1024]{1,0:T(8,128)(2,1)S(1)}, u32[]{:S(2)}, u32[]{:S(2)}) collective-permute-start(bf16[512,1024]{1,0:T(8,128)(2,1)} %collective-permute-done.58), channel_id=1, source_target_pairs={{0,1},{1,0},{2,3},{3,2},{4,5},{5,4},{6,7},{7,6},{8,9},{9,8},{10,11... | collective-permute-start | bytes 3145736 | tf_op jit(solution)/shard_map/ppermute | solution.py:315
  380.6 30.4 %collective-permute-start.61 = (bf16[512,1024]{1,0:T(8,128)(2,1)}, bf16[512,1024]{1,0:T(8,128)(2,1)S(1)}, u32[]{:S(2)}, u32[]{:S(2)}) collective-permute-start(bf16[512,1024]{1,0:T(8,128)(2,1)} %collective-permute-done.60), channel_id=1, source_target_pairs={{0,1},{1,0},{2,3},{3,2},{4,5},{5,4},{6,7},{7,6},{8,9},{9,8},{10,11... | collective-permute-start | bytes 3145736 | tf_op jit(solution)/shard_map/ppermute | solution.py:315
  384.8 29.9 %collective-permute-start.64 = (bf16[512,1024]{1,0:T(8,128)(2,1)S(1)}, bf16[512,1024]{1,0:T(8,128)(2,1)S(1)}, u32[]{:S(2)}, u32[]{:S(2)}) collective-permute-start(bf16[512,1024]{1,0:T(8,128)(2,1)S(1)} %broadcast_select_fusion.1), channel_id=1, source_target_pairs={{0,1},{1,0},{2,3},{3,2},{4,5},{5,4},{6,7},{7,6},{8,9},{9,8},{10,11... | collective-permute-start | bytes 3145736 | tf_op jit(solution)/shard_map/ppermute | solution.py:315
  390.1 12.1 %collective-permute-start.94 = (bf16[512,256]{1,0:T(8,128)(2,1)S(1)}, bf16[512,256]{1,0:T(8,128)(2,1)S(1)}, u32[]{:S(2)}, u32[]{:S(2)}) collective-permute-start(bf16[512,256]{1,0:T(8,128)(2,1)S(1)} %get-tuple-element.116), channel_id=1, source_target_pairs={{0,16},{8,24},{16,0},{24,8},{1,17},{9,25},{17,1},{25,9},{2,18},{10... | collective-permute-start | bytes 786440 | tf_op jit(solution)/shard_map/ppermute | solution.py:354
  402.6 14.7 %collective-permute-start.96 = (bf16[256,1024]{1,0:T(8,128)(2,1)S(1)}, bf16[256,1024]{1,0:T(8,128)(2,1)S(1)}, u32[]{:S(2)}, u32[]{:S(2)}) collective-permute-start(bf16[256,1024]{1,0:T(8,128)(2,1)S(1)} %get-tuple-element.107), channel_id=1, source_target_pairs={{0,1},{1,0},{2,3},{3,2},{4,5},{5,4},{6,7},{7,6},{8,9},{9,8},{10,11... | collective-permute-start | bytes 1572872 | tf_op jit(solution)/shard_map/ppermute | solution.py:315
  405.0 17.4 %collective-permute-start.98 = (bf16[256,1024]{1,0:T(8,128)(2,1)S(1)}, bf16[256,1024]{1,0:T(8,128)(2,1)S(1)}, u32[]{:S(2)}, u32[]{:S(2)}) collective-permute-start(bf16[256,1024]{1,0:T(8,128)(2,1)S(1)} %get-tuple-element.107), channel_id=1, source_target_pairs={{2,0},{3,1},{4,2},{5,3},{6,4},{7,5},{10,8},{11,9},{12,10},{13,11},... | collective-permute-start | bytes 1572872 | tf_op jit(solution)/shard_map/ppermute | solution.py:309
  411.2 22.4 %collective-permute-start.99 = (bf16[256,1024]{1,0:T(8,128)(2,1)S(1)}, bf16[256,1024]{1,0:T(8,128)(2,1)S(1)}, u32[]{:S(2)}, u32[]{:S(2)}) collective-permute-start(bf16[256,1024]{1,0:T(8,128)(2,1)S(1)} %get-tuple-element.106), channel_id=1, source_target_pairs={{2,0},{3,1},{4,2},{5,3},{6,4},{7,5},{10,8},{11,9},{12,10},{13,11},... | collective-permute-start | bytes 1572872 | tf_op jit(solution)/shard_map/ppermute | solution.py:309
  414.0 20.4 %collective-permute-start.97 = (bf16[256,1024]{1,0:T(8,128)(2,1)S(1)}, bf16[256,1024]{1,0:T(8,128)(2,1)S(1)}, u32[]{:S(2)}, u32[]{:S(2)}) collective-permute-start(bf16[256,1024]{1,0:T(8,128)(2,1)S(1)} %get-tuple-element.106), channel_id=1, source_target_pairs={{0,1},{1,0},{2,3},{3,2},{4,5},{5,4},{6,7},{7,6},{8,9},{9,8},{10,11... | collective-permute-start | bytes 1572872 | tf_op jit(solution)/shard_map/ppermute | solution.py:315
  414.7 20.5 %collective-permute-start.102 = (bf16[256,1024]{1,0:T(8,128)(2,1)S(1)}, bf16[256,1024]{1,0:T(8,128)(2,1)S(1)}, u32[]{:S(2)}, u32[]{:S(2)}) collective-permute-start(bf16[256,1024]{1,0:T(8,128)(2,1)S(1)} %get-tuple-element.107), channel_id=1, source_target_pairs={{0,2},{1,3},{2,4},{3,5},{4,6},{5,7},{8,10},{9,11},{10,12},{11,13},... | collective-permute-start | bytes 1572872 | tf_op jit(solution)/shard_map/ppermute | solution.py:308
  417.3 24.0 %collective-permute-start.103 = (bf16[256,1024]{1,0:T(8,128)(2,1)S(1)}, bf16[256,1024]{1,0:T(8,128)(2,1)S(1)}, u32[]{:S(2)}, u32[]{:S(2)}) collective-permute-start(bf16[256,1024]{1,0:T(8,128)(2,1)S(1)} %get-tuple-element.106), channel_id=1, source_target_pairs={{0,2},{1,3},{2,4},{3,5},{4,6},{5,7},{8,10},{9,11},{10,12},{11,13},... | collective-permute-start | bytes 1572872 | tf_op jit(solution)/shard_map/ppermute | solution.py:308
  422.4 20.2 %collective-permute-start.100 = (bf16[256,1024]{1,0:T(8,128)(2,1)S(1)}, bf16[256,1024]{1,0:T(8,128)(2,1)S(1)}, u32[]{:S(2)}, u32[]{:S(2)}) collective-permute-start(bf16[256,1024]{1,0:T(8,128)(2,1)S(1)} %collective-permute-done.98), channel_id=1, source_target_pairs={{0,1},{1,0},{2,3},{3,2},{4,5},{5,4},{6,7},{7,6},{8,9},{9,8},{10,11... | collective-permute-start | bytes 1572872 | tf_op jit(solution)/shard_map/ppermute | solution.py:315
  441.3 14.5 %collective-permute-start.107 = (bf16[256,1024]{1,0:T(8,128)(2,1)S(1)}, bf16[256,1024]{1,0:T(8,128)(2,1)S(1)}, u32[]{:S(2)}, u32[]{:S(2)}) collective-permute-start(bf16[256,1024]{1,0:T(8,128)(2,1)S(1)} %collective-permute-done.102), channel_id=1, source_target_pairs={{2,4},{3,5},{4,6},{5,7},{10,12},{11,13},{12,14},{13,15},{18,20},{1... | collective-permute-start | bytes 1572872 | tf_op jit(solution)/shard_map/ppermute | solution.py:308
  443.5 15.6 %collective-permute-start.108 = (bf16[256,1024]{1,0:T(8,128)(2,1)S(1)}, bf16[256,1024]{1,0:T(8,128)(2,1)S(1)}, u32[]{:S(2)}, u32[]{:S(2)}) collective-permute-start(bf16[256,1024]{1,0:T(8,128)(2,1)S(1)} %collective-permute-done.99), channel_id=1, source_target_pairs={{2,0},{3,1},{4,2},{5,3},{10,8},{11,9},{12,10},{13,11},{18,16},{19,... | collective-permute-start | bytes 1572872 | tf_op jit(solution)/shard_map/ppermute | solution.py:309
  444.4 22.7 %collective-permute-start.109 = (bf16[256,1024]{1,0:T(8,128)(2,1)S(1)}, bf16[256,1024]{1,0:T(8,128)(2,1)S(1)}, u32[]{:S(2)}, u32[]{:S(2)}) collective-permute-start(bf16[256,1024]{1,0:T(8,128)(2,1)S(1)} %collective-permute-done.103), channel_id=1, source_target_pairs={{2,4},{3,5},{4,6},{5,7},{10,12},{11,13},{12,14},{13,15},{18,20},{1... | collective-permute-start | bytes 1572872 | tf_op jit(solution)/shard_map/ppermute | solution.py:308
  445.7 60.1 %collective-permute-start.112 = (bf16[512,1024]{1,0:T(8,128)(2,1)S(1)}, bf16[512,1024]{1,0:T(8,128)(2,1)S(1)}, u32[]{:S(2)}, u32[]{:S(2)}) collective-permute-start(bf16[512,1024]{1,0:T(8,128)(2,1)S(1)} %broadcast_select_fusion), channel_id=1, source_target_pairs={{0,1},{1,0},{2,3},{3,2},{4,5},{5,4},{6,7},{7,6},{8,9},{9,8},{10,11... | collective-permute-start | bytes 3145736 | tf_op jit(solution)/shard_map/ppermute | solution.py:315
  456.1 23.4 %collective-permute-start.110 = (bf16[256,1024]{1,0:T(8,128)(2,1)S(1)}, bf16[256,1024]{1,0:T(8,128)(2,1)S(1)}, u32[]{:S(2)}, u32[]{:S(2)}) collective-permute-start(bf16[256,1024]{1,0:T(8,128)(2,1)S(1)} %get-tuple-element.83), channel_id=1, source_target_pairs={{0,1},{1,0},{2,3},{3,2},{4,5},{5,4},{6,7},{7,6},{8,9},{9,8},{10,11... | collective-permute-start | bytes 1572872 | tf_op jit(solution)/shard_map/ppermute | solution.py:315
  477.5 20.3 %collective-permute-start.115 = (bf16[256,1024]{1,0:T(8,128)(2,1)S(1)}, bf16[256,1024]{1,0:T(8,128)(2,1)S(1)}, u32[]{:S(2)}, u32[]{:S(2)}) collective-permute-start(bf16[256,1024]{1,0:T(8,128)(2,1)S(1)} %collective-permute-done.108), channel_id=1, source_target_pairs={{2,0},{3,1},{10,8},{11,9},{18,16},{19,17},{26,24},{27,25}} | collective-permute-start | bytes 1572872 | tf_op jit(solution)/shard_map/ppermute | solution.py:309
  478.2 19.6 %collective-permute-start.116 = (bf16[256,1024]{1,0:T(8,128)(2,1)S(1)}, bf16[256,1024]{1,0:T(8,128)(2,1)S(1)}, u32[]{:S(2)}, u32[]{:S(2)}) collective-permute-start(bf16[256,1024]{1,0:T(8,128)(2,1)S(1)} %collective-permute-done.109), channel_id=1, source_target_pairs={{4,6},{5,7},{12,14},{13,15},{20,22},{21,23},{28,30},{29,31}} | collective-permute-start | bytes 1572872 | tf_op jit(solution)/shard_map/ppermute | solution.py:308
  479.5 18.5 %collective-permute-start.113 = (bf16[256,1024]{1,0:T(8,128)(2,1)S(1)}, bf16[256,1024]{1,0:T(8,128)(2,1)S(1)}, u32[]{:S(2)}, u32[]{:S(2)}) collective-permute-start(bf16[256,1024]{1,0:T(8,128)(2,1)S(1)} %collective-permute-done.106), channel_id=1, source_target_pairs={{2,0},{3,1},{10,8},{11,9},{18,16},{19,17},{26,24},{27,25}} | collective-permute-start | bytes 1572872 | tf_op jit(solution)/shard_map/ppermute | solution.py:309
  481.1 23.6 %collective-permute-start.114 = (bf16[256,1024]{1,0:T(8,128)(2,1)S(1)}, bf16[256,1024]{1,0:T(8,128)(2,1)S(1)}, u32[]{:S(2)}, u32[]{:S(2)}) collective-permute-start(bf16[256,1024]{1,0:T(8,128)(2,1)S(1)} %collective-permute-done.107), channel_id=1, source_target_pairs={{4,6},{5,7},{12,14},{13,15},{20,22},{21,23},{28,30},{29,31}} | collective-permute-start | bytes 1572872 | tf_op jit(solution)/shard_map/ppermute | solution.py:308
  (108 other events, 1250.5 us)

commit v3 on v2

--- a/solution.py
+++ b/solution.py
@@ -17,7 +17,7 @@
 HIGH = lax.Precision.HIGHEST
 VMEM = pltpu.VMEM
 LIMIT = 24 * 2**20
-parts = 2
+parts = 1
 
 
 def fetch_weights(scal, sources, weights, sems):
@@ -222,7 +222,7 @@
         out_shape=shapes,
         in_specs=[pl.BlockSpec(memory_space=pltpu.SMEM)]
         + vmem(sections)
-        + [pl.BlockSpec(memory_space=pl.ANY)] * len(sources)
+        + [pl.BlockSpec(memory_space=pltpu.HBM)] * len(sources)
         + extra,
         out_specs=vmem(len(shapes)),
         scratch_shapes=[
@@ -255,7 +255,7 @@
         ring, part_rows = sources[0].shape[:2]
         depth = parts * part_rows
         operands += list(sources)
-        specs += [pl.BlockSpec(memory_space=pl.ANY)] * len(sources)
+        specs += [pl.BlockSpec(memory_space=pltpu.HBM)] * len(sources)
         shapes = [half, full] + [half] * (sections - 1)
         work = (
             [
@@ -296,34 +296,9 @@
     return [(2 * a + core, 2 * b + core) for a, b in pairs for core in range(2)]
 
 
-def ring_gather(pieces, ring, gates=()):
-    low = [[] for _ in pieces]
-    high = [[] for _ in pieces]
-    for step in range(1, ring):
-        for h, piece in enumerate(pieces):
-            up = low[h][-1] if step > 1 else piece
-            down = high[h][-1] if step > 1 else piece
-            if step == 1 and gates:
-                up = down = after(piece, *gates[h])
-            low[h].append(lax.ppermute(up, "dp", hops(step, 1, ring)))
-            high[h].append(lax.ppermute(down, "dp", hops(step, -1, ring)))
-    return low, high
-
-
 def swap_core(value):
     count = lax.axis_size("dp")
     return lax.ppermute(value, "dp", [(i, i ^ 1) for i in range(count)])
-
-
-def by_step(piece, low, high, z, ring):
-    result = [[piece]]
-    for step in range(1, ring):
-        up, down = low[step - 1], high[step - 1]
-        if 2 * step < ring:
-            result.append([down, up])
-        else:
-            result.append([jnp.where(z + step < ring, down, up)])
-    return result
 
 
 def adam_update(weights, first_moment, second_moment, grad_total):
@@ -377,37 +352,51 @@
     readout_own = lax.dynamic_slice_in_dim(readout, s * lanes, lanes, 0)
     readout_own = jnp.pad(readout_own, ((0, 0), (0, padded_classes - classes)))
 
-    inputs, results, chains, sources = [slices], [], [], []
-
-    def gather_block(b):
-        gates = ()
-        if b > 0:
-            low, high = chains[b - 1]
-            near = max(ring - 3, 0)
-            gates = [(low[h][near], high[h][near]) for h in range(parts)]
-            if b > 1:
-                gates = [gate + (results[b - 2][0],) for gate in gates]
-        own = [pick(pieces[h], s ^ b) for h in range(parts)]
-        low, high = ring_gather(own, ring, gates)
-        chains.append((low, high))
-        flat = []
-        for h in range(parts):
-            held = [own[h]]
+    inputs, results, sources = [slices], [], []
+
+    def forward(b, *earlier):
+        last = b == sections - 1
+        slices = list(inputs[b])
+        if earlier:
+            slices[0] = after(slices[0], *earlier)
+        results.append(run_forward(dims, last, scal, slices, sources[b], readout_own))
+        if not last:
+            out = results[b][0]
+            inputs.append([out] + exchange([out] * (sections - 1)))
+
+    done = {}
+    for first in range(0, sections, 2):
+        blocks = [b for b in (first, first + 1) if b < sections]
+        for step in range(1, ring):
+            for b in blocks:
+                if first and step == 2 and b == blocks[-1]:
+                    forward(first - 2, *done[first, 1])
+                gates = []
+                if step == 1 and len(done) >= 2:
+                    gates += list(done.values())[-2]
+                if (b, step) == (0, 1):
+                    gates += [readout_own, *slices]
+                if first and step == 2 and b == blocks[-1]:
+                    gates += [results[first - 2][0]]
+                up, down = done[b, step - 1] if step > 1 else [pick(pieces[0], s ^ b)] * 2
+                if gates:
+                    up, down = after(up, *gates), after(down, *gates)
+                done[b, step] = (
+                    lax.ppermute(up, "dp", hops(step, 1, ring)),
+                    lax.ppermute(down, "dp", hops(step, -1, ring)),
+                )
+        for b in blocks:
+            held = [pick(pieces[0], s ^ b)]
             for j in range(1, ring):
-                held.append(jnp.where(z + j < ring, high[h][j - 1], low[h][ring - j - 1]))
+                held.append(jnp.where(z + j < ring, done[b, j][1], done[b, ring - j][0]))
             held = jnp.stack(held)
-            flat += [held, swap_core(held)]
-        sources.append(flat)
-
-    gather_block(0)
-    for b in range(sections):
-        if b + 1 < sections:
-            gather_block(b + 1)
-        last = b == sections - 1
-        result = run_forward(dims, last, scal, inputs[b], sources[b], readout_own)
-        results.append(result)
-        if not last:
-            inputs.append([result[0]] + exchange([result[0]] * (sections - 1)))
+            sources.append([held, swap_core(held)])
+        if first and len(results) == first - 1:
+            forward(first - 1, *done[blocks[-1], max(1, ring - 2)])
+    while len(results) < sections:
+        b = len(results)
+        forward(b, *(done[sections - 1, ring - 1] if b < sections - 1 else ()))
+    result = results[-1]
     logits = result[2]
     heads = [logits] + exchange([logits] * (sections - 1))
     heads += [labels[:, None], readout_own]
@@ -415,17 +404,15 @@
     def ordered(parts):
         return jnp.concatenate([pick(parts, s ^ j) for j in range(sections)], axis=1)
 
-    own_inputs = [pick([inputs[b][k] for b in range(sections)], s) for k in range(sections)]
+    own_inputs = [
+        pick([after(inputs[b][k], logits) for b in range(sections)], s) for k in range(sections)
+    ]
     own_x = ordered(own_inputs)
-    x_low, x_high = ring_gather([own_x], ring)
-    x_low, x_high = x_low[0], x_high[0]
+    x_all = lax.all_gather(own_x, "dp")
 
     raws = [None] * sections
     for b in reversed(range(sections)):
         stage = 0 if b == sections - 1 else (2 if b == 0 else 1)
-        step = sections - 1 - b
-        if 0 < step < ring:
-            heads[0] = after(heads[0], x_low[step - 1], x_high[step - 1])
         result = run_backward(dims, stage, classes, scal, heads, results[b][1], sources[b])
         raws[b] = result[0]
         if b > 0:
@@ -433,22 +420,6 @@
 
     sent = [pick(raws, s ^ k) for k in range(sections)]
     own_raw = ordered([sent[0]] + exchange(sent[1:]))
-    raw_parts = [own_raw[h * rows // parts : (h + 1) * rows // parts] for h in range(parts)]
-    raw_low, raw_high = ring_gather(raw_parts, ring)
-    raw_steps = [by_step(raw_parts[h], raw_low[h], raw_high[h], z, ring) for h in range(parts)]
-    x_steps = by_step(own_x, x_low, x_high, z, ring)
-
-    def both_cores(values):
-        return [array for value in values for array in (value, swap_core(value))]
-
-    def raw_of(step, *earlier):
-        count = len(raw_steps[0][step])
-        values = [raw_steps[h][step] for h in range(parts)]
-        if earlier:
-            values = [[after(value, *earlier) for value in part] for part in values]
-        swapped = [both_cores(part) for part in values]
-        return [swapped[h][i] for i in range(2 * count) for h in range(parts)]
-
     start = d * depth
     channel = start % channels
     step = 1
@@ -456,7 +427,14 @@
         step *= 2
     spans = -(-(channels - step + depth) // channels)
 
-    def cols_of(pieces):
+    def cols_of(distances):
+        pieces = [
+            lax.dynamic_index_in_dim(
+                x_all, lax.rem(z + j, ring) * 2 + place, 0, keepdims=False
+            )
+            for j in distances
+            for place in (core, 1 - core)
+        ]
         count = len(pieces)
         fields = jnp.stack(pieces).reshape(count, height, width, group, channels)
         fields = jnp.pad(fields, ((0, 0), (1, 1), (1, 1), (0, 0), (0, 0)))
@@ -472,19 +450,41 @@
             )
         return lax.dynamic_slice_in_dim(jnp.concatenate(shifted, axis=1), channel, depth, 1)
 
-    def product(x_pieces, raw_pieces):
+    def product(cols, raw_pieces):
         return lax.dot_general(
-            cols_of(x_pieces),
+            cols,
             jnp.concatenate(raw_pieces),
             (((0,), (0,)), ((), ())),
             preferred_element_type=jnp.float32,
         )
 
-    early_x = both_cores([piece for pieces in x_steps[:-1] for piece in pieces])
-    early_raw = [piece for step in range(ring - 1) for piece in raw_of(step)]
-    late_x = both_cores(x_steps[-1])
-    early = product(early_x, early_raw)
-    grad = early + product(late_x, raw_of(ring - 1, early))
+    arrivals = [[0]]
+    for step in range(1, ring):
+        arrivals.append([step, ring - step] if 2 * step < ring else [None])
+
+    def origins(step):
+        if arrivals[step] == [None]:
+            return [jnp.where(z + step < ring, step, ring - step)]
+        return arrivals[step]
+
+    early_cols = cols_of([j for step in range(ring - 1) for j in origins(step)])
+    late_cols = cols_of(origins(ring - 1))
+    up = down = own_raw
+    early_raw = [own_raw, swap_core(own_raw)]
+    for step in range(1, ring):
+        if step == 2:
+            up, down = after(up, early_cols, late_cols), after(down, early_cols, late_cols)
+        up = lax.ppermute(up, "dp", hops(step, 1, ring))
+        down = lax.ppermute(down, "dp", hops(step, -1, ring))
+        if 2 * step < ring:
+            landed = [down, up]
+        else:
+            landed = [jnp.where(z + step < ring, down, up)]
+        if step < ring - 1:
+            early_raw += [array for value in landed for array in (value, swap_core(value))]
+    early = product(early_cols, early_raw)
+    late = [array for value in landed for array in (value, swap_core(after(value, early)))]
+    grad = early + product(late_cols, late)
     return adam_update(weights, first_moment, second_moment, grad[None])
 
 

time: 534 us -> 487 us (0.912)
  the two profiles are of different devices: /device:TPU:25 before, /device:TPU:0 now
where the time goes in v3:
time: 487 us; the launch traced here: 478 us
  waiting for transfers between devices  255 us (52%)
  starting transfers between devices  85.6 us (18%)
  local copies, waits for them, and re-layouts  38.3 us (8%)
  Pallas kernels  38.2 us (8%)
  matrix products  24.9 us (5%)
  other arithmetic  20.3 us (4%)
  between operations  15.8 us (3%)
    ppermute x12, waiting for transfers between devices, shards(): lax.ppermute(down, 'dp', hops(step, -1, ring))  115 us
    ppermute x27, waiting for transfers between devices, exchange(): lax.ppermute(values[k], 'section', [(i, i ^ k + 1) for i in range(section...  92.4 us
    ppermute x3, waiting for transfers between devices, shards(): down = lax.ppermute(down, 'dp', hops(step, -1, ring))  43.2 us
    ppermute x27, starting transfers between devices, exchange(): lax.ppermute(values[k], 'section', [(i, i ^ k + 1) for i in range(section...  32.8 us
    ppermute x12, starting transfers between devices, shards(): lax.ppermute(up, 'dp', hops(step, 1, ring))  26.4 us
    dot_general x2, matrix products, product(): lax.dot_general(cols, jnp.concatenate(raw_pieces), (((0,), (0,)), ((), ()...  24.9 us
    unnamed x77, local copies, waits for them, and re-layouts  20.7 us
    pallas_call x4, Pallas kernels, run_forward(): pl.pallas_call(functools.partial(forward_kernel, dims, last), out_shape=s...  20 us
  transfers between devices with their start and end apart: 67, of which 40 were waited for; matrix products, arithmetic and copies ran while one was open for 12% of the time, Pallas kernels for 7%

profile of v3, /device:TPU:0, one launch (start us, length us, event | category | flops | bytes accessed | tf_op | source)
XLA Modules:
  0.0 478.3 jit_solution(423712338948384021)
XLA Ops:
  7.2 3.8 dynamic-slice_convert_fusion.3
  11.1 3.0 collective-permute-start.1
  17.2 1.8 copy.9
  20.2 7.5 %collective-permute-done.1 = bf16[1152,256]{1,0:T(8,128)(2,1)} collective-permute-done((bf16[1152,256]{1,0:T(8,128)(2,1)}, bf16[1152,256]{1,0:T(8,128)(2,1)}, u32[]{:S(2)}, u32[]{:S(2)}) %collective-permute-start.1) | collective-permute-done | bytes 589856 | tf_op jit(solution)/shard_map/ppermute | solution.py:329
  27.7 2.9 collective-permute-done
  30.6 10.9 %collective-permute-done.2 = bf16[1152,256]{1,0:T(8,128)(2,1)} collective-permute-done((bf16[1152,256]{1,0:T(8,128)(2,1)}, bf16[1152,256]{1,0:T(8,128)(2,1)}, u32[]{:S(2)}, u32[]{:S(2)}) %collective-permute-start.2) | collective-permute-done | bytes 589856 | tf_op jit(solution)/shard_map/ppermute | solution.py:329
  41.5 1.9 pad_maximum_fusion
  45.7 5.4 %collective-permute-start.3 = (bf16[1152,256]{1,0:T(8,128)(2,1)S(1)}, bf16[1152,256]{1,0:T(8,128)(2,1)}, u32[]{:S(2)}, u32[]{:S(2)}) collective-permute-start(bf16[1152,256]{1,0:T(8,128)(2,1)S(1)} %bitcast.146), channel_id=1, source_target_pairs={{0,2},{1,3},{2,4},{3,5},{4,6},{5,7},{8,10},{9,11},{10,12},{11,13},... | collective-permute-start | bytes 1769480 | tf_op jit(solution)/shard_map/ppermute | solution.py:385
  52.4 4.6 collective-permute-start.12
  57.0 5.7 %collective-permute-done.6 = bf16[1152,256]{1,0:T(8,128)(2,1)} collective-permute-done((bf16[1152,256]{1,0:T(8,128)(2,1)S(1)}, bf16[1152,256]{1,0:T(8,128)(2,1)}, u32[]{:S(2)}, u32[]{:S(2)}) %collective-permute-start.6) | collective-permute-done | bytes 589856 | tf_op jit(solution)/shard_map/ppermute | solution.py:386
  65.5 9.7 %collective-permute-done.15 = bf16[1152,256]{1,0:T(8,128)(2,1)S(1)} collective-permute-done((bf16[1152,256]{1,0:T(8,128)(2,1)S(1)}, bf16[1152,256]{1,0:T(8,128)(2,1)S(1)}, u32[]{:S(2)}, u32[]{:S(2)}) %collective-permute-start.15) | collective-permute-done | bytes 589856 | tf_op jit(solution)/shard_map/ppermute | solution.py:386
  78.0 10.0 %collective-permute-done.7 = bf16[1152,256]{1,0:T(8,128)(2,1)} collective-permute-done((bf16[1152,256]{1,0:T(8,128)(2,1)}, bf16[1152,256]{1,0:T(8,128)(2,1)}, u32[]{:S(2)}, u32[]{:S(2)}) %collective-permute-start.7) | collective-permute-done | bytes 589856 | tf_op jit(solution)/shard_map/ppermute | solution.py:386
  90.0 10.6 %collective-permute-done.16 = bf16[1152,256]{1,0:T(8,128)(2,1)} collective-permute-done((bf16[1152,256]{1,0:T(8,128)(2,1)S(1)}, bf16[1152,256]{1,0:T(8,128)(2,1)}, u32[]{:S(2)}, u32[]{:S(2)}) %collective-permute-start.16) | collective-permute-done | bytes 589856 | tf_op jit(solution)/shard_map/ppermute | solution.py:386
  103.7 9.4 %collective-permute-done.8 = bf16[1152,256]{1,0:T(8,128)(2,1)S(1)} collective-permute-done((bf16[1152,256]{1,0:T(8,128)(2,1)}, bf16[1152,256]{1,0:T(8,128)(2,1)S(1)}, u32[]{:S(2)}, u32[]{:S(2)}) %collective-permute-start.8) | collective-permute-done | bytes 589856 | tf_op jit(solution)/shard_map/ppermute | solution.py:386
  114.4 4.6 collective-permute-start.9
  121.8 4.0 collective-permute-done.17
  127.2 4.6 collective-permute-start.18
  131.9 6.5 %collective-permute-done.10 = bf16[1152,256]{1,0:T(8,128)(2,1)S(1)} collective-permute-done((bf16[1152,256]{1,0:T(8,128)(2,1)S(1)}, bf16[1152,256]{1,0:T(8,128)(2,1)S(1)}, u32[]{:S(2)}, u32[]{:S(2)}) %collective-permute-start.10) | collective-permute-done | bytes 589856 | tf_op jit(solution)/shard_map/ppermute | solution.py:386
  140.8 20.8 %collective-permute-done.33 = bf16[1152,256]{1,0:T(8,128)(2,1)S(1)} collective-permute-done((bf16[1152,256]{1,0:T(8,128)(2,1)S(1)}, bf16[1152,256]{1,0:T(8,128)(2,1)S(1)}, u32[]{:S(2)}, u32[]{:S(2)}) %collective-permute-start.33) | collective-permute-done | bytes 589856 | tf_op jit(solution)/shard_map/ppermute | solution.py:386
  163.9 4.7 forward_block.4
  169.2 10.0 %collective-permute-done.34 = bf16[1152,256]{1,0:T(8,128)(2,1)S(1)} collective-permute-done((bf16[1152,256]{1,0:T(8,128)(2,1)S(1)}, bf16[1152,256]{1,0:T(8,128)(2,1)S(1)}, u32[]{:S(2)}, u32[]{:S(2)}) %collective-permute-start.34) | collective-permute-done | bytes 589856 | tf_op jit(solution)/shard_map/ppermute | solution.py:386
  181.8 14.3 %collective-permute-done.21 = bf16[1152,256]{1,0:T(8,128)(2,1)S(1)} collective-permute-done((bf16[1152,256]{1,0:T(8,128)(2,1)S(1)}, bf16[1152,256]{1,0:T(8,128)(2,1)S(1)}, u32[]{:S(2)}, u32[]{:S(2)}) %collective-permute-start.21) | collective-permute-done | bytes 589856 | tf_op jit(solution)/shard_map/ppermute | solution.py:386
  197.8 14.3 %collective-permute-done.27 = bf16[1152,256]{1,0:T(8,128)(2,1)S(1)} collective-permute-done((bf16[1152,256]{1,0:T(8,128)(2,1)S(1)}, bf16[1152,256]{1,0:T(8,128)(2,1)S(1)}, u32[]{:S(2)}, u32[]{:S(2)}) %collective-permute-start.27) | collective-permute-done | bytes 589856 | tf_op jit(solution)/shard_map/ppermute | solution.py:386
  213.6 2.4 collective-permute-start.24
  217.2 6.6 %collective-permute-done.24.refs_3_ = bf16[512,256]{1,0:T(8,128)(2,1)S(1)} collective-permute-done((bf16[512,256]{1,0:T(8,128)(2,1)S(1)}, bf16[512,256]{1,0:T(8,128)(2,1)S(1)}, u32[]{:S(2)}, u32[]{:S(2)}) %collective-permute-start.24) | collective-permute-done | bytes 262176 | tf_op jit(solution)/shard_map/ppermute | solution.py:329
  223.7 5.1 %collective-permute-done.23.refs_2_ = bf16[512,256]{1,0:T(8,128)(2,1)S(1)} collective-permute-done((bf16[512,256]{1,0:T(8,128)(2,1)S(1)}, bf16[512,256]{1,0:T(8,128)(2,1)S(1)}, u32[]{:S(2)}, u32[]{:S(2)}) %collective-permute-start.23) | collective-permute-done | bytes 262176 | tf_op jit(solution)/shard_map/ppermute | solution.py:329
  228.9 4.7 forward_block.5
  233.5 1.8 collective-permute-start.30
  237.1 6.6 %collective-permute-done.30.refs_3_ = bf16[512,256]{1,0:T(8,128)(2,1)S(1)} collective-permute-done((bf16[512,256]{1,0:T(8,128)(2,1)S(1)}, bf16[512,256]{1,0:T(8,128)(2,1)S(1)}, u32[]{:S(2)}, u32[]{:S(2)}) %collective-permute-start.30) | collective-permute-done | bytes 262176 | tf_op jit(solution)/shard_map/ppermute | solution.py:329
  243.7 4.6 collective-permute-done.29.refs_2_
  248.4 4.7 forward_block.6
  257.4 6.6 %collective-permute-done.38.refs_3_ = bf16[512,256]{1,0:T(8,128)(2,1)S(1)} collective-permute-done((bf16[512,256]{1,0:T(8,128)(2,1)S(1)}, bf16[512,256]{1,0:T(8,128)(2,1)S(1)}, u32[]{:S(2)}, u32[]{:S(2)}) %collective-permute-start.38) | collective-permute-done | bytes 262176 | tf_op jit(solution)/shard_map/ppermute | solution.py:329
  264.0 4.6 collective-permute-done.37.refs_2_
  268.7 6.1 %forward_block.7 = (bf16[512,256]{1,0:T(8,128)(2,1)}, f32[2,512,128]{2,1,0:T(8,128)S(1)}, f32[4,1024]{1,0:T(4,128)S(1)}) custom-call(s32[3]{0:T(128)S(1)} %pad_add_fusion.scal, bf16[512,256]{1,0:T(8,128)(2,1)S(1)} %get-tuple-element.68.refs_0_, bf16[512,256]{1,0:T(8,128)(2,1)S(1)} %collective-permute-done.36.refs_1_, ...), custom_call_target="tpu_custom_call" | custom-call | flops 2415919104 | bytes 4718592 | tf_op jit(solution)/shard_map/forward_block/pallas_call | solution.py:220
  283.7 1.9 copy-done.3
  285.5 1.7 copy-done.15
  288.3 7.5 %backward_block.4 = (bf16[512,256]{1,0:T(8,128)(2,1)S(1)}, f32[512,256]{1,0:T(8,128)S(1)}, bf16[512,256]{1,0:T(8,128)(2,1)S(1)}, bf16[512,256]{1,0:T(8,128)(2,1)S(1)}, bf16[512,256]{1,0:T(8,128)(2,1)S(1)}) custom-call(s32[3]{0:T(128)S(1)} %pad_add_fusion.scal, f32[4,1024]{1,0:T(4,128)S(1)} %get-tuple-element.64.refs_0_, ...), custom_call_target="tpu_custom_call" | custom-call | flops 2429026304 | bytes 5767168 | tf_op jit(solution)/shard_map/backward_block/pallas_call | solution.py:271
  299.3 5.8 %collective-permute-done.43.refs_1_ = bf16[512,256]{1,0:T(8,128)(2,1)S(1)} collective-permute-done((bf16[512,256]{1,0:T(8,128)(2,1)S(1)}, bf16[512,256]{1,0:T(8,128)(2,1)S(1)}, u32[]{:S(2)}, u32[]{:S(2)}) %collective-permute-start.43) | collective-permute-done | bytes 262176 | tf_op jit(solution)/shard_map/ppermute | solution.py:329
  305.1 4.0 collective-permute-done.44.refs_2_
  309.1 4.8 %backward_block.5 = (bf16[512,256]{1,0:T(8,128)(2,1)S(1)}, f32[512,256]{1,0:T(8,128)S(1)}, bf16[512,256]{1,0:T(8,128)(2,1)S(1)}, bf16[512,256]{1,0:T(8,128)(2,1)S(1)}, bf16[512,256]{1,0:T(8,128)(2,1)S(1)}) custom-call(s32[3]{0:T(128)S(1)} %pad_add_fusion.scal, f32[512,256]{1,0:T(8,128)S(1)} %get-tuple-element.82.refs_0_, ...), custom_call_target="tpu_custom_call" | custom-call | flops 2429026304 | bytes 5767168 | tf_op jit(solution)/shard_map/backward_block/pallas_call | solution.py:271
  315.8 1.6 collective-permute-start.48
  317.4 5.1 %collective-permute-done.46.refs_1_ = bf16[512,256]{1,0:T(8,128)(2,1)S(1)} collective-permute-done((bf16[512,256]{1,0:T(8,128)(2,1)S(1)}, bf16[512,256]{1,0:T(8,128)(2,1)S(1)}, u32[]{:S(2)}, u32[]{:S(2)}) %collective-permute-start.46) | collective-permute-done | bytes 262176 | tf_op jit(solution)/shard_map/ppermute | solution.py:329
  322.6 4.3 collective-permute-done.47.refs_2_
  326.9 4.8 %backward_block.6 = (bf16[512,256]{1,0:T(8,128)(2,1)S(1)}, f32[512,256]{1,0:T(8,128)S(1)}, bf16[512,256]{1,0:T(8,128)(2,1)S(1)}, bf16[512,256]{1,0:T(8,128)(2,1)S(1)}, bf16[512,256]{1,0:T(8,128)(2,1)S(1)}) custom-call(s32[3]{0:T(128)S(1)} %pad_add_fusion.scal, f32[512,256]{1,0:T(8,128)S(1)} %get-tuple-element.87.refs_0_, ...), custom_call_target="tpu_custom_call" | custom-call | flops 2429026304 | bytes 5767168 | tf_op jit(solution)/shard_map/backward_block/pallas_call | solution.py:271
  332.3 1.6 collective-permute-start.50
  335.2 3.4 collective-permute-done.49.refs_1_
  338.6 4.1 collective-permute-done.50.refs_2_
  344.0 1.5 collective-permute-start.54
  345.5 1.6 collective-permute-start.53
  347.5 4.3 collective-permute-done.54
  351.9 2.7 collective-permute-done.53
  357.6 4.6 collective-permute-start.58
  362.5 15.6 %collective-permute-done.56 = bf16[512,1024]{1,0:T(8,128)(2,1)S(1)} collective-permute-done((bf16[512,1024]{1,0:T(8,128)(2,1)S(1)}, bf16[512,1024]{1,0:T(8,128)(2,1)S(1)}, u32[]{:S(2)}, u32[]{:S(2)}) %collective-permute-start.56) | collective-permute-done | bytes 1048608 | tf_op jit(solution)/shard_map/ppermute | solution.py:478
  380.8 1.6 dynamic-slice_dynamic-update-slice_fusion.6
  385.6 5.5 %pad_dynamic-slice_fusion = (bf16[8,4,4,32,1024]{4,3,2,1,0:T(8,128)(2,1)S(1)}, bf16[8,4,4,32,1024]{4,3,2,1,0:T(8,128)(2,1)S(1)}) fusion(s32[]{:T(128)S(6)} %select_n.257, s32[]{:T(128)S(6)} %select_n.259, bf16[8,4,4,32,1024]{4,3,2,1,0:T(8,128)(2,1)S(1)} %bitcast.136, s32[]{:T(128)S(6)} %select_n.253, s32[]{:T(128)S(6)} %select_n.255), kind=kLoop, calls=%fused_computation | loop fusion | bytes 25165840 | tf_op jit(solution)/shard_map/dynamic_slice | solution.py:445
  391.1 5.4 %fusion = bf16[4096,1152]{1,0:T(8,128)(2,1)S(1)} fusion(s32[]{:T(128)S(6)} %select_n.261, bf16[4096,1024]{1,0:T(8,128)(2,1)S(1)} %bitcast.127, bf16[4096,1024]{1,0:T(8,128)(2,1)S(1)} %bitcast.126), kind=kLoop, calls=%fused_computation.4 | loop fusion | flops 18874368 | bytes 26214404 | tf_op jit(solution)/shard_map/concatenate | solution.py:451
  401.4 2.3 constant_dynamic-update-slice_fusion.6
  404.8 2.3 constant_dynamic-update-slice_fusion.4
  408.1 2.3 constant_dynamic-update-slice_fusion.2
  410.4 16.9 %collective-permute-done.60 = bf16[512,1024]{1,0:T(8,128)(2,1)S(1)} collective-permute-done((bf16[512,1024]{1,0:T(8,128)(2,1)S(1)}, bf16[512,1024]{1,0:T(8,128)(2,1)S(1)}, u32[]{:S(2)}, u32[]{:S(2)}) %collective-permute-start.60) | collective-permute-done | bytes 1048608 | tf_op jit(solution)/shard_map/ppermute | solution.py:478
  432.4 14.2 %fusion.24 = f32[1152,1024]{1,0:T(8,128)} fusion(bf16[4096,1152]{1,0:T(8,128)(2,1)S(1)} %fusion, bf16[4096,1024]{1,0:T(8,128)(2,1)} %constant_dynamic-update-slice_fusion), kind=kOutput, calls=%fused_computation.120 | convolution fusion | flops 9663676416 | bytes 22544384 | tf_op jit(solution)/shard_map/dot_general | solution.py:454
  446.7 10.7 %collective-permute-done.63 = bf16[512,1024]{1,0:T(8,128)(2,1)S(1)} collective-permute-done((bf16[512,1024]{1,0:T(8,128)(2,1)S(1)}, bf16[512,1024]{1,0:T(8,128)(2,1)S(1)}, u32[]{:S(2)}, u32[]{:S(2)}) %collective-permute-start.63) | collective-permute-done | bytes 1048608 | tf_op jit(solution)/shard_map/ppermute | solution.py:478
  457.6 2.6 collective-permute-done.65
  460.2 10.7 %divide_subtract_fusion = (f32[1,1152,1024]{2,1,0:T(8,128)}, f32[1,1152,1024]{2,1,0:T(8,128)}, f32[1,1152,1024]{2,1,0:T(8,128)}) fusion(f32[1,1152,1024]{2,1,0:T(8,128)S(1)} %bitcast.148, f32[1,1152,1024]{2,1,0:T(8,128)S(1)} %bitcast.155, f32[1,1152,1024]{2,1,0:T(8,128)} %param.11, f32[1152,1024]{1,0:T(8,128)} %fusion.24, ...), kind=kOutput, calls=%fused_computation.11 | convolution fusion | flops 2434269184 | bytes 37486592 | tf_op jit(solution)/shard_map/dot_general | solution.py:454
  (204 shorter events, 82.7 us)
Async XLA Ops:
  7.2 372.2 %all-gather.3.cloned.1.call-start = ((), (), s32[]{:S(2)}) async-start(), calls=%async_computation | async-start | bytes 9437184 | tf_op jit(solution)/shard_map/all_gather | solution.py:411
  11.1 16.6 %collective-permute-start.1 = (bf16[1152,256]{1,0:T(8,128)(2,1)}, bf16[1152,256]{1,0:T(8,128)(2,1)}, u32[]{:S(2)}, u32[]{:S(2)}) collective-permute-start(bf16[1152,256]{1,0:T(8,128)(2,1)} %get-tuple-element.114), channel_id=1, source_target_pairs={{0,16},{8,24},{16,0},{24,8},{1,17},{9,25},{17,1},{25,9},{2,18},{10... | collective-permute-start | bytes 1769480 | tf_op jit(solution)/shard_map/ppermute | solution.py:329
  14.1 16.6 %collective-permute-start = (bf16[1152,256]{1,0:T(8,128)(2,1)}, bf16[1152,256]{1,0:T(8,128)(2,1)}, u32[]{:S(2)}, u32[]{:S(2)}) collective-permute-start(bf16[1152,256]{1,0:T(8,128)(2,1)} %get-tuple-element.115), channel_id=1, source_target_pairs={{0,8},{8,0},{16,24},{24,16},{1,9},{9,1},{17,25},{25,17},{2,10},{10... | collective-permute-start | bytes 1769480 | tf_op jit(solution)/shard_map/ppermute | solution.py:329
  15.5 26.0 %collective-permute-start.2 = (bf16[1152,256]{1,0:T(8,128)(2,1)}, bf16[1152,256]{1,0:T(8,128)(2,1)}, u32[]{:S(2)}, u32[]{:S(2)}) collective-permute-start(bf16[1152,256]{1,0:T(8,128)(2,1)} %get-tuple-element.116), channel_id=1, source_target_pairs={{0,24},{8,16},{16,8},{24,0},{1,25},{9,17},{17,9},{25,1},{2,26},{10... | collective-permute-start | bytes 1769480 | tf_op jit(solution)/shard_map/ppermute | solution.py:329
  44.4 18.3 %collective-permute-start.6 = (bf16[1152,256]{1,0:T(8,128)(2,1)S(1)}, bf16[1152,256]{1,0:T(8,128)(2,1)}, u32[]{:S(2)}, u32[]{:S(2)}) collective-permute-start(bf16[1152,256]{1,0:T(8,128)(2,1)S(1)} %bitcast.145), channel_id=1, source_target_pairs={{2,0},{3,1},{4,2},{5,3},{6,4},{7,5},{10,8},{11,9},{12,10},{13,11},... | collective-permute-start | bytes 1769480 | tf_op jit(solution)/shard_map/ppermute | solution.py:386
  45.7 18.3 %collective-permute-start.3 = (bf16[1152,256]{1,0:T(8,128)(2,1)S(1)}, bf16[1152,256]{1,0:T(8,128)(2,1)}, u32[]{:S(2)}, u32[]{:S(2)}) collective-permute-start(bf16[1152,256]{1,0:T(8,128)(2,1)S(1)} %bitcast.146), channel_id=1, source_target_pairs={{0,2},{1,3},{2,4},{3,5},{4,6},{5,7},{8,10},{9,11},{10,12},{11,13},... | collective-permute-start | bytes 1769480 | tf_op jit(solution)/shard_map/ppermute | solution.py:385
  51.1 24.1 %collective-permute-start.15 = (bf16[1152,256]{1,0:T(8,128)(2,1)S(1)}, bf16[1152,256]{1,0:T(8,128)(2,1)S(1)}, u32[]{:S(2)}, u32[]{:S(2)}) collective-permute-start(bf16[1152,256]{1,0:T(8,128)(2,1)S(1)} %bitcast.143), channel_id=1, source_target_pairs={{2,0},{3,1},{4,2},{5,3},{6,4},{7,5},{10,8},{11,9},{12,10},{13,11},... | collective-permute-start | bytes 1769480 | tf_op jit(solution)/shard_map/ppermute | solution.py:386
  52.4 24.1 %collective-permute-start.12 = (bf16[1152,256]{1,0:T(8,128)(2,1)S(1)}, bf16[1152,256]{1,0:T(8,128)(2,1)S(1)}, u32[]{:S(2)}, u32[]{:S(2)}) collective-permute-start(bf16[1152,256]{1,0:T(8,128)(2,1)S(1)} %bitcast.144), channel_id=1, source_target_pairs={{0,2},{1,3},{2,4},{3,5},{4,6},{5,7},{8,10},{9,11},{10,12},{11,13},... | collective-permute-start | bytes 1769480 | tf_op jit(solution)/shard_map/ppermute | solution.py:385
  62.6 25.3 %collective-permute-start.7 = (bf16[1152,256]{1,0:T(8,128)(2,1)}, bf16[1152,256]{1,0:T(8,128)(2,1)}, u32[]{:S(2)}, u32[]{:S(2)}) collective-permute-start(bf16[1152,256]{1,0:T(8,128)(2,1)} %collective-permute-done.6), channel_id=1, source_target_pairs={{2,0},{3,1},{4,2},{5,3},{10,8},{11,9},{12,10},{13,11},{18,16},{19,... | collective-permute-start | bytes 1769480 | tf_op jit(solution)/shard_map/ppermute | solution.py:386
  64.0 25.2 %collective-permute-start.4 = (bf16[1152,256]{1,0:T(8,128)(2,1)}, bf16[1152,256]{1,0:T(8,128)(2,1)}, u32[]{:S(2)}, u32[]{:S(2)}) collective-permute-start(bf16[1152,256]{1,0:T(8,128)(2,1)} %collective-permute-done.3), channel_id=1, source_target_pairs={{2,4},{3,5},{4,6},{5,7},{10,12},{11,13},{12,14},{13,15},{18,20},{1... | collective-permute-start | bytes 1769480 | tf_op jit(solution)/shard_map/ppermute | solution.py:385
  75.2 25.4 %collective-permute-start.16 = (bf16[1152,256]{1,0:T(8,128)(2,1)S(1)}, bf16[1152,256]{1,0:T(8,128)(2,1)}, u32[]{:S(2)}, u32[]{:S(2)}) collective-permute-start(bf16[1152,256]{1,0:T(8,128)(2,1)S(1)} %collective-permute-done.15), channel_id=1, source_target_pairs={{2,0},{3,1},{4,2},{5,3},{10,8},{11,9},{12,10},{13,11},{18,16},{19,... | collective-permute-start | bytes 1769480 | tf_op jit(solution)/shard_map/ppermute | solution.py:386
  76.5 25.4 %collective-permute-start.13 = (bf16[1152,256]{1,0:T(8,128)(2,1)S(1)}, bf16[1152,256]{1,0:T(8,128)(2,1)}, u32[]{:S(2)}, u32[]{:S(2)}) collective-permute-start(bf16[1152,256]{1,0:T(8,128)(2,1)S(1)} %collective-permute-done.12), channel_id=1, source_target_pairs={{2,4},{3,5},{4,6},{5,7},{10,12},{11,13},{12,14},{13,15},{18,20},{1... | collective-permute-start | bytes 1769480 | tf_op jit(solution)/shard_map/ppermute | solution.py:385
  87.9 25.2 %collective-permute-start.8 = (bf16[1152,256]{1,0:T(8,128)(2,1)}, bf16[1152,256]{1,0:T(8,128)(2,1)S(1)}, u32[]{:S(2)}, u32[]{:S(2)}) collective-permute-start(bf16[1152,256]{1,0:T(8,128)(2,1)} %collective-permute-done.7), channel_id=1, source_target_pairs={{2,0},{3,1},{10,8},{11,9},{18,16},{19,17},{26,24},{27,25}} | collective-permute-start | bytes 1769480 | tf_op jit(solution)/shard_map/ppermute | solution.py:386
  89.2 23.9 %collective-permute-start.5 = (bf16[1152,256]{1,0:T(8,128)(2,1)}, bf16[1152,256]{1,0:T(8,128)(2,1)S(1)}, u32[]{:S(2)}, u32[]{:S(2)}) collective-permute-start(bf16[1152,256]{1,0:T(8,128)(2,1)} %collective-permute-done.4), channel_id=1, source_target_pairs={{4,6},{5,7},{12,14},{13,15},{20,22},{21,23},{28,30},{29,31}} | collective-permute-start | bytes 1769480 | tf_op jit(solution)/shard_map/ppermute | solution.py:385
  100.6 25.2 %collective-permute-start.17 = (bf16[1152,256]{1,0:T(8,128)(2,1)}, bf16[1152,256]{1,0:T(8,128)(2,1)S(1)}, u32[]{:S(2)}, u32[]{:S(2)}) collective-permute-start(bf16[1152,256]{1,0:T(8,128)(2,1)} %collective-permute-done.16), channel_id=1, source_target_pairs={{2,0},{3,1},{10,8},{11,9},{18,16},{19,17},{26,24},{27,25}} | collective-permute-start | bytes 1769480 | tf_op jit(solution)/shard_map/ppermute | solution.py:386
  101.9 23.9 %collective-permute-start.14 = (bf16[1152,256]{1,0:T(8,128)(2,1)}, bf16[1152,256]{1,0:T(8,128)(2,1)S(1)}, u32[]{:S(2)}, u32[]{:S(2)}) collective-permute-start(bf16[1152,256]{1,0:T(8,128)(2,1)} %collective-permute-done.13), channel_id=1, source_target_pairs={{4,6},{5,7},{12,14},{13,15},{20,22},{21,23},{28,30},{29,31}} | collective-permute-start | bytes 1769480 | tf_op jit(solution)/shard_map/ppermute | solution.py:385
  113.1 25.3 %collective-permute-start.10 = (bf16[1152,256]{1,0:T(8,128)(2,1)S(1)}, bf16[1152,256]{1,0:T(8,128)(2,1)S(1)}, u32[]{:S(2)}, u32[]{:S(2)}) collective-permute-start(bf16[1152,256]{1,0:T(8,128)(2,1)S(1)} %bitcast.141), channel_id=1, source_target_pairs={{2,0},{3,1},{4,2},{5,3},{6,4},{7,5},{10,8},{11,9},{12,10},{13,11},... | collective-permute-start | bytes 1769480 | tf_op jit(solution)/shard_map/ppermute | solution.py:386
  114.4 25.3 %collective-permute-start.9 = (bf16[1152,256]{1,0:T(8,128)(2,1)S(1)}, bf16[1152,256]{1,0:T(8,128)(2,1)S(1)}, u32[]{:S(2)}, u32[]{:S(2)}) collective-permute-start(bf16[1152,256]{1,0:T(8,128)(2,1)S(1)} %bitcast.142), channel_id=1, source_target_pairs={{0,2},{1,3},{2,4},{3,5},{4,6},{5,7},{8,10},{9,11},{10,12},{11,13},... | collective-permute-start | bytes 1769480 | tf_op jit(solution)/shard_map/ppermute | solution.py:385
  120.5 42.4 %collective-permute-start.11 = (bf16[4,1152,256]{2,1,0:T(8,128)(2,1)S(1)}, bf16[4,1152,256]{2,1,0:T(8,128)(2,1)S(1)}, u32[]{:S(2)}, u32[]{:S(2)}) collective-permute-start(bf16[4,1152,256]{2,1,0:T(8,128)(2,1)S(1)} %pad_maximum_fusion.1.refs_4_), channel_id=1, source_target_pairs={{0,1},{1,0},{2,3},{3,2},{4,5},{5,4},{6,7},{7,6},{8,9},{9,8},{10,11... | collective-permute-start | bytes 7077896 | tf_op jit(solution)/shard_map/ppermute | solution.py:301
  125.8 53.5 %collective-permute-start.20 = (bf16[1152,256]{1,0:T(8,128)(2,1)}, bf16[1152,256]{1,0:T(8,128)(2,1)S(1)}, u32[]{:S(2)}, u32[]{:S(2)}) collective-permute-start(bf16[1152,256]{1,0:T(8,128)(2,1)} %bitcast.16), channel_id=1, source_target_pairs={{2,0},{3,1},{4,2},{5,3},{6,4},{7,5},{10,8},{11,9},{12,10},{13,11},... | collective-permute-start | bytes 1769480 | tf_op jit(solution)/shard_map/ppermute | solution.py:386
  127.2 41.3 %collective-permute-start.18 = (bf16[1152,256]{1,0:T(8,128)(2,1)}, bf16[1152,256]{1,0:T(8,128)(2,1)S(1)}, u32[]{:S(2)}, u32[]{:S(2)}) collective-permute-start(bf16[1152,256]{1,0:T(8,128)(2,1)} %bitcast.16), channel_id=1, source_target_pairs={{0,2},{1,3},{2,4},{3,5},{4,6},{5,7},{8,10},{9,11},{10,12},{11,13},... | collective-permute-start | bytes 1769480 | tf_op jit(solution)/shard_map/ppermute | solution.py:385
  138.4 23.2 %collective-permute-start.33 = (bf16[1152,256]{1,0:T(8,128)(2,1)S(1)}, bf16[1152,256]{1,0:T(8,128)(2,1)S(1)}, u32[]{:S(2)}, u32[]{:S(2)}) collective-permute-start(bf16[1152,256]{1,0:T(8,128)(2,1)S(1)} %collective-permute-done.10), channel_id=1, source_target_pairs={{2,0},{3,1},{4,2},{5,3},{10,8},{11,9},{12,10},{13,11},{18,16},{19,... | collective-permute-start | bytes 1769480 | tf_op jit(solution)/shard_map/ppermute | solution.py:386
  139.7 21.9 %collective-permute-start.31 = (bf16[1152,256]{1,0:T(8,128)(2,1)S(1)}, bf16[1152,256]{1,0:T(8,128)(2,1)S(1)}, u32[]{:S(2)}, u32[]{:S(2)}) collective-permute-start(bf16[1152,256]{1,0:T(8,128)(2,1)S(1)} %collective-permute-done.9), channel_id=1, source_target_pairs={{2,4},{3,5},{4,6},{5,7},{10,12},{11,13},{12,14},{13,15},{18,20},{1... | collective-permute-start | bytes 1769480 | tf_op jit(solution)/shard_map/ppermute | solution.py:385
  161.6 55.0 %collective-permute-start.25 = (bf16[4,1152,256]{2,1,0:T(8,128)(2,1)S(1)}, bf16[4,1152,256]{2,1,0:T(8,128)(2,1)S(1)}, u32[]{:S(2)}, u32[]{:S(2)}) collective-permute-start(bf16[4,1152,256]{2,1,0:T(8,128)(2,1)S(1)} %pad_maximum_fusion.2.refs_4_.refs_5_), channel_id=1, source_target_pairs={{0,1},{1,0},{2,3},{3,2},{4,5},{5,4},{6,7},{7,6},{8,9},{9,8},{10,11... | collective-permute-start | bytes 7077896 | tf_op jit(solution)/shard_map/ppermute | solution.py:301
  161.6 17.6 %collective-permute-start.34 = (bf16[1152,256]{1,0:T(8,128)(2,1)S(1)}, bf16[1152,256]{1,0:T(8,128)(2,1)S(1)}, u32[]{:S(2)}, u32[]{:S(2)}) collective-permute-start(bf16[1152,256]{1,0:T(8,128)(2,1)S(1)} %collective-permute-done.33), channel_id=1, source_target_pairs={{2,0},{3,1},{10,8},{11,9},{18,16},{19,17},{26,24},{27,25}} | collective-permute-start | bytes 1769480 | tf_op jit(solution)/shard_map/ppermute | solution.py:386
  163.0 17.6 %collective-permute-start.32 = (bf16[1152,256]{1,0:T(8,128)(2,1)S(1)}, bf16[1152,256]{1,0:T(8,128)(2,1)S(1)}, u32[]{:S(2)}, u32[]{:S(2)}) collective-permute-start(bf16[1152,256]{1,0:T(8,128)(2,1)S(1)} %collective-permute-done.31), channel_id=1, source_target_pairs={{4,6},{5,7},{12,14},{13,15},{20,22},{21,23},{28,30},{29,31}} | collective-permute-start | bytes 1769480 | tf_op jit(solution)/shard_map/ppermute | solution.py:385
  168.5 12.1 %collective-permute-start.19 = (bf16[1152,256]{1,0:T(8,128)(2,1)S(1)}, bf16[1152,256]{1,0:T(8,128)(2,1)S(1)}, u32[]{:S(2)}, u32[]{:S(2)}) collective-permute-start(bf16[1152,256]{1,0:T(8,128)(2,1)S(1)} %collective-permute-done.18), channel_id=1, source_target_pairs={{2,4},{3,5},{4,6},{5,7},{10,12},{11,13},{12,14},{13,15},{18,20},{1... | collective-permute-start | bytes 1769480 | tf_op jit(solution)/shard_map/ppermute | solution.py:385
  179.3 16.9 %collective-permute-start.21 = (bf16[1152,256]{1,0:T(8,128)(2,1)S(1)}, bf16[1152,256]{1,0:T(8,128)(2,1)S(1)}, u32[]{:S(2)}, u32[]{:S(2)}) collective-permute-start(bf16[1152,256]{1,0:T(8,128)(2,1)S(1)} %collective-permute-done.20), channel_id=1, source_target_pairs={{2,0},{3,1},{4,2},{5,3},{10,8},{11,9},{12,10},{13,11},{18,16},{19,... | collective-permute-start | bytes 1769480 | tf_op jit(solution)/shard_map/ppermute | solution.py:386
  180.7 17.0 %collective-permute-start.26 = (bf16[1152,256]{1,0:T(8,128)(2,1)S(1)}, bf16[1152,256]{1,0:T(8,128)(2,1)S(1)}, u32[]{:S(2)}, u32[]{:S(2)}) collective-permute-start(bf16[1152,256]{1,0:T(8,128)(2,1)S(1)} %collective-permute-done.19), channel_id=1, source_target_pairs={{4,6},{5,7},{12,14},{13,15},{20,22},{21,23},{28,30},{29,31}} | collective-permute-start | bytes 1769480 | tf_op jit(solution)/shard_map/ppermute | solution.py:385
  181.7 66.7 %collective-permute-start.35 = (bf16[4,1152,256]{2,1,0:T(8,128)(2,1)S(1)}, bf16[4,1152,256]{2,1,0:T(8,128)(2,1)S(1)}, u32[]{:S(2)}, u32[]{:S(2)}) collective-permute-start(bf16[4,1152,256]{2,1,0:T(8,128)(2,1)S(1)} %pad_maximum_fusion.3.refs_4_.refs_5_), channel_id=1, source_target_pairs={{0,1},{1,0},{2,3},{3,2},{4,5},{5,4},{6,7},{7,6},{8,9},{9,8},{10,11... | collective-permute-start | bytes 7077896 | tf_op jit(solution)/shard_map/ppermute | solution.py:301
  196.2 16.0 %collective-permute-start.27 = (bf16[1152,256]{1,0:T(8,128)(2,1)S(1)}, bf16[1152,256]{1,0:T(8,128)(2,1)S(1)}, u32[]{:S(2)}, u32[]{:S(2)}) collective-permute-start(bf16[1152,256]{1,0:T(8,128)(2,1)S(1)} %collective-permute-done.21), channel_id=1, source_target_pairs={{2,0},{3,1},{10,8},{11,9},{18,16},{19,17},{26,24},{27,25}} | collective-permute-start | bytes 1769480 | tf_op jit(solution)/shard_map/ppermute | solution.py:386
  213.5 55.1 %collective-permute-start.39 = (bf16[4,1152,256]{2,1,0:T(8,128)(2,1)S(1)}, bf16[4,1152,256]{2,1,0:T(8,128)(2,1)S(1)}, u32[]{:S(2)}, u32[]{:S(2)}) collective-permute-start(bf16[4,1152,256]{2,1,0:T(8,128)(2,1)S(1)} %pad_maximum_fusion.4.refs_4_.refs_7_), channel_id=1, source_target_pairs={{0,1},{1,0},{2,3},{3,2},{4,5},{5,4},{6,7},{7,6},{8,9},{9,8},{10,11... | collective-permute-start | bytes 7077896 | tf_op jit(solution)/shard_map/ppermute | solution.py:301
  213.6 10.1 %collective-permute-start.24 = (bf16[512,256]{1,0:T(8,128)(2,1)S(1)}, bf16[512,256]{1,0:T(8,128)(2,1)S(1)}, u32[]{:S(2)}, u32[]{:S(2)}) collective-permute-start(bf16[512,256]{1,0:T(8,128)(2,1)S(1)} %get-tuple-element.66.refs_0_), channel_id=1, source_target_pairs={{0,24},{8,16},{16,8},{24,0},{1,25},{9,17},{17,9},{25,1},{2,26},{10... | collective-permute-start | bytes 786440 | tf_op jit(solution)/shard_map/ppermute | solution.py:329
  216.0 12.8 %collective-permute-start.23 = (bf16[512,256]{1,0:T(8,128)(2,1)S(1)}, bf16[512,256]{1,0:T(8,128)(2,1)S(1)}, u32[]{:S(2)}, u32[]{:S(2)}) collective-permute-start(bf16[512,256]{1,0:T(8,128)(2,1)S(1)} %get-tuple-element.66.refs_0_), channel_id=1, source_target_pairs={{0,16},{8,24},{16,0},{24,8},{1,17},{9,25},{17,1},{25,9},{2,18},{10... | collective-permute-start | bytes 786440 | tf_op jit(solution)/shard_map/ppermute | solution.py:329
  216.6 12.3 %collective-permute-start.22 = (bf16[512,256]{1,0:T(8,128)(2,1)S(1)}, bf16[512,256]{1,0:T(8,128)(2,1)S(1)}, u32[]{:S(2)}, u32[]{:S(2)}) collective-permute-start(bf16[512,256]{1,0:T(8,128)(2,1)S(1)} %get-tuple-element.66.refs_0_), channel_id=1, source_target_pairs={{0,8},{8,0},{16,24},{24,16},{1,9},{9,1},{17,25},{25,17},{2,10},{10... | collective-permute-start | bytes 786440 | tf_op jit(solution)/shard_map/ppermute | solution.py:329
  233.5 10.2 %collective-permute-start.30 = (bf16[512,256]{1,0:T(8,128)(2,1)S(1)}, bf16[512,256]{1,0:T(8,128)(2,1)S(1)}, u32[]{:S(2)}, u32[]{:S(2)}) collective-permute-start(bf16[512,256]{1,0:T(8,128)(2,1)S(1)} %get-tuple-element.67.refs_0_), channel_id=1, source_target_pairs={{0,24},{8,16},{16,8},{24,0},{1,25},{9,17},{17,9},{25,1},{2,26},{10... | collective-permute-start | bytes 786440 | tf_op jit(solution)/shard_map/ppermute | solution.py:329
  235.4 13.0 %collective-permute-start.29 = (bf16[512,256]{1,0:T(8,128)(2,1)S(1)}, bf16[512,256]{1,0:T(8,128)(2,1)S(1)}, u32[]{:S(2)}, u32[]{:S(2)}) collective-permute-start(bf16[512,256]{1,0:T(8,128)(2,1)S(1)} %get-tuple-element.67.refs_0_), channel_id=1, source_target_pairs={{0,16},{8,24},{16,0},{24,8},{1,17},{9,25},{17,1},{25,9},{2,18},{10... | collective-permute-start | bytes 786440 | tf_op jit(solution)/shard_map/ppermute | solution.py:329
  236.6 11.8 %collective-permute-start.28 = (bf16[512,256]{1,0:T(8,128)(2,1)S(1)}, bf16[512,256]{1,0:T(8,128)(2,1)S(1)}, u32[]{:S(2)}, u32[]{:S(2)}) collective-permute-start(bf16[512,256]{1,0:T(8,128)(2,1)S(1)} %get-tuple-element.67.refs_0_), channel_id=1, source_target_pairs={{0,8},{8,0},{16,24},{24,16},{1,9},{9,1},{17,25},{25,17},{2,10},{10... | collective-permute-start | bytes 786440 | tf_op jit(solution)/shard_map/ppermute | solution.py:329
  253.9 10.1 %collective-permute-start.38 = (bf16[512,256]{1,0:T(8,128)(2,1)S(1)}, bf16[512,256]{1,0:T(8,128)(2,1)S(1)}, u32[]{:S(2)}, u32[]{:S(2)}) collective-permute-start(bf16[512,256]{1,0:T(8,128)(2,1)S(1)} %get-tuple-element.68.refs_0_), channel_id=1, source_target_pairs={{0,24},{8,16},{16,8},{24,0},{1,25},{9,17},{17,9},{25,1},{2,26},{10... | collective-permute-start | bytes 786440 | tf_op jit(solution)/shard_map/ppermute | solution.py:329
  255.3 13.2 %collective-permute-start.37 = (bf16[512,256]{1,0:T(8,128)(2,1)S(1)}, bf16[512,256]{1,0:T(8,128)(2,1)S(1)}, u32[]{:S(2)}, u32[]{:S(2)}) collective-permute-start(bf16[512,256]{1,0:T(8,128)(2,1)S(1)} %get-tuple-element.68.refs_0_), channel_id=1, source_target_pairs={{0,16},{8,24},{16,0},{24,8},{1,17},{9,25},{17,1},{25,9},{2,18},{10... | collective-permute-start | bytes 786440 | tf_op jit(solution)/shard_map/ppermute | solution.py:329
  256.8 11.9 %collective-permute-start.36 = (bf16[512,256]{1,0:T(8,128)(2,1)S(1)}, bf16[512,256]{1,0:T(8,128)(2,1)S(1)}, u32[]{:S(2)}, u32[]{:S(2)}) collective-permute-start(bf16[512,256]{1,0:T(8,128)(2,1)S(1)} %get-tuple-element.68.refs_0_), channel_id=1, source_target_pairs={{0,8},{8,0},{16,24},{24,16},{1,9},{9,1},{17,25},{25,17},{2,10},{10... | collective-permute-start | bytes 786440 | tf_op jit(solution)/shard_map/ppermute | solution.py:329
  277.0 4.7 collective-permute-start.42
  278.5 3.7 collective-permute-start.41
  295.8 9.3 %collective-permute-start.43 = (bf16[512,256]{1,0:T(8,128)(2,1)S(1)}, bf16[512,256]{1,0:T(8,128)(2,1)S(1)}, u32[]{:S(2)}, u32[]{:S(2)}) collective-permute-start(bf16[512,256]{1,0:T(8,128)(2,1)S(1)} %get-tuple-element.83), channel_id=1, source_target_pairs={{0,8},{8,0},{16,24},{24,16},{1,9},{9,1},{17,25},{25,17},{2,10},{10... | collective-permute-start | bytes 786440 | tf_op jit(solution)/shard_map/ppermute | solution.py:329
  296.6 12.4 %collective-permute-start.44 = (bf16[512,256]{1,0:T(8,128)(2,1)S(1)}, bf16[512,256]{1,0:T(8,128)(2,1)S(1)}, u32[]{:S(2)}, u32[]{:S(2)}) collective-permute-start(bf16[512,256]{1,0:T(8,128)(2,1)S(1)} %get-tuple-element.84), channel_id=1, source_target_pairs={{0,16},{8,24},{16,0},{24,8},{1,17},{9,25},{17,1},{25,9},{2,18},{10... | collective-permute-start | bytes 786440 | tf_op jit(solution)/shard_map/ppermute | solution.py:329
  298.0 11.0 %collective-permute-start.45 = (bf16[512,256]{1,0:T(8,128)(2,1)S(1)}, bf16[512,256]{1,0:T(8,128)(2,1)S(1)}, u32[]{:S(2)}, u32[]{:S(2)}) collective-permute-start(bf16[512,256]{1,0:T(8,128)(2,1)S(1)} %get-tuple-element.85), channel_id=1, source_target_pairs={{0,24},{8,16},{16,8},{24,0},{1,25},{9,17},{17,9},{25,1},{2,26},{10... | collective-permute-start | bytes 786440 | tf_op jit(solution)/shard_map/ppermute | solution.py:329
  313.9 8.7 %collective-permute-start.46 = (bf16[512,256]{1,0:T(8,128)(2,1)S(1)}, bf16[512,256]{1,0:T(8,128)(2,1)S(1)}, u32[]{:S(2)}, u32[]{:S(2)}) collective-permute-start(bf16[512,256]{1,0:T(8,128)(2,1)S(1)} %get-tuple-element.88), channel_id=1, source_target_pairs={{0,8},{8,0},{16,24},{24,16},{1,9},{9,1},{17,25},{25,17},{2,10},{10... | collective-permute-start | bytes 786440 | tf_op jit(solution)/shard_map/ppermute | solution.py:329
  315.2 11.7 %collective-permute-start.47 = (bf16[512,256]{1,0:T(8,128)(2,1)S(1)}, bf16[512,256]{1,0:T(8,128)(2,1)S(1)}, u32[]{:S(2)}, u32[]{:S(2)}) collective-permute-start(bf16[512,256]{1,0:T(8,128)(2,1)S(1)} %get-tuple-element.89), channel_id=1, source_target_pairs={{0,16},{8,24},{16,0},{24,8},{1,17},{9,25},{17,1},{25,9},{2,18},{10... | collective-permute-start | bytes 786440 | tf_op jit(solution)/shard_map/ppermute | solution.py:329
  315.8 11.0 %collective-permute-start.48 = (bf16[512,256]{1,0:T(8,128)(2,1)S(1)}, bf16[512,256]{1,0:T(8,128)(2,1)S(1)}, u32[]{:S(2)}, u32[]{:S(2)}) collective-permute-start(bf16[512,256]{1,0:T(8,128)(2,1)S(1)} %get-tuple-element.90), channel_id=1, source_target_pairs={{0,24},{8,16},{16,8},{24,0},{1,25},{9,17},{17,9},{25,1},{2,26},{10... | collective-permute-start | bytes 786440 | tf_op jit(solution)/shard_map/ppermute | solution.py:329
  331.7 6.9 %collective-permute-start.49 = (bf16[512,256]{1,0:T(8,128)(2,1)S(1)}, bf16[512,256]{1,0:T(8,128)(2,1)S(1)}, u32[]{:S(2)}, u32[]{:S(2)}) collective-permute-start(bf16[512,256]{1,0:T(8,128)(2,1)S(1)} %get-tuple-element.93), channel_id=1, source_target_pairs={{0,8},{8,0},{16,24},{24,16},{1,9},{9,1},{17,25},{25,17},{2,10},{10... | collective-permute-start | bytes 786440 | tf_op jit(solution)/shard_map/ppermute | solution.py:329
  332.3 10.4 %collective-permute-start.50 = (bf16[512,256]{1,0:T(8,128)(2,1)S(1)}, bf16[512,256]{1,0:T(8,128)(2,1)S(1)}, u32[]{:S(2)}, u32[]{:S(2)}) collective-permute-start(bf16[512,256]{1,0:T(8,128)(2,1)S(1)} %get-tuple-element.94), channel_id=1, source_target_pairs={{0,16},{8,24},{16,0},{24,8},{1,17},{9,25},{17,1},{25,9},{2,18},{10... | collective-permute-start | bytes 786440 | tf_op jit(solution)/shard_map/ppermute | solution.py:329
  333.9 8.8 %collective-permute-start.51 = (bf16[512,256]{1,0:T(8,128)(2,1)S(1)}, bf16[512,256]{1,0:T(8,128)(2,1)S(1)}, u32[]{:S(2)}, u32[]{:S(2)}) collective-permute-start(bf16[512,256]{1,0:T(8,128)(2,1)S(1)} %get-tuple-element.95), channel_id=1, source_target_pairs={{0,24},{8,16},{16,8},{24,0},{1,25},{9,17},{17,9},{25,1},{2,26},{10... | collective-permute-start | bytes 786440 | tf_op jit(solution)/shard_map/ppermute | solution.py:329
  344.0 7.9 %collective-permute-start.54 = (bf16[512,256]{1,0:T(8,128)(2,1)S(1)}, bf16[512,256]{1,0:T(8,128)(2,1)S(1)}, u32[]{:S(2)}, u32[]{:S(2)}) collective-permute-start(bf16[512,256]{1,0:T(8,128)(2,1)S(1)} %get-tuple-element.130), channel_id=1, source_target_pairs={{0,24},{8,16},{16,8},{24,0},{1,25},{9,17},{17,9},{25,1},{2,26},{10... | collective-permute-start | bytes 786440 | tf_op jit(solution)/shard_map/ppermute | solution.py:329
  345.5 9.0 %collective-permute-start.53 = (bf16[512,256]{1,0:T(8,128)(2,1)S(1)}, bf16[512,256]{1,0:T(8,128)(2,1)S(1)}, u32[]{:S(2)}, u32[]{:S(2)}) collective-permute-start(bf16[512,256]{1,0:T(8,128)(2,1)S(1)} %get-tuple-element.131), channel_id=1, source_target_pairs={{0,16},{8,24},{16,0},{24,8},{1,17},{9,25},{17,1},{25,9},{2,18},{10... | collective-permute-start | bytes 786440 | tf_op jit(solution)/shard_map/ppermute | solution.py:329
  347.1 7.7 %collective-permute-start.52 = (bf16[512,256]{1,0:T(8,128)(2,1)S(1)}, bf16[512,256]{1,0:T(8,128)(2,1)S(1)}, u32[]{:S(2)}, u32[]{:S(2)}) collective-permute-start(bf16[512,256]{1,0:T(8,128)(2,1)S(1)} %get-tuple-element.132), channel_id=1, source_target_pairs={{0,8},{8,0},{16,24},{24,16},{1,9},{9,1},{17,25},{25,17},{2,10},{10... | collective-permute-start | bytes 786440 | tf_op jit(solution)/shard_map/ppermute | solution.py:329
  356.3 21.9 %collective-permute-start.56 = (bf16[512,1024]{1,0:T(8,128)(2,1)S(1)}, bf16[512,1024]{1,0:T(8,128)(2,1)S(1)}, u32[]{:S(2)}, u32[]{:S(2)}) collective-permute-start(bf16[512,1024]{1,0:T(8,128)(2,1)S(1)} %get-tuple-element.123), channel_id=1, source_target_pairs={{2,0},{3,1},{4,2},{5,3},{6,4},{7,5},{10,8},{11,9},{12,10},{13,11},... | collective-permute-start | bytes 3145736 | tf_op jit(solution)/shard_map/ppermute | solution.py:478
  357.6 21.8 %collective-permute-start.58 = (bf16[512,1024]{1,0:T(8,128)(2,1)S(1)}, bf16[512,1024]{1,0:T(8,128)(2,1)S(1)}, u32[]{:S(2)}, u32[]{:S(2)}) collective-permute-start(bf16[512,1024]{1,0:T(8,128)(2,1)S(1)} %get-tuple-element.123), channel_id=1, source_target_pairs={{0,2},{1,3},{2,4},{3,5},{4,6},{5,7},{8,10},{9,11},{10,12},{11,13},... | collective-permute-start | bytes 3145736 | tf_op jit(solution)/shard_map/ppermute | solution.py:477
  362.4 39.0 %collective-permute-start.55 = (bf16[512,1024]{1,0:T(8,128)(2,1)S(1)}, bf16[512,1024]{1,0:T(8,128)(2,1)}, u32[]{:S(2)}, u32[]{:S(2)}) collective-permute-start(bf16[512,1024]{1,0:T(8,128)(2,1)S(1)} %get-tuple-element.123), channel_id=1, source_target_pairs={{0,1},{1,0},{2,3},{3,2},{4,5},{5,4},{6,7},{7,6},{8,9},{9,8},{10,11... | collective-permute-start | bytes 3145736 | tf_op jit(solution)/shard_map/ppermute | solution.py:301
  378.2 26.6 %collective-permute-start.57 = (bf16[512,1024]{1,0:T(8,128)(2,1)S(1)}, bf16[512,1024]{1,0:T(8,128)(2,1)}, u32[]{:S(2)}, u32[]{:S(2)}) collective-permute-start(bf16[512,1024]{1,0:T(8,128)(2,1)S(1)} %collective-permute-done.56), channel_id=1, source_target_pairs={{0,1},{1,0},{2,3},{3,2},{4,5},{5,4},{6,7},{7,6},{8,9},{9,8},{10,11... | collective-permute-start | bytes 3145736 | tf_op jit(solution)/shard_map/ppermute | solution.py:301
  379.3 28.8 %collective-permute-start.59 = (bf16[512,1024]{1,0:T(8,128)(2,1)S(1)}, bf16[512,1024]{1,0:T(8,128)(2,1)}, u32[]{:S(2)}, u32[]{:S(2)}) collective-permute-start(bf16[512,1024]{1,0:T(8,128)(2,1)S(1)} %collective-permute-done.58), channel_id=1, source_target_pairs={{0,1},{1,0},{2,3},{3,2},{4,5},{5,4},{6,7},{7,6},{8,9},{9,8},{10,11... | collective-permute-start | bytes 3145736 | tf_op jit(solution)/shard_map/ppermute | solution.py:301
  399.4 27.9 %collective-permute-start.60 = (bf16[512,1024]{1,0:T(8,128)(2,1)S(1)}, bf16[512,1024]{1,0:T(8,128)(2,1)S(1)}, u32[]{:S(2)}, u32[]{:S(2)}) collective-permute-start(bf16[512,1024]{1,0:T(8,128)(2,1)S(1)} %collective-permute-done.56), channel_id=1, source_target_pairs={{2,0},{3,1},{4,2},{5,3},{10,8},{11,9},{12,10},{13,11},{18,16},{19,... | collective-permute-start | bytes 3145736 | tf_op jit(solution)/shard_map/ppermute | solution.py:478
  400.7 26.6 %collective-permute-start.61 = (bf16[512,1024]{1,0:T(8,128)(2,1)S(1)}, bf16[512,1024]{1,0:T(8,128)(2,1)S(1)}, u32[]{:S(2)}, u32[]{:S(2)}) collective-permute-start(bf16[512,1024]{1,0:T(8,128)(2,1)S(1)} %collective-permute-done.58), channel_id=1, source_target_pairs={{2,4},{3,5},{4,6},{5,7},{10,12},{11,13},{12,14},{13,15},{18,20},{1... | collective-permute-start | bytes 3145736 | tf_op jit(solution)/shard_map/ppermute | solution.py:477
  428.8 28.6 %collective-permute-start.63 = (bf16[512,1024]{1,0:T(8,128)(2,1)S(1)}, bf16[512,1024]{1,0:T(8,128)(2,1)S(1)}, u32[]{:S(2)}, u32[]{:S(2)}) collective-permute-start(bf16[512,1024]{1,0:T(8,128)(2,1)S(1)} %collective-permute-done.60), channel_id=1, source_target_pairs={{2,0},{3,1},{10,8},{11,9},{18,16},{19,17},{26,24},{27,25}} | collective-permute-start | bytes 3145736 | tf_op jit(solution)/shard_map/ppermute | solution.py:478
  430.3 27.0 %collective-permute-start.64 = (bf16[512,1024]{1,0:T(8,128)(2,1)S(1)}, bf16[512,1024]{1,0:T(8,128)(2,1)S(1)}, u32[]{:S(2)}, u32[]{:S(2)}) collective-permute-start(bf16[512,1024]{1,0:T(8,128)(2,1)S(1)} %collective-permute-done.61), channel_id=1, source_target_pairs={{4,6},{5,7},{12,14},{13,15},{20,22},{21,23},{28,30},{29,31}} | collective-permute-start | bytes 3145736 | tf_op jit(solution)/shard_map/ppermute | solution.py:477
  (35 other events, 804.6 us)
Sparse Core Ops, SparseCore 0:
  277.1 80.0 all-gather.2
